TPU v7x, 32 devices: a whole 2x2x4 slice. The times are simulated.
32 devices in a mesh: gx: 4 (over z), gy: 8 (over y, x, core).
Axes of the slice: x: 2, y: 2, z: 4, core: 2. Of those that a mesh axis runs over, the one named last changes fastest.
Arguments:
- populations: float32 [19, 128, 16, 16, 128], P(None, ('gx', 'gy')), may hold values from 0.01 to 0.1
- charge: float32 [128, 16, 16, 128], P(('gx', 'gy')), may hold values from -6 to 6
- fluid_mask: int32 [128, 18, 18, 128], P(('gx', 'gy')), may hold values from 0 to 1, as said below
- tile_ids: int32 [128], P(('gx', 'gy')), may hold values from 0 to 31, as said below
- phase_label: int32 [128, 256, 128], P('gx', 'gy'), may hold values from 0 to 3
- permittivity: float32 [4], replicated, may hold values from 0.5 to 5
Outputs:
- populations_next: float32 [19, 128, 16, 16, 128], P(None, ('gx', 'gy'))
- charge_next: float32 [128, 16, 16, 128], P(('gx', 'gy'))
- potential: float32 [128, 256, 128], P('gx', 'gy')
Inputs may be any that keep to these rules, and one draw needn't show every extreme that they name: Within the slots of the devices of one gx index, tile_ids is a permutation of 0 to 31. Position p belongs to the regular block of gy index (p % 16) // 2; every device holds at most 1 positions of any one such block, and some device holds exactly 1. fluid_mask[s, i, j, z] is the fluid flag of grid cell (x0 + i - 1, y0 + j - 1, z), periodic, where (x0, y0) is the first cell of slot s's tile; the rim repeats flags of the neighbouring tiles.
All inputs are finite; a program needn't handle non-finite values.
Results may differ from a plain program's by a relative error of at most 0.0003.
Values sent between devices are 32-bit elements; how exact they have to be, the bound alone decides.
No kernel may reach another device: no remote copies, remote signals or barrier semaphores. Data moves between devices by JAX's collectives and lax.ppermute only.
A program may use at most 192 MiB of HBM per device.

v0:
```python
import jax
import jax.numpy as jnp
from jax import lax
from jax.sharding import PartitionSpec as P

EDGE = 16
DEPTH = 128
TILE_ROWS = 2
TILE_COLS = 2
PHASES = 4
SWEEPS = 4


LATTICE = (
    (0, 0, 0),
    (1, 0, 0),
    (-1, 0, 0),
    (0, 1, 0),
    (0, -1, 0),
    (0, 0, 1),
    (0, 0, -1),
    (1, 1, 0),
    (-1, -1, 0),
    (1, -1, 0),
    (-1, 1, 0),
    (1, 0, 1),
    (-1, 0, -1),
    (1, 0, -1),
    (-1, 0, 1),
    (0, 1, 1),
    (0, -1, -1),
    (0, 1, -1),
    (0, -1, 1),
)
relax_time = 0.8
screening = 0.001
spectrum_low = 0.1
spectrum_high = 2.0


def extended(value, sides, width):
    for axis, dim in sides:
        size, length = (lax.axis_size(axis), value.shape[dim])
        up = [(i, (i + 1) % size) for i in range(size)]
        down = [(j, i) for i, j in up]
        last = lax.slice_in_dim(value, length - width, length, axis=dim)
        first = lax.slice_in_dim(value, 0, width, axis=dim)
        before = lax.ppermute(last, axis, up)
        after = lax.ppermute(first, axis, down)
        value = jnp.concatenate([before, value, after], axis=dim)
    return value


def lattice_weight(direction):
    length = sum((abs(entry) for entry in LATTICE[direction]))
    if length == 0:
        return 1.0 / 3.0
    if length == 1:
        return 1.0 / 18.0
    return 1.0 / 36.0


def opposite(direction):
    return LATTICE.index(tuple((-entry for entry in LATTICE[direction])))


def crossing(axis_index, face_sign):
    return [direction for direction in range(19) if LATTICE[direction][axis_index] == face_sign]


def population_sum(population):
    density = population[0]
    for direction in range(1, 19):
        density = density + population[direction]
    return density


def velocity_sums(population):
    sums_list = []
    for axis_index in range(3):
        total = None
        for direction in range(19):
            component = LATTICE[direction][axis_index]
            if component != 0:
                contrib = population[direction] if component > 0 else -population[direction]
                total = contrib if total is None else total + contrib
        sums_list.append(total)
    return sums_list


def collide(population, density, velocity, body_force):
    speed_sq = velocity[0] * velocity[0] + velocity[1] * velocity[1] + velocity[2] * velocity[2]
    source_scale = 1.0 - 0.5 / relax_time
    result = []
    for direction in range(19):
        lattice_step = LATTICE[direction]
        weight = lattice_weight(direction)
        projected = (
            lattice_step[0] * velocity[0]
            + lattice_step[1] * velocity[1]
            + lattice_step[2] * velocity[2]
        )
        force_dot = (
            lattice_step[0] * body_force[0]
            + lattice_step[1] * body_force[1]
            + lattice_step[2] * body_force[2]
        )
        drift_dot = (
            (lattice_step[0] - velocity[0]) * body_force[0]
            + (lattice_step[1] - velocity[1]) * body_force[1]
            + (lattice_step[2] - velocity[2]) * body_force[2]
        )
        equilibrium = (
            weight
            * density
            * (1.0 + 3.0 * projected + 4.5 * projected * projected - 1.5 * speed_sq)
        )
        source = source_scale * weight * (3.0 * drift_dot + 9.0 * projected * force_dot)
        result.append(
            population[direction] - (population[direction] - equilibrium) / relax_time + source
        )
    return result


def harmonic(left_value, right_value):
    return 2.0 * left_value * right_value / (left_value + right_value)


def block_from_tiles(tile_data):
    pieces = tile_data.reshape(TILE_ROWS, TILE_COLS, EDGE, EDGE, DEPTH)
    pieces = jnp.transpose(pieces, (0, 2, 1, 3, 4))
    return pieces.reshape(TILE_ROWS * EDGE, TILE_COLS * EDGE, DEPTH)


def spread_rows(row_data, selector, present):
    picked = row_data[selector]
    full_shape = present.shape + (1,) * (picked.ndim - present.ndim)
    return jnp.where(present.reshape(full_shape), picked, jnp.zeros((), picked.dtype))


def with_margin(field_value):
    return extended(field_value, (("gx", 0), ("gy", 1)), 1)


def face_package(relaxed, charge, velocity):
    faces = []
    for axis_index, face_sign, layer_index in (
        (0, -1, 0),
        (0, 1, EDGE - 1),
        (1, -1, 0),
        (1, 1, EDGE - 1),
    ):
        channels = [relaxed[direction] for direction in crossing(axis_index, face_sign)]
        channels = channels + [charge, velocity[axis_index]]
        if axis_index == 0:
            face_parts = [channel[:, layer_index] for channel in channels]
        else:
            face_parts = [channel[:, :, layer_index] for channel in channels]
        faces.append(jnp.stack(face_parts, axis=1))
    return jnp.stack(faces, axis=1)


def build_cycles(xlo_table, xhi_table, ylo_table, yhi_table, index_of):
    below = jnp.concatenate(
        [
            xhi_table[index_of(-1, -1)][:, :, EDGE - 1 :],
            xhi_table[index_of(-1, 0)],
            xhi_table[index_of(-1, 1)][:, :, :1],
        ],
        axis=2,
    )
    above = jnp.concatenate(
        [
            xlo_table[index_of(1, -1)][:, :, EDGE - 1 :],
            xlo_table[index_of(1, 0)],
            xlo_table[index_of(1, 1)][:, :, :1],
        ],
        axis=2,
    )
    left_side = yhi_table[index_of(0, -1)]
    right_side = ylo_table[index_of(0, 1)]
    return (jnp.stack([below, above], axis=1), jnp.stack([left_side, right_side], axis=1))


def stream_tiles(relaxed, populations, fluid_mask, cycle_x, cycle_y):
    own_fluid = fluid_mask[:, 1 : EDGE + 1, 1 : EDGE + 1] == 1
    x_plus = crossing(0, 1)
    x_minus = crossing(0, -1)
    y_plus = crossing(1, 1)
    y_minus = crossing(1, -1)
    outputs = []
    for direction in range(19):
        step_x, step_y, step_z = LATTICE[direction]
        middle = relaxed[direction]
        if step_y == 1:
            middle = jnp.concatenate(
                [cycle_y[:, 0, y_plus.index(direction)][:, :, None], middle], axis=2
            )
            y_window = slice(0, EDGE + 1)
        elif step_y == -1:
            middle = jnp.concatenate(
                [middle, cycle_y[:, 1, y_minus.index(direction)][:, :, None]], axis=2
            )
            y_window = slice(1, EDGE + 2)
        else:
            y_window = slice(1, EDGE + 1)
        if step_x == 1:
            middle = jnp.concatenate(
                [cycle_x[:, 0, x_plus.index(direction), y_window][:, None], middle], axis=1
            )
        elif step_x == -1:
            middle = jnp.concatenate(
                [middle, cycle_x[:, 1, x_minus.index(direction), y_window][:, None]], axis=1
            )
        start_x = 1 if step_x == -1 else 0
        start_y = 1 if step_y == -1 else 0
        pulled = middle[:, start_x : start_x + EDGE, start_y : start_y + EDGE]
        source_fluid = fluid_mask[:, 1 - step_x : 1 - step_x + EDGE, 1 - step_y : 1 - step_y + EDGE]
        if step_z != 0:
            pulled = jnp.roll(pulled, step_z, axis=3)
            source_fluid = jnp.roll(source_fluid, step_z, axis=3)
        read = jnp.where(source_fluid == 1, pulled, relaxed[opposite(direction)])
        outputs.append(jnp.where(own_fluid, read, populations[direction]))
    return jnp.stack(outputs)


def face_difference(values, speeds, flags, axis_index):
    count = values.shape[axis_index]
    lower_values = lax.slice_in_dim(values, 0, count - 1, axis=axis_index)
    upper_values = lax.slice_in_dim(values, 1, count, axis=axis_index)
    lower_speeds = lax.slice_in_dim(speeds, 0, count - 1, axis=axis_index)
    upper_speeds = lax.slice_in_dim(speeds, 1, count, axis=axis_index)
    lower_flags = lax.slice_in_dim(flags, 0, count - 1, axis=axis_index)
    upper_flags = lax.slice_in_dim(flags, 1, count, axis=axis_index)
    face_vel = 0.5 * (lower_speeds + upper_speeds)
    upwind = jnp.where(face_vel > 0, lower_values, upper_values)
    face_flux = face_vel * upwind * lower_flags * upper_flags
    return lax.slice_in_dim(face_flux, 1, count - 1, axis=axis_index) - lax.slice_in_dim(
        face_flux, 0, count - 2, axis=axis_index
    )


def advect_tiles(charge, velocity, fluid_mask, cycle_x, cycle_y):
    flags_all = fluid_mask.astype(jnp.float32)
    values_x = jnp.concatenate(
        [cycle_x[:, 0, 5, 1 : EDGE + 1][:, None], charge, cycle_x[:, 1, 5, 1 : EDGE + 1][:, None]],
        axis=1,
    )
    speeds_x = jnp.concatenate(
        [
            cycle_x[:, 0, 6, 1 : EDGE + 1][:, None],
            velocity[0],
            cycle_x[:, 1, 6, 1 : EDGE + 1][:, None],
        ],
        axis=1,
    )
    term_x = face_difference(values_x, speeds_x, flags_all[:, :, 1 : EDGE + 1], 1)
    values_y = jnp.concatenate(
        [cycle_y[:, 0, 5][:, :, None], charge, cycle_y[:, 1, 5][:, :, None]], axis=2
    )
    speeds_y = jnp.concatenate(
        [cycle_y[:, 0, 6][:, :, None], velocity[1], cycle_y[:, 1, 6][:, :, None]], axis=2
    )
    term_y = face_difference(values_y, speeds_y, flags_all[:, 1 : EDGE + 1], 2)
    inner_flags = flags_all[:, 1 : EDGE + 1, 1 : EDGE + 1]
    face_vel = 0.5 * (velocity[2] + jnp.roll(velocity[2], -1, 3))
    upwind = jnp.where(face_vel > 0, charge, jnp.roll(charge, -1, 3))
    face_flux = face_vel * upwind * inner_flags * jnp.roll(inner_flags, -1, 3)
    term_z = face_flux - jnp.roll(face_flux, 1, 3)
    return term_x + term_y + term_z


def per_device(populations, charge, fluid_mask, tile_ids, phase_label, permittivity):
    groups = lax.axis_size("gy")
    tiles_dev = charge.shape[0]
    capacity = (tiles_dev + groups - 1) // groups
    band_cols = TILE_COLS * groups
    slot_index = jnp.arange(tiles_dev, dtype=jnp.int32)
    owner_peer = tile_ids % band_cols // TILE_COLS
    earlier = (owner_peer[:, None] == owner_peer[None, :]) & (
        slot_index[None, :] < slot_index[:, None]
    )
    rank_in_peer = jnp.sum(earlier.astype(jnp.int32), axis=1)
    slot_match = (
        owner_peer[None, None, :] == jnp.arange(groups, dtype=jnp.int32)[:, None, None]
    ) & (rank_in_peer[None, None, :] == jnp.arange(capacity, dtype=jnp.int32)[None, :, None])
    send_filled = jnp.any(slot_match, axis=2)
    send_slot = jnp.sum(jnp.where(slot_match, slot_index[None, None, :], 0), axis=2)
    band_ids = lax.all_gather(tile_ids, "gy", axis=0, tiled=True)
    band_table = band_ids.reshape(groups, tiles_dev)
    owner_all = band_table % band_cols // TILE_COLS
    local_all = band_table // band_cols * TILE_COLS + band_table % TILE_COLS
    earlier_all = (owner_all[:, :, None] == owner_all[:, None, :]) & (
        slot_index[None, None, :] < slot_index[None, :, None]
    )
    rank_all = jnp.sum(earlier_all.astype(jnp.int32), axis=2)
    is_mine = owner_all == lax.axis_index("gy")
    found_slot = is_mine[None] & (local_all[None] == slot_index[:, None, None])
    flat_slot = jnp.arange(groups, dtype=jnp.int32)[:, None] * capacity + rank_all
    source_index = jnp.sum(jnp.where(found_slot, flat_slot[None], 0), axis=(1, 2))
    back_match = is_mine[:, None, :] & (
        rank_all[:, None, :] == jnp.arange(capacity, dtype=jnp.int32)[None, :, None]
    )
    back_filled = jnp.any(back_match, axis=2)
    back_tile = jnp.sum(jnp.where(back_match, local_all[:, None, :], 0), axis=2)
    own_fluid = fluid_mask[:, 1 : EDGE + 1, 1 : EDGE + 1] == 1
    masked_charge = charge * own_fluid.astype(jnp.float32)
    arrived_charge = lax.all_to_all(
        spread_rows(masked_charge, send_slot, send_filled),
        "gy",
        split_axis=0,
        concat_axis=0,
        tiled=True,
    )
    source = block_from_tiles(
        arrived_charge.reshape((groups * capacity,) + arrived_charge.shape[2:])[source_index]
    )
    permit = jnp.zeros(phase_label.shape, jnp.float32)
    for phase_index in range(PHASES):
        permit = jnp.where(phase_label == phase_index, permittivity[phase_index], permit)
    permit_rim = extended(permit, (("gx", 0), ("gy", 1)), 1)
    center = permit_rim[1:-1, 1:-1]
    weights_plus = [
        harmonic(center, permit_rim[2:, 1:-1]),
        harmonic(center, permit_rim[1:-1, 2:]),
        harmonic(center, jnp.roll(center, -1, 2)),
    ]
    weights_minus = [
        harmonic(permit_rim[:-2, 1:-1], center),
        harmonic(permit_rim[1:-1, :-2], center),
        harmonic(jnp.roll(center, 1, 2), center),
    ]
    diagonal = (
        weights_plus[0]
        + weights_minus[0]
        + weights_plus[1]
        + weights_minus[1]
        + weights_plus[2]
        + weights_minus[2]
        + screening
    )
    center_value = 0.5 * (spectrum_high + spectrum_low)
    half_width = 0.5 * (spectrum_high - spectrum_low)
    ratio_value = center_value / half_width
    rho_old = 1.0 / ratio_value
    residual = source / diagonal
    update = residual / center_value
    potential = update
    for sweep_index in range(SWEEPS - 1):
        with_rim = with_margin(update)
        result = diagonal * update
        result = (
            result - weights_plus[0] * with_rim[2:, 1:-1] - weights_minus[0] * with_rim[:-2, 1:-1]
        )
        result = (
            result - weights_plus[1] * with_rim[1:-1, 2:] - weights_minus[1] * with_rim[1:-1, :-2]
        )
        result = (
            result
            - weights_plus[2] * jnp.roll(update, -1, 2)
            - weights_minus[2] * jnp.roll(update, 1, 2)
        )
        residual = residual - result / diagonal
        rho_new = 1.0 / (2.0 * ratio_value - rho_old)
        update = rho_new * rho_old * update + 2.0 * rho_new / half_width * residual
        potential = potential + update
        rho_old = rho_new
    potential_rim = with_margin(potential)
    spread = jnp.arange(EDGE + 2, dtype=jnp.int32)
    row_index = (slot_index // TILE_COLS)[:, None] * EDGE + spread[None, :]
    col_index = (slot_index % TILE_COLS)[:, None] * EDGE + spread[None, :]
    framed = potential_rim[row_index[:, :, None], col_index[:, None, :]]
    returned = lax.all_to_all(
        spread_rows(framed, back_tile, back_filled), "gy", split_axis=0, concat_axis=0, tiled=True
    )
    framed_mine = returned[owner_peer, rank_in_peer]
    inner_potential = framed_mine[:, 1:-1, 1:-1]
    field_tiles = [
        0.5 * (framed_mine[:, :-2, 1:-1] - framed_mine[:, 2:, 1:-1]),
        0.5 * (framed_mine[:, 1:-1, :-2] - framed_mine[:, 1:-1, 2:]),
        0.5 * (jnp.roll(inner_potential, 1, 3) - jnp.roll(inner_potential, -1, 3)),
    ]
    body_force = [charge * field_tiles[axis_index] for axis_index in range(3)]
    density = population_sum(populations)
    momentum = velocity_sums(populations)
    velocity = [
        (momentum[axis_index] + 0.5 * body_force[axis_index]) / density for axis_index in range(3)
    ]
    relaxed = collide(populations, density, velocity, body_force)
    package = face_package(relaxed, charge, velocity)
    gathered = lax.all_gather(package, "gy", axis=0, tiled=True)
    band_count = groups * tiles_dev
    positions = jnp.arange(band_count, dtype=jnp.int32)
    row_of = jnp.sum(
        jnp.where(band_ids[None, :] == positions[:, None], positions[None, :], 0), axis=1
    )
    low_edge = gathered[row_of[:band_cols], 0]
    high_edge = gathered[row_of[(TILE_ROWS - 1) * band_cols :], 1]
    band_rims = extended(jnp.stack([low_edge, high_edge]), (("gx", 0),), 1)
    xhi_table = jnp.concatenate([band_rims[0], gathered[:, 1]])
    xlo_table = jnp.concatenate([gathered[:, 0], band_rims[3]])
    my_row = tile_ids // band_cols
    my_col = tile_ids % band_cols

    def band_index(row_step, col_step):
        row_value = my_row + row_step
        col_value = (my_col + col_step) % band_cols
        inside = row_of[jnp.clip(row_value, 0, TILE_ROWS - 1) * band_cols + col_value]
        if row_step < 0:
            return jnp.where(row_value < 0, col_value, band_cols + inside)
        if row_step > 0:
            return jnp.where(row_value >= TILE_ROWS, band_count + col_value, inside)
        return inside

    cycle_x, cycle_y = build_cycles(
        xlo_table, xhi_table, gathered[:, 2], gathered[:, 3], band_index
    )
    populations_next = stream_tiles(relaxed, populations, fluid_mask, cycle_x, cycle_y)
    change = advect_tiles(charge, velocity, fluid_mask, cycle_x, cycle_y)
    charge_next = jnp.where(own_fluid, charge - change, charge)
    return (populations_next, charge_next, potential)


def solution(mesh):
    placed = (
        P(None, ("gx", "gy"), None, None, None),
        P(("gx", "gy"), None, None, None),
        P(("gx", "gy"), None, None, None),
        P(("gx", "gy")),
        P("gx", "gy", None),
        P(),
    )
    return jax.shard_map(
        per_device,
        mesh=mesh,
        in_specs=placed,
        out_specs=(
            P(None, ("gx", "gy"), None, None, None),
            P(("gx", "gy"), None, None, None),
            P("gx", "gy", None),
        ),
        check_vma=False,
    )
```

profile of v0, /device:TPU:0, one launch (start us, length us, event | category | flops | bytes accessed | tf_op | source)
XLA Modules:
  0.0 372.2 jit_solution(7665107541406298843)
XLA Ops:
  11.3 9.5 %all-reduce.2 = s32[32]{0:T(128)S(1)} all-reduce(s32[32]{0:T(128)S(1)} %dynamic-update-slice), channel_id=1, replica_groups=mesh['gx'=4,'gy'=8] {'gy'}, use_global_device_ids=true, to_apply=%add.2 | all-reduce | flops 32 | bytes 256
  23.1 2.1 copy_convert_fusion
  28.1 3.6 all-to-all-start
  32.4 2.8 select_select_fusion
  35.2 3.7 collective-permute-start
  50.8 2.2 broadcast_multiply_fusion.10
  53.0 3.6 collective-permute-start.4
  58.0 4.1 %collective-permute-done.5 = f32[1,32,128]{2,1,0:T(8,128)S(1)} collective-permute-done((f32[1,32,128]{2,1,0:T(8,128)S(1)}, f32[1,32,128]{2,1,0:T(8,128)S(1)}, u32[]{:S(2)}, u32[]{:S(2)}) %collective-permute-start.5) | collective-permute-done | bytes 16416 | tf_op jit(solution)/shard_map/ppermute | solution.py:48
  63.7 2.7 collective-permute-done.7
  66.4 2.8 multiply_add_fusion.3
  69.3 2.0 collective-permute-start.9
  73.0 1.9 collective-permute-done.9
  76.4 2.7 collective-permute-done.11
  79.1 2.8 multiply_add_fusion.2
  82.0 2.0 collective-permute-start.13
  85.7 1.9 collective-permute-done.13
  89.1 2.7 collective-permute-done.15
  91.8 2.9 add_add_fusion.2
  95.0 3.7 collective-permute-start.17
  100.5 14.1 %collective-permute-start.19 = (f32[34,1,128]{2,1,0:T(1,128)S(1)}, f32[34,1,128]{2,1,0:T(1,128)S(1)}, u32[]{:S(2)}, u32[]{:S(2)}) collective-permute-start(f32[34,1,128]{2,1,0:T(1,128)S(1)} %get-tuple-element.142), channel_id=1, source_target_pairs={{1,0},{2,1},{3,2},{4,3},{5,4},{6,5},{7,6},{0,7},{9,8},{10,9},{11,1... | collective-permute-start | bytes 52232 | tf_op jit(solution)/shard_map/ppermute | solution.py:49
  116.2 14.6 %gather_fusion.2 = f32[1296,128]{1,0:T(8,128)S(1)} fusion(f32[34,34,128]{2,1,0:T(8,128)S(1)} %pad_maximum_fusion.3, s32[1296]{0:T(1024)S(1)} %reshape.715), kind=kCustom, calls=%fused_computation.2 | custom fusion | bytes 1337472 | tf_op jit(solution)/shard_map/gather | solution.py:372
  130.9 1.9 gather_fusion.3
  134.4 2.4 copy.1409
  136.8 4.3 %all-to-all-start.1 = ((f32[8,1,18,18,128]{4,1,3,2,0:T(1,128)}), f32[8,1,18,18,128]{4,1,3,2,0:T(1,128)}, u32[]{:S(2)}, u32[]{:S(2)}) async-start(f32[8,1,18,18,128]{4,1,3,2,0:T(1,128)} %copy.1409), calls=%async_computation.1 | async-start | bytes 2654208 | tf_op jit(solution)/shard_map/all_to_all | solution.py:373
  141.2 4.5 %slice_bitcast_fusion.18 = (f32[4,16,16,128]{3,2,1,0:T(8,128)S(1)}, f32[1,4,16,16,128]{4,3,2,1,0:T(8,128)S(1)}, f32[1,4,16,16,128]{4,3,2,1,0:T(8,128)S(1)}, f32[...) fusion(f32[19,4,16,16,128]{4,3,2,1,0:T(8,128)} %param.6), kind=kLoop, calls=%fused_computation.569 | loop fusion | bytes 19922944 | tf_op jit(solution)/shard_map/squeeze | solution.py:120
  148.8 2.1 broadcast_multiply_fusion.8
  150.9 8.7 %all-to-all-done.1 = f32[8,1,18,18,128]{4,1,3,2,0:T(1,128)} async-done(((f32[8,1,18,18,128]{4,1,3,2,0:T(1,128)}), f32[8,1,18,18,128]{4,1,3,2,0:T(1,128)}, u32[]{:S(2)}, u32[]{:S(2)}) %all-to-all-start.1) | async-done | bytes 1327136 | tf_op jit(solution)/shard_map/all_to_all | solution.py:373
  159.5 2.8 copy.1410
  162.3 3.0 gather_fusion.4
  165.4 2.3 fusion.384
  167.7 2.4 fusion.385
  177.0 2.7 fusion.129
  181.4 1.9 fusion.94
  186.8 4.5 %fusion.84 = (f32[4,16,16,128]{3,2,0,1:T(8,128)S(1)}, f32[4,16,16,128]{3,2,0,1:T(8,128)S(1)}, f32[4,16,16,128]{3,2,0,1:T(8,128)}, f32[4,16,16,128]{3,2,0,1:T(8,1...) fusion(f32[4,16,16,128]{3,2,1,0:T(8,128)} %get-tuple-element.21, ...), kind=kLoop, calls=%fused_computation.162 | loop fusion | flops 10354688 | bytes 14680064 | tf_op jit(solution)/shard_map/add | solution.py:120
  192.3 2.5 fusion.304
  197.4 3.9 %fusion.101 = (f32[4,16,16,128]{3,2,1,0:T(8,128)S(1)}, f32[4,16,16,128]{3,2,1,0:T(8,128)S(1)}, f32[4,16,16,128]{3,2,1,0:T(8,128)S(1)}, f32[4,16,16,128]{3,2,1,0:T(8,128)}) fusion(f32[4,16,16,128]{3,2,1,0:T(8,128)S(1)} %get-tuple-element.6, f32[4,16,16,128]{3,2,1,0:T(8,128)S(1)} %get-tuple-element.22, f32[4,16,16,128]{3,2,1,0:T(8,128)S(1)} %get-tuple-element.7, ...), kind=kLoop, calls=%fused_computation.179 | loop fusion | flops 9043968 | bytes 11534336 | tf_op jit(solution)/shard_map/add | solution.py:120
  233.6 1.8 fusion.389
  241.5 2.3 fusion.18
  243.7 10.3 %all-gather.2.cloned.1.call-done = f32[32,4,7,16,128]{4,3,0,2,1:T(8,128)} async-done(((f32[4,4,7,16,128]{4,3,0,2,1:T(8,128)}), f32[32,4,7,16,128]{4,3,0,2,1:T(8,128)}) %all-gather.2.cloned.1.call-update) | async-done | bytes 7340048 | tf_op jit(solution)/shard_map/all_gather | solution.py:391
  254.1 7.1 %copy.1614 = f32[32,4,7,16,128]{4,3,2,1,0:T(8,128)} copy(f32[32,4,7,16,128]{4,3,0,2,1:T(8,128)} %all-gather.2.cloned.1.call-done) | data formatting | bytes 14680064 | tf_op jit(solution)/shard_map/all_gather | solution.py:391
  261.2 4.6 %gather_fusion.5 = f32[16,7,16,128]{3,2,1,0:T(8,128)} fusion(f32[32,4,7,16,128]{4,3,2,1,0:T(8,128)} %copy.1614, s32[16]{0:T(128)S(1)} %get-tuple-element.258), kind=kCustom, calls=%fused_computation.5 | custom fusion | bytes 1835136 | tf_op jit(solution)/shard_map/gather | solution.py:398
  265.8 2.2 copy.2331
  269.5 4.6 %gather_fusion.12 = f32[16,7,16,128]{3,2,1,0:T(8,128)} fusion(f32[32,4,7,16,128]{4,3,0,2,1:T(8,128)} %all-gather.2.cloned.1.call-done, s32[16]{0:T(128)S(1)} %get-tuple-element.257), kind=kCustom, calls=%fused_computation.12 | custom fusion | bytes 1835136 | tf_op jit(solution)/shard_map/gather | solution.py:397
  274.1 2.5 collective-permute-start.21
  276.6 5.7 %slice_bitcast_fusion = (f32[32,7,16,128]{3,2,0,1:T(8,128)}, f32[32,7,16,128]{3,2,0,1:T(8,128)S(1)}, f32[32,7,16,128]{3,2,0,1:T(8,128)}, f32[32,7,16,128]{3,2,0,1:T(8,128)}) fusion(f32[32,4,7,16,128]{4,3,0,2,1:T(8,128)} %all-gather.2.cloned.1.call-done), kind=kLoop, calls=%fused_computation.25 | loop fusion | bytes 14680064 | tf_op jit(solution)/shard_map/squeeze | solution.py:416
  283.7 2.7 gather_fusion.20
  288.1 2.1 fusion.140
  290.2 2.9 copy.1638
  293.1 2.7 gather_fusion.22
  297.4 2.1 fusion.139
  299.6 2.7 slice_multiply_fusion
  302.2 2.1 fusion.138
  304.4 2.1 fusion.137
  306.5 1.9 pad_maximum_fusion
  310.1 2.3 gather_fusion.9
  312.5 2.3 gather_fusion.7
  314.9 2.3 gather_fusion.11
  318.6 1.9 pad_maximum_fusion.1
  322.3 3.0 gather_fusion.16
  325.3 3.0 gather_fusion.14
  329.3 3.2 gather_fusion.18
  335.3 1.9 fusion.6
  337.2 3.8 %fusion.208 = (f32[1,4,16,16,128]{4,3,1,2,0:T(8,128)S(1)}, f32[1,4,16,16,128]{4,3,1,2,0:T(8,128)S(1)}, f32[1,4,16,16,128]{4,3,1,2,0:T(8,128)S(1)}) fusion(f32[4,16,16,128]{3,2,0,1:T(8,128)} %get-tuple-element.87, f32[4,1,16,128]{3,2,0,1:T(8,128)S(1)} %get-tuple-element.220, f32[4,16,16,128]{3,2,0,1:T(8,128)} %get-tuple-element.97, ...), kind=kLoop, calls=%fused_computation.308 | loop fusion | flops 1966080 | bytes 7962624 | tf_op jit(solution)/shard_map/stack | solution.py:224
  342.7 2.1 fusion.205
  (613 shorter events, 128.3 us)
Async XLA Ops:
  7.2 24.5 %copy-start.166 = (f32[4]{0:T(128)S(1)}, f32[4]{0:T(128)}, u32[]{:S(2)}) copy-start(f32[4]{0:T(128)} %param.11) | copy-start | bytes 52
  7.2 25.2 %copy-start.145 = (s32[32,32,128]{2,1,0:T(8,128)S(1)}, s32[32,32,128]{2,1,0:T(8,128)}, u32[]{:S(2)}) copy-start(s32[32,32,128]{2,1,0:T(8,128)} %param.10) | copy-start | bytes 1572868
  28.1 18.9 %all-to-all-start = ((f32[8,1,16,16,128]{4,3,2,1,0:T(8,128)}), f32[8,1,16,16,128]{4,3,2,1,0:T(8,128)S(1)}, u32[]{:S(2)}, u32[]{:S(2)}) async-start(f32[8,1,16,16,128]{4,3,2,1,0:T(8,128)} %fusion), calls=%async_computation | async-start | bytes 2097152 | tf_op jit(solution)/shard_map/all_to_all | solution.py:308
  35.2 8.2 %collective-permute-start = (f32[1,32,128]{2,1,0:T(8,128)S(1)}, f32[1,32,128]{2,1,0:T(8,128)S(1)}, u32[]{:S(2)}, u32[]{:S(2)}) collective-permute-start(f32[1,32,128]{2,1,0:T(8,128)S(1)} %get-tuple-element.210), channel_id=1, source_target_pairs={{8,0},{16,8},{24,16},{0,24},{9,1},{17,9},{25,17},{1,25},{10,2},{18... | collective-permute-start | bytes 49160 | tf_op jit(solution)/shard_map/ppermute | solution.py:49
  38.8 5.5 %collective-permute-start.1 = (f32[1,32,128]{2,1,0:T(8,128)S(1)}, f32[1,32,128]{2,1,0:T(8,128)S(1)}, u32[]{:S(2)}, u32[]{:S(2)}) collective-permute-start(f32[1,32,128]{2,1,0:T(8,128)S(1)} %get-tuple-element.209), channel_id=1, source_target_pairs={{0,8},{8,16},{16,24},{24,0},{1,9},{9,17},{17,25},{25,1},{2,10},{10... | collective-permute-start | bytes 49160 | tf_op jit(solution)/shard_map/ppermute | solution.py:48
  45.0 4.5 %collective-permute-start.2 = (f32[34,1,128]{2,1,0:T(1,128)}, f32[34,1,128]{2,1,0:T(1,128)}, u32[]{:S(2)}, u32[]{:S(2)}) collective-permute-start(f32[34,1,128]{2,1,0:T(1,128)} %get-tuple-element.149), channel_id=1, source_target_pairs={{1,0},{2,1},{3,2},{4,3},{5,4},{6,5},{7,6},{0,7},{9,8},{10,9},{11,1... | collective-permute-start | bytes 52232 | tf_op jit(solution)/shard_map/ppermute | solution.py:49
  46.4 4.4 %collective-permute-start.3 = (f32[34,1,128]{2,1,0:T(1,128)}, f32[34,1,128]{2,1,0:T(1,128)}, u32[]{:S(2)}, u32[]{:S(2)}) collective-permute-start(f32[34,1,128]{2,1,0:T(1,128)} %get-tuple-element.150), channel_id=1, source_target_pairs={{0,1},{1,2},{2,3},{3,4},{4,5},{5,6},{6,7},{7,0},{8,9},{9,10},{10,1... | collective-permute-start | bytes 52232 | tf_op jit(solution)/shard_map/ppermute | solution.py:48
  53.0 5.0 %collective-permute-start.4 = (f32[1,32,128]{2,1,0:T(8,128)S(1)}, f32[1,32,128]{2,1,0:T(8,128)S(1)}, u32[]{:S(2)}, u32[]{:S(2)}) collective-permute-start(f32[1,32,128]{2,1,0:T(8,128)S(1)} %get-tuple-element.200), channel_id=1, source_target_pairs={{8,0},{16,8},{24,16},{0,24},{9,1},{17,9},{25,17},{1,25},{10,2},{18... | collective-permute-start | bytes 49160 | tf_op jit(solution)/shard_map/ppermute | solution.py:49
  56.6 5.5 %collective-permute-start.5 = (f32[1,32,128]{2,1,0:T(8,128)S(1)}, f32[1,32,128]{2,1,0:T(8,128)S(1)}, u32[]{:S(2)}, u32[]{:S(2)}) collective-permute-start(f32[1,32,128]{2,1,0:T(8,128)S(1)} %get-tuple-element.199), channel_id=1, source_target_pairs={{0,8},{8,16},{16,24},{24,0},{1,9},{9,17},{17,25},{25,1},{2,10},{10... | collective-permute-start | bytes 49160 | tf_op jit(solution)/shard_map/ppermute | solution.py:48
  62.2 1.5 collective-permute-start.6
  62.2 4.1 %collective-permute-start.7 = (f32[34,1,128]{2,1,0:T(1,128)S(1)}, f32[34,1,128]{2,1,0:T(1,128)S(1)}, u32[]{:S(2)}, u32[]{:S(2)}) collective-permute-start(f32[34,1,128]{2,1,0:T(1,128)S(1)} %get-tuple-element.148), channel_id=1, source_target_pairs={{0,1},{1,2},{2,3},{3,4},{4,5},{5,6},{6,7},{7,0},{8,9},{9,10},{10,1... | collective-permute-start | bytes 52232 | tf_op jit(solution)/shard_map/ppermute | solution.py:48
  69.2 3.8 %collective-permute-start.8 = (f32[1,32,128]{2,1,0:T(8,128)S(1)}, f32[1,32,128]{2,1,0:T(8,128)S(1)}, u32[]{:S(2)}, u32[]{:S(2)}) collective-permute-start(f32[1,32,128]{2,1,0:T(8,128)S(1)} %get-tuple-element.194), channel_id=1, source_target_pairs={{8,0},{16,8},{24,16},{0,24},{9,1},{17,9},{25,17},{1,25},{10,2},{18... | collective-permute-start | bytes 49160 | tf_op jit(solution)/shard_map/ppermute | solution.py:49
  69.3 5.5 %collective-permute-start.9 = (f32[1,32,128]{2,1,0:T(8,128)S(1)}, f32[1,32,128]{2,1,0:T(8,128)S(1)}, u32[]{:S(2)}, u32[]{:S(2)}) collective-permute-start(f32[1,32,128]{2,1,0:T(8,128)S(1)} %get-tuple-element.193), channel_id=1, source_target_pairs={{0,8},{8,16},{16,24},{24,0},{1,9},{9,17},{17,25},{25,1},{2,10},{10... | collective-permute-start | bytes 49160 | tf_op jit(solution)/shard_map/ppermute | solution.py:48
  74.9 23.8 %copy-start.175 = (s32[4]{0:T(128)S(1)}, s32[4]{0:T(128)}, u32[]{:S(2)}) copy-start(s32[4]{0:T(128)} %fusion.348) | copy-start | bytes 52
  74.9 23.8 %copy-start.176 = (s32[4]{0:T(128)S(1)}, s32[4]{0:T(128)}, u32[]{:S(2)}) copy-start(s32[4]{0:T(128)} %fusion.349) | copy-start | bytes 52
  74.9 1.5 collective-permute-start.10
  74.9 4.1 %collective-permute-start.11 = (f32[34,1,128]{2,1,0:T(1,128)S(1)}, f32[34,1,128]{2,1,0:T(1,128)S(1)}, u32[]{:S(2)}, u32[]{:S(2)}) collective-permute-start(f32[34,1,128]{2,1,0:T(1,128)S(1)} %get-tuple-element.146), channel_id=1, source_target_pairs={{0,1},{1,2},{2,3},{3,4},{4,5},{5,6},{6,7},{7,0},{8,9},{9,10},{10,1... | collective-permute-start | bytes 52232 | tf_op jit(solution)/shard_map/ppermute | solution.py:48
  81.9 3.8 %collective-permute-start.12 = (f32[1,32,128]{2,1,0:T(8,128)S(1)}, f32[1,32,128]{2,1,0:T(8,128)S(1)}, u32[]{:S(2)}, u32[]{:S(2)}) collective-permute-start(f32[1,32,128]{2,1,0:T(8,128)S(1)} %get-tuple-element.188), channel_id=1, source_target_pairs={{8,0},{16,8},{24,16},{0,24},{9,1},{17,9},{25,17},{1,25},{10,2},{18... | collective-permute-start | bytes 49160 | tf_op jit(solution)/shard_map/ppermute | solution.py:49
  82.0 5.6 %collective-permute-start.13 = (f32[1,32,128]{2,1,0:T(8,128)S(1)}, f32[1,32,128]{2,1,0:T(8,128)S(1)}, u32[]{:S(2)}, u32[]{:S(2)}) collective-permute-start(f32[1,32,128]{2,1,0:T(8,128)S(1)} %get-tuple-element.187), channel_id=1, source_target_pairs={{0,8},{8,16},{16,24},{24,0},{1,9},{9,17},{17,25},{25,1},{2,10},{10... | collective-permute-start | bytes 49160 | tf_op jit(solution)/shard_map/ppermute | solution.py:48
  87.6 1.5 collective-permute-start.14
  87.7 4.1 %collective-permute-start.15 = (f32[34,1,128]{2,1,0:T(1,128)S(1)}, f32[34,1,128]{2,1,0:T(1,128)S(1)}, u32[]{:S(2)}, u32[]{:S(2)}) collective-permute-start(f32[34,1,128]{2,1,0:T(1,128)S(1)} %get-tuple-element.144), channel_id=1, source_target_pairs={{0,1},{1,2},{2,3},{3,4},{4,5},{5,6},{6,7},{7,0},{8,9},{9,10},{10,1... | collective-permute-start | bytes 52232 | tf_op jit(solution)/shard_map/ppermute | solution.py:48
  91.8 40.9 %copy-start.172 = (pred[8]{0:T(512)(128)(4,1)S(1)}, pred[8]{0:T(512)(128)(4,1)}, u32[]{:S(2)}) copy-start(pred[8]{0:T(512)(128)(4,1)} %get-tuple-element.40) | copy-start | bytes 28
  94.8 42.1 %copy-start.84 = (f32[32,32,128]{2,1,0:T(8,128)}, f32[32,32,128]{2,1,0:T(8,128)S(1)}, u32[]{:S(2)}) copy-start(f32[32,32,128]{2,1,0:T(8,128)S(1)} %add_add_fusion.2) | copy-start | bytes 1572868
  94.8 5.6 %collective-permute-start.16 = (f32[1,32,128]{2,1,0:T(8,128)S(1)}, f32[1,32,128]{2,1,0:T(8,128)S(1)}, u32[]{:S(2)}, u32[]{:S(2)}) collective-permute-start(f32[1,32,128]{2,1,0:T(8,128)S(1)} %get-tuple-element.185), channel_id=1, source_target_pairs={{0,8},{8,16},{16,24},{24,0},{1,9},{9,17},{17,25},{25,1},{2,10},{10... | collective-permute-start | bytes 49160 | tf_op jit(solution)/shard_map/ppermute | solution.py:48
  95.0 5.4 %collective-permute-start.17 = (f32[1,32,128]{2,1,0:T(8,128)S(1)}, f32[1,32,128]{2,1,0:T(8,128)S(1)}, u32[]{:S(2)}, u32[]{:S(2)}) collective-permute-start(f32[1,32,128]{2,1,0:T(8,128)S(1)} %get-tuple-element.186), channel_id=1, source_target_pairs={{8,0},{16,8},{24,16},{0,24},{9,1},{17,9},{25,17},{1,25},{10,2},{18... | collective-permute-start | bytes 49160 | tf_op jit(solution)/shard_map/ppermute | solution.py:49
  100.4 14.4 %collective-permute-start.18 = (f32[34,1,128]{2,1,0:T(1,128)S(1)}, f32[34,1,128]{2,1,0:T(1,128)S(1)}, u32[]{:S(2)}, u32[]{:S(2)}) collective-permute-start(f32[34,1,128]{2,1,0:T(1,128)S(1)} %get-tuple-element.141), channel_id=1, source_target_pairs={{0,1},{1,2},{2,3},{3,4},{4,5},{5,6},{6,7},{7,0},{8,9},{9,10},{10,1... | collective-permute-start | bytes 52232 | tf_op jit(solution)/shard_map/ppermute | solution.py:48
  100.5 15.6 %collective-permute-start.19 = (f32[34,1,128]{2,1,0:T(1,128)S(1)}, f32[34,1,128]{2,1,0:T(1,128)S(1)}, u32[]{:S(2)}, u32[]{:S(2)}) collective-permute-start(f32[34,1,128]{2,1,0:T(1,128)S(1)} %get-tuple-element.142), channel_id=1, source_target_pairs={{1,0},{2,1},{3,2},{4,3},{5,4},{6,5},{7,6},{0,7},{9,8},{10,9},{11,1... | collective-permute-start | bytes 52232 | tf_op jit(solution)/shard_map/ppermute | solution.py:49
  116.1 25.0 %copy-start.174 = (s32[4]{0:T(128)S(1)}, s32[4]{0:T(128)}, u32[]{:S(2)}) copy-start(s32[4]{0:T(128)} %copy-done.173) | copy-start | bytes 52
  116.1 25.0 %copy-start.178 = (s32[4]{0:T(128)S(1)}, s32[4]{0:T(128)}, u32[]{:S(2)}) copy-start(s32[4]{0:T(128)} %copy-done.177) | copy-start | bytes 52
  136.8 22.7 %all-to-all-start.1 = ((f32[8,1,18,18,128]{4,1,3,2,0:T(1,128)}), f32[8,1,18,18,128]{4,1,3,2,0:T(1,128)}, u32[]{:S(2)}, u32[]{:S(2)}) async-start(f32[8,1,18,18,128]{4,1,3,2,0:T(1,128)} %copy.1409), calls=%async_computation.1 | async-start | bytes 2654208 | tf_op jit(solution)/shard_map/all_to_all | solution.py:373
  141.1 112.9 %all-gather.2.cloned.1.call-start = ((), (), s32[]{:S(2)}) async-start(), calls=%async_computation.2 | async-start | bytes 8257536 | tf_op jit(solution)/shard_map/all_gather | solution.py:391
  148.8 22.9 %copy-start.12 = (f32[4,16,16,128]{3,2,1,0:T(8,128)S(1)}, f32[4,16,16,128]{3,2,1,0:T(8,128)}, u32[]{:S(2)}) copy-start(f32[4,16,16,128]{3,2,1,0:T(8,128)} %param.7) | copy-start | bytes 1572868
  150.9 22.3 %copy-start.1 = (f32[4,16,16,128]{3,2,0,1:T(8,128)}, f32[4,16,16,128]{3,2,0,1:T(8,128)S(1)}, u32[]{:S(2)}) copy-start(f32[4,16,16,128]{3,2,0,1:T(8,128)S(1)} %get-tuple-element.37) | copy-start | bytes 1572868
  159.5 13.6 %slice-start = ((s8[9961472]{0:T(1024)(128)(4,1)}), s8[1572864]{0:T(1024)(128)(4,1)S(1)}, s32[]{:S(2)}) async-start(s8[9961472]{0:T(1024)(128)(4,1)} %bitcast.490), calls=%async_computation.3 | async-start | bytes 3145728
  171.9 30.5 %copy-start.70 = (f32[4,16,16,128]{3,2,0,1:T(8,128)}, f32[4,16,16,128]{3,2,0,1:T(8,128)S(1)}, u32[]{:S(2)}) copy-start(f32[4,16,16,128]{3,2,0,1:T(8,128)S(1)} %get-tuple-element.166) | copy-start | bytes 1572868
  175.7 16.6 %copy-start.8 = (f32[4,16,16,128]{3,2,1,0:T(8,128)}, f32[4,16,16,128]{3,2,1,0:T(8,128)S(1)}, u32[]{:S(2)}) copy-start(f32[4,16,16,128]{3,2,1,0:T(8,128)S(1)} %get-tuple-element.177) | copy-start | bytes 1572868
  175.7 20.2 %copy-start.3 = (f32[4,16,16,128]{3,2,1,0:T(8,128)}, f32[4,16,16,128]{3,2,1,0:T(8,128)S(1)}, u32[]{:S(2)}) copy-start(f32[4,16,16,128]{3,2,1,0:T(8,128)S(1)} %get-tuple-element.175) | copy-start | bytes 1572868
  176.2 19.8 %copy-start.5 = (f32[4,16,16,128]{3,2,0,1:T(8,128)}, f32[4,16,16,128]{3,2,0,1:T(8,128)S(1)}, u32[]{:S(2)}) copy-start(f32[4,16,16,128]{3,2,0,1:T(8,128)S(1)} %get-tuple-element.180) | copy-start | bytes 1572868
  176.2 21.1 %copy-start.16 = (f32[4,16,16,128]{3,2,0,1:T(8,128)}, f32[4,16,16,128]{3,2,0,1:T(8,128)S(1)}, u32[]{:S(2)}) copy-start(f32[4,16,16,128]{3,2,0,1:T(8,128)S(1)} %get-tuple-element.182) | copy-start | bytes 1572868
  183.3 14.0 %copy-start.23 = (f32[4,16,16,128]{3,2,0,1:T(8,128)}, f32[4,16,16,128]{3,2,0,1:T(8,128)S(1)}, u32[]{:S(2)}) copy-start(f32[4,16,16,128]{3,2,0,1:T(8,128)S(1)} %get-tuple-element.173) | copy-start | bytes 1572868
  184.3 13.0 %copy-start.19 = (f32[4,16,16,128]{3,2,1,0:T(8,128)}, f32[4,16,16,128]{3,2,1,0:T(8,128)S(1)}, u32[]{:S(2)}) copy-start(f32[4,16,16,128]{3,2,1,0:T(8,128)S(1)} %get-tuple-element.60) | copy-start | bytes 1572868
  184.3 17.2 %copy-start.25 = (f32[4,16,16,128]{3,2,1,0:T(8,128)}, f32[4,16,16,128]{3,2,1,0:T(8,128)S(1)}, u32[]{:S(2)}) copy-start(f32[4,16,16,128]{3,2,1,0:T(8,128)S(1)} %get-tuple-element.16) | copy-start | bytes 1572868
  197.4 12.2 %copy-start.169 = (s32[4]{0:T(128)S(1)}, s32[4]{0:T(128)}, u32[]{:S(2)}) copy-start(s32[4]{0:T(128)} %get-tuple-element.12) | copy-start | bytes 52
  197.4 13.5 %copy-start.168 = (s32[4]{0:T(128)S(1)}, s32[4]{0:T(128)}, u32[]{:S(2)}) copy-start(s32[4]{0:T(128)} %get-tuple-element.8) | copy-start | bytes 52
  197.4 14.8 %copy-start = (s32[4,18,18,128]{3,0,2,1:T(4,128)S(1)}, s32[4,18,18,128]{3,0,2,1:T(4,128)}, u32[]{:S(2)}) copy-start(s32[4,18,18,128]{3,0,2,1:T(4,128)} %param.8) | copy-start | bytes 1990660
  268.0 38.5 %collective-permute-start.20 = (f32[1,16,7,16,128]{4,3,1,2,0:T(8,128)}, f32[1,16,7,16,128]{4,3,1,2,0:T(8,128)}, u32[]{:S(2)}, u32[]{:S(2)}) collective-permute-start(f32[1,16,7,16,128]{4,3,1,2,0:T(8,128)} %bitcast.482), channel_id=1, source_target_pairs={{0,8},{8,16},{16,24},{24,0},{1,9},{9,17},{17,25},{25,1},{2,10},{10... | collective-permute-start | bytes 2752520 | tf_op jit(solution)/shard_map/ppermute | solution.py:48
  274.1 25.4 %copy-start.4 = (f32[4,16,16,128]{3,2,1,0:T(8,128)S(1)}, f32[4,16,16,128]{3,2,1,0:T(8,128)}, u32[]{:S(2)}) copy-start(f32[4,16,16,128]{3,2,1,0:T(8,128)} %copy-done.3) | copy-start | bytes 1572868
  274.1 44.5 %collective-permute-start.21 = (f32[1,16,7,16,128]{4,3,2,1,0:T(8,128)}, f32[1,16,7,16,128]{4,3,2,1,0:T(8,128)}, u32[]{:S(2)}, u32[]{:S(2)}) collective-permute-start(f32[1,16,7,16,128]{4,3,2,1,0:T(8,128)} %bitcast.502), channel_id=1, source_target_pairs={{8,0},{16,8},{24,16},{0,24},{9,1},{17,9},{25,17},{1,25},{10,2},{18... | collective-permute-start | bytes 2752520 | tf_op jit(solution)/shard_map/ppermute | solution.py:49
  297.4 20.5 %copy-start.146 = (f32[4,1,1,16,128]{4,3,0,2,1:T(8,128)}, f32[4,1,1,16,128]{4,3,0,2,1:T(8,128)S(1)}, u32[]{:S(2)}) copy-start(f32[4,1,1,16,128]{4,3,0,2,1:T(8,128)S(1)} %get-tuple-element.234) | copy-start | bytes 98308
  297.4 20.5 %copy-start.150 = (f32[4,1,1,16,128]{4,3,0,2,1:T(8,128)}, f32[4,1,1,16,128]{4,3,0,2,1:T(8,128)S(1)}, u32[]{:S(2)}) copy-start(f32[4,1,1,16,128]{4,3,0,2,1:T(8,128)S(1)} %get-tuple-element.235) | copy-start | bytes 98308
  320.6 24.3 %slice-start.3 = ((s8[9961472]{0:T(1024)(128)(4,1)}), s8[1572864]{0:T(1024)(128)(4,1)S(1)}, s32[]{:S(2)}) async-start(s8[9961472]{0:T(1024)(128)(4,1)} %bitcast.492), calls=%async_computation.6 | async-start | bytes 3145728
  332.4 12.4 %copy-start.143 = (pred[4,16,16,128]{3,2,0,1:T(8,128)(4,1)S(1)}, pred[4,16,16,128]{3,2,0,1:T(8,128)(4,1)}, u32[]{:S(2)}) copy-start(pred[4,16,16,128]{3,2,0,1:T(8,128)(4,1)} %get-tuple-element.282) | copy-start | bytes 393220
  332.4 12.4 %copy-start.160 = (f32[4,1,1,16,128]{4,3,0,2,1:T(8,128)S(1)}, f32[4,1,1,16,128]{4,3,0,2,1:T(8,128)}, u32[]{:S(2)}) copy-start(f32[4,1,1,16,128]{4,3,0,2,1:T(8,128)} %get-tuple-element.238) | copy-start | bytes 98308
  332.5 13.5 %copy-start.7 = (f32[4,16,16,128]{3,2,0,1:T(8,128)S(1)}, f32[4,16,16,128]{3,2,0,1:T(8,128)}, u32[]{:S(2)}) copy-start(f32[4,16,16,128]{3,2,0,1:T(8,128)} %copy-done.5) | copy-start | bytes 1572868
  332.5 13.5 %copy-start.18 = (f32[4,16,16,128]{3,2,0,1:T(8,128)S(1)}, f32[4,16,16,128]{3,2,0,1:T(8,128)}, u32[]{:S(2)}) copy-start(f32[4,16,16,128]{3,2,0,1:T(8,128)} %copy-done.16) | copy-start | bytes 1572868
  332.5 13.5 %copy-start.22 = (f32[4,16,16,128]{3,2,1,0:T(8,128)S(1)}, f32[4,16,16,128]{3,2,1,0:T(8,128)}, u32[]{:S(2)}) copy-start(f32[4,16,16,128]{3,2,1,0:T(8,128)} %copy-done.21) | copy-start | bytes 1572868
  332.5 13.4 %copy-start.42 = (f32[4,16,16,128]{3,2,0,1:T(8,128)S(1)}, f32[4,16,16,128]{3,2,0,1:T(8,128)}, u32[]{:S(2)}) copy-start(f32[4,16,16,128]{3,2,0,1:T(8,128)} %get-tuple-element.36) | copy-start | bytes 1572868
  332.5 13.4 %copy-start.51 = (f32[4,16,16,128]{3,2,0,1:T(8,128)S(1)}, f32[4,16,16,128]{3,2,0,1:T(8,128)}, u32[]{:S(2)}) copy-start(f32[4,16,16,128]{3,2,0,1:T(8,128)} %copy-done.49) | copy-start | bytes 1572868
  332.5 13.4 %copy-start.54 = (f32[4,16,16,128]{3,2,0,1:T(8,128)S(1)}, f32[4,16,16,128]{3,2,0,1:T(8,128)}, u32[]{:S(2)}) copy-start(f32[4,16,16,128]{3,2,0,1:T(8,128)} %copy-done.52) | copy-start | bytes 1572868
  332.5 13.4 %copy-start.69 = (f32[4,16,16,128]{3,2,1,0:T(8,128)S(1)}, f32[4,16,16,128]{3,2,1,0:T(8,128)}, u32[]{:S(2)}) copy-start(f32[4,16,16,128]{3,2,1,0:T(8,128)} %get-tuple-element.5) | copy-start | bytes 1572868
  332.5 13.4 %copy-start.86 = (f32[4,16,16,128]{3,2,0,1:T(8,128)S(1)}, f32[4,16,16,128]{3,2,0,1:T(8,128)}, u32[]{:S(2)}) copy-start(f32[4,16,16,128]{3,2,0,1:T(8,128)} %copy-done.85) | copy-start | bytes 1572868
  332.5 13.4 %copy-start.112 = (s32[4,16,16,1]{3,2,0,1:T(8,128)S(1)}, s32[4,16,16,1]{3,2,0,1:T(8,128)}, u32[]{:S(2)}) copy-start(s32[4,16,16,1]{3,2,0,1:T(8,128)} %copy.1754) | copy-start | bytes 12292
  332.5 13.4 %copy-start.113 = (s32[4,16,16,127]{3,2,0,1:T(8,128)S(1)}, s32[4,16,16,127]{3,2,0,1:T(8,128)}, u32[]{:S(2)}) copy-start(s32[4,16,16,127]{3,2,0,1:T(8,128)} %copy.1755) | copy-start | bytes 1560580
  332.6 13.4 %copy-start.115 = (f32[4,16,16,1]{3,2,1,0:T(8,128)S(1)}, f32[4,16,16,1]{3,2,1,0:T(8,128)}, u32[]{:S(2)}) copy-start(f32[4,16,16,1]{3,2,1,0:T(8,128)} %slice.1211) | copy-start | bytes 12292
  (146 other events, 857.2 us)
Sparse Core Ops, SparseCore 0:
  204.4 49.5 all-gather.1
where the time goes:
time: 376 us; the launch traced here: 372 us
  local copies, waits for them, and re-layouts  153 us (41%)
  other arithmetic  101 us (27%)
  waiting for transfers between devices  46.6 us (12%)
  starting transfers between devices  44.3 us (12%)
  between operations  17.5 us (5%)
  blocking collectives  9.46 us (3%)
    unnamed x419, local copies, waits for them, and re-layouts  30.9 us
    ppermute x11, starting transfers between devices, extended(): after = lax.ppermute(first, axis, down)  29.2 us
    ppermute x11, waiting for transfers between devices, extended(): before = lax.ppermute(last, axis, up)  19.7 us
    unnamed x17, other arithmetic  19.6 us
    add x7, other arithmetic, collide(): population[direction] - (population[direction] - equilibrium) / relax_time  16.4 us
    gather x2, local copies, waits for them, and re-layouts, per_device(): framed = potential_rim[row_index[:, :, None], col_index[:, None, :]]  14.7 us
    all_gather x1, waiting for transfers between devices, per_device(): gathered = lax.all_gather(package, 'gy', axis=0, tiled=True)  10.3 us
    unnamed x1, blocking collectives  9.46 us
  transfers between devices with their start and end apart: 25, of which 19 were waited for; matrix products, arithmetic and copies ran while one was open for 28% of the time, Pallas kernels for 0%

commit v1 on v0

v1 whole, which is shorter than its diff:
```python
import functools

import jax
import jax.numpy as jnp
from jax import lax
from jax.experimental import pallas as pl
from jax.experimental.pallas import tpu as pltpu
from jax.sharding import PartitionSpec as P

EDGE = 16
DEPTH = 128
TILE_ROWS = 2
TILE_COLS = 2
PHASES = 4
SWEEPS = 4

LATTICE = (
    (0, 0, 0),
    (1, 0, 0),
    (-1, 0, 0),
    (0, 1, 0),
    (0, -1, 0),
    (0, 0, 1),
    (0, 0, -1),
    (1, 1, 0),
    (-1, -1, 0),
    (1, -1, 0),
    (-1, 1, 0),
    (1, 0, 1),
    (-1, 0, -1),
    (1, 0, -1),
    (-1, 0, 1),
    (0, 1, 1),
    (0, -1, -1),
    (0, 1, -1),
    (0, -1, 1),
)
relax_time = 0.8
screening = 0.001
spectrum_low = 0.1
spectrum_high = 2.0

AREA = EDGE * EDGE
SIDE = 8
RING = 2
WIDE = RING + SWEEPS - 1
WIDER = WIDE + 1
FRAME = EDGE + 2 * RING
PADDED = EDGE + 2 * SIDE
CHANNELS = 10
HALVES = 2 * CHANNELS
VMEM = pl.BlockSpec(memory_space=pltpu.VMEM)
SMEM = pl.BlockSpec(memory_space=pltpu.SMEM)
PARAMS = pltpu.CompilerParams(vmem_limit_bytes=56 * 2**20)


def crossing(axis_index, face_sign):
    return [q for q in range(19) if LATTICE[q][axis_index] == face_sign]


def opposite(direction):
    return LATTICE.index(tuple(-entry for entry in LATTICE[direction]))


def lattice_weight(direction):
    return (1.0 / 3.0, 1.0 / 18.0, 1.0 / 36.0)[sum(abs(e) for e in LATTICE[direction])]


def along(direction, vector):
    total = None
    for entry, part in zip(LATTICE[direction], vector):
        if entry:
            term = part if entry > 0 else -part
            total = term if total is None else total + term
    return total


def moments(pops):
    density = pops[0]
    for q in range(1, 19):
        density = density + pops[q]
    momentum = []
    for axis in range(3):
        plus = sum_of([pops[q] for q in crossing(axis, 1)])
        minus = sum_of([pops[q] for q in crossing(axis, -1)])
        momentum.append(plus - minus)
    return density, momentum


def sum_of(values):
    total = values[0]
    for value in values[1:]:
        total = total + value
    return total


def collide(pops, density, momentum, force):
    source_scale = 1.0 - 0.5 / relax_time
    gain = 1.0 / relax_time
    inverse = 1.0 / density
    carried = [m + 0.5 * f for m, f in zip(momentum, force)]
    velocity = [c * inverse for c in carried]
    energy = sum_of([c * v for c, v in zip(carried, velocity)])
    power = sum_of([v * f for v, f in zip(velocity, force)])
    base = gain * density - (1.5 * gain) * energy - (3.0 * source_scale) * power
    relaxed = {}
    for q in pops:
        weight = lattice_weight(q)
        kept = (1.0 - gain) * pops[q]
        if q == 0:
            relaxed[q] = kept + weight * base
            continue
        if q in relaxed:
            continue
        p, g, rp = along(q, velocity), along(q, force), along(q, carried)
        even = weight * base + p * ((4.5 * gain * weight) * rp + (9.0 * source_scale * weight) * g)
        odd = (3.0 * gain * weight) * rp + (3.0 * source_scale * weight) * g
        relaxed[q] = kept + (even + odd)
        back = opposite(q)
        if back in pops:
            relaxed[back] = (1.0 - gain) * pops[back] + (even - odd)
    return relaxed, velocity


def ring_pairs(axis):
    size = lax.axis_size(axis)
    up = [(i, (i + 1) % size) for i in range(size)]
    return up, [(j, i) for i, j in up]


def pack_source(tiles, band_cols, ids, charge, mask, out):
    out[...] = jnp.zeros_like(out)
    lane = lax.broadcasted_iota(jnp.int32, (8, DEPTH), 1)
    header = jnp.zeros((8, DEPTH), jnp.int32)
    for t in range(tiles):
        owner = ids[t] % band_cols // TILE_COLS
        header = jnp.where(lane == t, ids[t], header)
        for i in range(EDGE):
            flags = mask[t, i + 1, 1 : EDGE + 1, :].astype(jnp.float32)
            out[owner, pl.ds(i * EDGE, EDGE), :] = charge[t, pl.ds(i * EDGE, EDGE), :] * flags
    for peer in range(out.shape[0]):
        out[peer, pl.ds(AREA, 8), :] = header.astype(jnp.float32)


def assemble(hold, arrived, block, left, right):
    for local in range(TILE_ROWS * TILE_COLS):
        r, c = local // TILE_COLS, local % TILE_COLS
        slot = hold[local]
        for i in range(EDGE):
            row = r * EDGE + i
            cells = arrived[slot, pl.ds(i * EDGE, EDGE), :]
            block[row, pl.ds(c * EDGE, EDGE), :] = cells
            if c == 0:
                left[row] = cells[:SIDE]
            if c == TILE_COLS - 1:
                right[row] = cells[EDGE - SIDE :]


def harmonic(a, b):
    return 2.0 * a * b / (a + b)


def face_weights(table, labels, before, after, wx, wy, wz, inverse, permit):
    rows = labels.shape[0]
    total = rows + 2 * WIDER

    def look(label):
        value = jnp.full(label.shape, table[PHASES - 1], jnp.float32)
        for phase in range(PHASES - 1):
            value = jnp.where(label == phase, table[phase], value)
        return value

    for row in range(WIDER):
        permit[row] = look(before[row])
        permit[WIDER + rows + row] = look(after[row])

    def fill(row, carry):
        permit[WIDER + row] = look(labels[row])
        return carry

    lax.fori_loop(0, rows, fill, 0, unroll=2)
    width = labels.shape[1]
    wx[0] = harmonic(permit[0], permit[1])

    def weigh(row, carry):
        here = permit[row]
        x_plus = harmonic(here, permit[row + 1])
        y_plus = harmonic(here, pltpu.roll(here, width - 1, 0))
        z_plus = harmonic(here, pltpu.roll(here, DEPTH - 1, 1))
        wx[row] = x_plus
        wy[row] = y_plus
        wz[row] = z_plus
        diagonal = x_plus + wx[row - 1] + y_plus + pltpu.roll(y_plus, 1, 0)
        diagonal = diagonal + z_plus + pltpu.roll(z_plus, 1, 1) + screening
        inverse[row] = 1.0 / diagonal
        return carry

    lax.fori_loop(1, total - 1, weigh, 0, unroll=2)


def solve(hold, middle, before, after, wx, wy, wz, inverse, out, frames, u0, u1, residual, potential):
    rows, width = middle.shape[0], middle.shape[1]
    center_value = 0.5 * (spectrum_high + spectrum_low)
    half_width = 0.5 * (spectrum_high - spectrum_low)
    ratio = center_value / half_width

    def start(row, source):
        r = source * inverse[row]
        residual[row] = r
        u = r * (1.0 / center_value)
        u0[row] = u
        potential[row] = u

    for row in range(WIDE):
        start(1 + row, before[row])
        start(1 + WIDE + rows + row, after[row])

    def begin(row, carry):
        start(1 + WIDE + row, middle[row])
        return carry

    lax.fori_loop(0, rows, begin, 0, unroll=2)
    old, new = u0, u1
    rho = 1.0 / ratio
    for sweep in range(1, SWEEPS):
        rho_new = 1.0 / (2.0 * ratio - rho)
        a, b = rho_new * rho, 2.0 * rho_new / half_width
        last = sweep == SWEEPS - 1

        def step(row, carry):
            u = old[row]
            y_weight, z_weight = wy[row], wz[row]
            spread = wx[row] * old[row + 1] + wx[row - 1] * old[row - 1]
            spread = spread + y_weight * pltpu.roll(u, width - 1, 0) + pltpu.roll(y_weight * u, 1, 0)
            spread = spread + z_weight * pltpu.roll(u, DEPTH - 1, 1) + pltpu.roll(z_weight * u, 1, 1)
            r = residual[row] - u + inverse[row] * spread
            u = a * u + b * r
            potential[row] = potential[row] + u
            if not last:
                residual[row] = r
                new[row] = u
            return carry

        lax.fori_loop(1 + sweep, rows + 2 * WIDER - 1 - sweep, step, 0, unroll=2)
        old, new = new, old
        rho = rho_new
    inner = width - 2 * SIDE

    def give(row, carry):
        out[row] = potential[WIDER + row, pl.ds(SIDE, inner), :]
        return carry

    lax.fori_loop(0, rows, give, 0, unroll=2)
    frames[...] = jnp.zeros_like(frames)
    for local in range(TILE_ROWS * TILE_COLS):
        r, c = local // TILE_COLS, local % TILE_COLS
        slot = hold[local]
        for a in range(FRAME):
            frames[slot, pl.ds(a * FRAME, FRAME), :] = potential[
                WIDER + r * EDGE - RING + a, pl.ds(SIDE + c * EDGE - RING, FRAME), :
            ]


def unit_counts(peers):
    per_x = -(-HALVES // peers)
    per_y = -(-2 * HALVES // peers)
    return per_x, per_y


def unit_places(peers):
    per_x, per_y = unit_counts(peers)
    places = {}
    for unit in range(HALVES):
        for face in range(2):
            places[face, unit // 2, unit % 2] = (unit % peers, (face * per_x + unit // peers) * 8)
    for unit in range(2 * HALVES):
        face, rest = 2 + unit // HALVES, unit % HALVES
        places[face, rest // 2, rest % 2] = (unit % peers, (2 * per_x + unit // peers) * 8)
    return places


FACES = ((0, -1), (0, 1), (1, -1), (1, 1))


def raw_faces(peers, pops, charge, out):
    places = unit_places(peers)
    taken = set(places.values())
    for peer in range(peers):
        for row in range(0, out.shape[2], 8):
            if (peer, row) not in taken:
                out[peer, 0, pl.ds(row, 8), :] = jnp.zeros((8, DEPTH), jnp.float32)
    for face, (axis, sign) in enumerate(FACES):
        layer = 0 if sign < 0 else EDGE - 1
        for half in range(2):
            if axis == 0:
                where = pl.ds(layer * EDGE + 8 * half, 8)
            else:
                where = pl.ds(8 * half * EDGE + layer, 8, stride=EDGE)
            values = [pops[q, 0, where, :] for q in range(19)]
            density, momentum = moments(values)
            channels = [values[q] for q in crossing(axis, sign)]
            channels += [density] + momentum + [charge[0, where, :]]
            for channel, value in enumerate(channels):
                peer, row = places[face, channel, half]
                out[peer, 0, pl.ds(row, 8), :] = value


def outer_rows(band_cols, per_x, slot_of, arrived, low, high):
    size = per_x * 8
    for col in range(band_cols):
        low[col] = arrived[slot_of[col], pl.ds(0, size), :]
        high[col] = arrived[slot_of[(TILE_ROWS - 1) * band_cols + col], pl.ds(size, size), :]


def turn_faces(band_cols, per_x, slot_of, tile_at, odd, arrived, below, above, out, from_low, from_high):
    size = per_x * 8
    rest = arrived.shape[1] - 2 * size

    def lay(col, carry):
        from_low[col] = below[col]
        from_high[(TILE_ROWS - 1) * band_cols + col] = above[col]
        for row in range(1, TILE_ROWS):
            from_low[row * band_cols + col] = arrived[slot_of[(row - 1) * band_cols + col], pl.ds(size, size), :]
            from_high[(row - 1) * band_cols + col] = arrived[slot_of[row * band_cols + col], pl.ds(0, size), :]
        return carry

    lax.fori_loop(0, band_cols, lay, 0)
    half = odd[0]
    pick = 7 * half
    per_y = rest // 8
    me = odd[1]
    peers = out.shape[0] // (out.shape[0] // (band_cols // TILE_COLS))

    def send(d, carry):
        p = tile_at[d]
        row, col = p // band_cols, p % band_cols
        right, left = (col + 1) % band_cols, (col + band_cols - 1) % band_cols
        out[d, pl.ds(0, size), :] = from_high[p]
        out[d, pl.ds(size, size), :] = from_low[p]
        slot_right = slot_of[row * band_cols + right]
        slot_left = slot_of[row * band_cols + left]
        for q in range(per_y):
            is_low = q * peers + me < HALVES
            slot = jnp.where(is_low, slot_right, slot_left)
            out[d, pl.ds(2 * size + q * 8, 8), :] = arrived[slot, pl.ds(2 * size + q * 8, 8), :]
        beside = row * band_cols + jnp.where(half == 0, right, left)
        for q in range(per_x):
            out[d, pl.ds(2 * size + rest + q, 1), :] = from_high[beside, pl.ds(q * 8 + pick, 1), :]
            out[d, pl.ds(2 * size + rest + per_x + q, 1), :] = from_low[beside, pl.ds(q * 8 + pick, 1), :]
        return carry

    lax.fori_loop(0, out.shape[0], send, 0)


def step_tile(peers, ids, pops, charge, mask, frame, rims, out, charge_out,
              near, flags, relaxed, rim, conc, vx, vy, vz):
    per_x, per_y = unit_counts(peers)
    places = unit_places(peers)
    corner_row = (2 * per_x + per_y) * 8

    for a in range(FRAME):
        near[a, pl.ds(SIDE - RING, FRAME), :] = frame[0, pl.ds(a * FRAME, FRAME), :]
    for i in range(EDGE + 2):
        row = mask[0, i]
        flags[1, i, pl.ds(SIDE - 1, EDGE + 2), :] = row
        flags[2, i, pl.ds(SIDE - 1, EDGE + 2), :] = pltpu.roll(row, 1, 1)
        flags[0, i, pl.ds(SIDE - 1, EDGE + 2), :] = pltpu.roll(row, DEPTH - 1, 1)

    def field_of(x_low, x_high, y_low, y_high, here):
        return [
            0.5 * (x_low - x_high),
            0.5 * (y_low - y_high),
            0.5 * (pltpu.roll(here, 1, 1) - pltpu.roll(here, DEPTH - 1, 1)),
        ]

    for face, layer in ((1, 0), (0, EDGE + 1)):
        for channel in range(CHANNELS):
            for half in range(2):
                peer, row = places[face, channel, half]
                rim[channel, pl.ds(SIDE + 8 * half, 8), :] = rims[peer, 0, pl.ds(row, 8), :]
                corner = corner_row + row // 8
                column = SIDE + EDGE if half == 0 else SIDE - 1
                rim[channel, pl.ds(column, 1), :] = rims[peer, 0, pl.ds(corner, 1), :]
        here = near[layer + 1]
        field = field_of(near[layer], near[layer + 2], pltpu.roll(here, 1, 0), pltpu.roll(here, PADDED - 1, 0), here)
        density, momentum, held = rim[5], [rim[6], rim[7], rim[8]], rim[9]
        force = [held * f for f in field]
        dirs = crossing(*FACES[face])
        done, velocity = collide({q: rim[n] for n, q in enumerate(dirs)}, density, momentum, force)
        for q in dirs:
            relaxed[q, layer] = done[q]
        conc[layer] = held
        vx[layer] = velocity[0]

    flat_near = near.reshape(FRAME * PADDED, DEPTH)
    flat_relaxed = relaxed.reshape(19, (EDGE + 2) * PADDED, DEPTH)
    flat_conc = conc.reshape((EDGE + 2) * PADDED, DEPTH)
    flat_vy = vy.reshape((EDGE + 2) * PADDED, DEPTH)
    for face, column in ((3, SIDE - 1), (2, SIDE + EDGE)):
        for half in range(2):
            def at(row, col):
                return flat_near[pl.ds((RING + 8 * half + row) * PADDED + col, 8, stride=PADDED), :]

            raw = [rims[places[face, c, half][0], 0, pl.ds(places[face, c, half][1], 8), :] for c in range(CHANNELS)]
            field = field_of(at(-1, column), at(1, column), at(0, column - 1), at(0, column + 1), at(0, column))
            force = [raw[9] * f for f in field]
            dirs = crossing(*FACES[face])
            done, velocity = collide({q: raw[n] for n, q in enumerate(dirs)}, raw[5], raw[6:9], force)
            target = pl.ds((1 + 8 * half) * PADDED + column, 8, stride=PADDED)
            for q in dirs:
                flat_relaxed[q, target, :] = done[q]
            flat_conc[target, :] = raw[9]
            flat_vy[target, :] = velocity[1]

    def relax_row(i, carry):
        for half in range(2):
            cells = pl.ds(pl.multiple_of(i * EDGE + 8 * half, 8), 8)
            base = SIDE + 8 * half
            field = field_of(
                near[i + RING - 1, pl.ds(base, 8), :], near[i + RING + 1, pl.ds(base, 8), :],
                near[i + RING, pl.ds(base - 1, 8), :], near[i + RING, pl.ds(base + 1, 8), :],
                near[i + RING, pl.ds(base, 8), :],
            )
            values = [pops[q, 0, cells, :] for q in range(19)]
            held = charge[0, cells, :]
            force = [held * f for f in field]
            density, momentum = moments(values)
            done, velocity = collide(dict(enumerate(values)), density, momentum, force)
            for q in range(19):
                relaxed[q, i + 1, pl.ds(base, 8), :] = done[q]
            conc[i + 1, pl.ds(base, 8), :] = held
            vx[i + 1, pl.ds(base, 8), :] = velocity[0]
            vy[i + 1, pl.ds(base, 8), :] = velocity[1]
            vz[i + 1, pl.ds(base, 8), :] = velocity[2]
        return carry

    lax.fori_loop(0, EDGE, relax_row, 0)

    def flux(speed_a, speed_b, a, b, flag_a, flag_b):
        face = 0.5 * (speed_a + speed_b)
        return jnp.where((flag_a == 1) & (flag_b == 1), face * jnp.where(face > 0, a, b), 0.0)

    def stream_row(i, carry):
        for half in range(2):
            cells = pl.ds(pl.multiple_of(i * EDGE + 8 * half, 8), 8)
            base = SIDE + 8 * half
            here = i + 1
            mid = pl.ds(base, 8)
            own = flags[1, here, mid, :] == 1
            for q in range(19):
                cx, cy, cz = LATTICE[q]
                from_columns = pl.ds(base - cy, 8)
                pulled = relaxed[q, here - cx, from_columns, :]
                if cz:
                    pulled = pltpu.roll(pulled, cz % DEPTH, 1)
                if q:
                    open_side = flags[cz + 1, here - cx, from_columns, :] == 1
                    pulled = jnp.where(open_side, pulled, relaxed[opposite(q), here, mid, :])
                out[q, 0, cells, :] = jnp.where(own, pulled, pops[q, 0, cells, :])
            held = conc[here, mid, :]
            flag = flags[1, here, mid, :]
            change = flux(vx[here, mid, :], vx[here + 1, mid, :], held, conc[here + 1, mid, :],
                          flag, flags[1, here + 1, mid, :])
            change = change - flux(vx[here - 1, mid, :], vx[here, mid, :], conc[here - 1, mid, :], held,
                                   flags[1, here - 1, mid, :], flag)
            low, high = pl.ds(base - 1, 8), pl.ds(base + 1, 8)
            change = change + flux(vy[here, mid, :], vy[here, high, :], held, conc[here, high, :],
                                   flag, flags[1, here, high, :])
            change = change - flux(vy[here, low, :], vy[here, mid, :], conc[here, low, :], held,
                                   flags[1, here, low, :], flag)
            speed = vz[here, mid, :]
            z_flux = flux(speed, pltpu.roll(speed, DEPTH - 1, 1), held, pltpu.roll(held, DEPTH - 1, 1),
                          flag, flags[0, here, mid, :])
            change = change + (z_flux - pltpu.roll(z_flux, 1, 1))
            charge_out[0, cells, :] = jnp.where(own, held - change, held)
        return carry

    lax.fori_loop(0, EDGE, stream_row, 0)


def per_device(populations, charge, fluid_mask, tile_ids, phase_label, permittivity):
    peers = lax.axis_size("gy")
    tiles = charge.shape[0]
    rows, cols = phase_label.shape[0], phase_label.shape[1]
    band_cols = TILE_COLS * peers
    band = peers * tiles
    per_x, per_y = unit_counts(peers)
    out_rows = (2 * per_x + per_y) * 8
    in_rows = out_rows + -(-2 * per_x // 8) * 8
    f32 = jnp.float32
    shape = jax.ShapeDtypeStruct
    gx_up, gx_down = ring_pairs("gx")
    gy_up, gy_down = ring_pairs("gy")
    me = lax.axis_index("gy").astype(jnp.int32)
    pops = populations.reshape(19, tiles, AREA, DEPTH)
    held = charge.reshape(tiles, AREA, DEPTH)

    outgoing = pl.pallas_call(
        functools.partial(pack_source, tiles, band_cols),
        out_shape=shape((peers, AREA + 8, DEPTH), f32),
        in_specs=[SMEM, VMEM, VMEM], out_specs=VMEM, compiler_params=PARAMS, name="pack_source",
    )(tile_ids, held, fluid_mask)
    arrived = lax.all_to_all(outgoing, "gy", split_axis=0, concat_axis=0, tiled=True)

    tile_at = arrived[:, AREA, :tiles].astype(jnp.int32).reshape(band)
    slots = jnp.arange(band, dtype=jnp.int32)
    slot_of = jnp.sum(jnp.where(tile_at[None, :] == slots[:, None], slots[None, :], 0), axis=1)
    local = jnp.arange(tiles, dtype=jnp.int32)
    mine = local // TILE_COLS * band_cols + TILE_COLS * me + local % TILE_COLS
    hold = jnp.sum(jnp.where(tile_at[None, :] == mine[:, None], slots[None, :] // tiles, 0), axis=1)

    before = lax.ppermute(phase_label[:, cols - SIDE :], "gy", gy_up)
    after = lax.ppermute(phase_label[:, :SIDE], "gy", gy_down)
    labels = jnp.concatenate([before, phase_label, after], axis=1)
    before = lax.ppermute(labels[rows - WIDER :], "gx", gx_up)
    after = lax.ppermute(labels[:WIDER], "gx", gx_down)
    wide = shape((rows + 2 * WIDER, cols + 2 * SIDE, DEPTH), f32)
    scratch = pltpu.VMEM(wide.shape, f32)
    weights = pl.pallas_call(
        face_weights, out_shape=[wide] * 4, in_specs=[SMEM, VMEM, VMEM, VMEM], out_specs=[VMEM] * 4,
        scratch_shapes=[scratch], compiler_params=PARAMS, name="face_weights",
    )(permittivity, labels, before, after)

    raw = pl.pallas_call(
        functools.partial(raw_faces, peers),
        grid=(tiles,),
        out_shape=shape((peers, tiles, out_rows, DEPTH), f32),
        in_specs=[
            pl.BlockSpec((19, 1, AREA, DEPTH), lambda t: (0, t, 0, 0)),
            pl.BlockSpec((1, AREA, DEPTH), lambda t: (t, 0, 0)),
        ],
        out_specs=pl.BlockSpec((peers, 1, out_rows, DEPTH), lambda t: (0, t, 0, 0)),
        compiler_params=PARAMS, name="raw_faces",
    )(pops, held)
    faces = lax.all_to_all(raw, "gy", split_axis=0, concat_axis=0, tiled=True).reshape(band, out_rows, DEPTH)
    strip = shape((band_cols, per_x * 8, DEPTH), f32)
    low, high = pl.pallas_call(
        functools.partial(outer_rows, band_cols, per_x),
        out_shape=[strip, strip], in_specs=[SMEM, VMEM], out_specs=[VMEM, VMEM],
        compiler_params=PARAMS, name="outer_rows",
    )(slot_of, faces)
    below = lax.ppermute(high, "gx", gx_up)
    above = lax.ppermute(low, "gx", gx_down)
    table = pltpu.VMEM((band, per_x * 8, DEPTH), f32)
    turned = pl.pallas_call(
        functools.partial(turn_faces, band_cols, per_x),
        out_shape=shape((band, in_rows, DEPTH), f32),
        in_specs=[SMEM, SMEM, SMEM, VMEM, VMEM, VMEM], out_specs=VMEM,
        scratch_shapes=[table, table], compiler_params=PARAMS, name="turn_faces",
    )(slot_of, tile_at, jnp.stack([me % 2, me]), faces, below, above)
    rims = lax.all_to_all(turned.reshape(peers, tiles, in_rows, DEPTH), "gy", split_axis=0, concat_axis=0, tiled=True)

    block, left, right = pl.pallas_call(
        assemble,
        out_shape=[shape((rows, cols, DEPTH), f32), shape((rows, SIDE, DEPTH), f32), shape((rows, SIDE, DEPTH), f32)],
        in_specs=[SMEM, VMEM], out_specs=[VMEM] * 3, compiler_params=PARAMS, name="assemble",
    )(hold, arrived)
    before = lax.ppermute(right, "gy", gy_up)
    after = lax.ppermute(left, "gy", gy_down)
    middle = jnp.concatenate([before, block, after], axis=1)
    before = lax.ppermute(middle[rows - WIDE :], "gx", gx_up)
    after = lax.ppermute(middle[:WIDE], "gx", gx_down)
    potential, frames = pl.pallas_call(
        solve,
        out_shape=[shape((rows, cols, DEPTH), f32), shape((peers, FRAME * FRAME, DEPTH), f32)],
        in_specs=[SMEM] + [VMEM] * 7, out_specs=[VMEM, VMEM],
        scratch_shapes=[scratch] * 4, compiler_params=PARAMS, name="solve",
    )(hold, middle, before, after, *weights)
    frames = lax.all_to_all(frames, "gy", split_axis=0, concat_axis=0, tiled=True)

    padded = pltpu.VMEM((EDGE + 2, PADDED, DEPTH), f32)
    by_tile = lambda t, ids: (t, 0, 0)
    populations_next, charge_next = pl.pallas_call(
        functools.partial(step_tile, peers),
        grid_spec=pltpu.PrefetchScalarGridSpec(
            num_scalar_prefetch=1,
            grid=(tiles,),
            in_specs=[
                pl.BlockSpec((19, 1, AREA, DEPTH), lambda t, ids: (0, t, 0, 0)),
                pl.BlockSpec((1, AREA, DEPTH), by_tile),
                pl.BlockSpec((1, EDGE + 2, EDGE + 2, DEPTH), lambda t, ids: (t, 0, 0, 0)),
                pl.BlockSpec((1, FRAME * FRAME, DEPTH), lambda t, ids: (ids[t] % band_cols // TILE_COLS, 0, 0)),
                pl.BlockSpec((peers, 1, in_rows, DEPTH), lambda t, ids: (0, t, 0, 0)),
            ],
            out_specs=[
                pl.BlockSpec((19, 1, AREA, DEPTH), lambda t, ids: (0, t, 0, 0)),
                pl.BlockSpec((1, AREA, DEPTH), by_tile),
            ],
            scratch_shapes=[
                pltpu.VMEM((FRAME, PADDED, DEPTH), f32),
                pltpu.VMEM((3, EDGE + 2, PADDED, DEPTH), jnp.int32),
                pltpu.VMEM((19, EDGE + 2, PADDED, DEPTH), f32),
                pltpu.VMEM((CHANNELS, PADDED, DEPTH), f32),
                padded, padded, padded, padded,
            ],
        ),
        out_shape=[shape(pops.shape, f32), shape(held.shape, f32)],
        compiler_params=PARAMS, name="step_tile",
    )(tile_ids, pops, held, fluid_mask, frames, rims)
    return (populations_next.reshape(populations.shape), charge_next.reshape(charge.shape), potential)


def solution(mesh):
    placed = (
        P(None, ("gx", "gy"), None, None, None),
        P(("gx", "gy"), None, None, None),
        P(("gx", "gy"), None, None, None),
        P(("gx", "gy")),
        P("gx", "gy", None),
        P(),
    )
    return jax.shard_map(
        per_device,
        mesh=mesh,
        in_specs=placed,
        out_specs=(
            P(None, ("gx", "gy"), None, None, None),
            P(("gx", "gy"), None, None, None),
            P("gx", "gy", None),
        ),
        check_vma=False,
    )
```

time: 376 us -> 153 us (0.41)
  local copies, waits for them, and re-layouts: 153 us -> 7.84 us
  other arithmetic: 101 us -> 2.16 us
  Pallas kernels: 0 us -> 56.1 us
  between operations: 17.5 us -> 0.83 us
  blocking collectives: 9.46 us -> 25.3 us
  starting transfers between devices: 44.3 us -> 28.7 us
  waiting for transfers between devices: 46.6 us -> 31.7 us
    gather x27 -> x0, local copies, waits for them, and re-layouts: 61.8 us -> none  [the longest x2 14.7 us: per_device(): framed = potential_rim[row_index[:, :, None], col_index[:, None, :]]]
    pallas_call x0 -> x8, Pallas kernels: none -> 56.1 us  [the longest x1 22.9 us: per_device(): pl.pallas_call(functools.partial(step_tile, peers), grid_spec=pltpu.Prefe...]
    slice x45 -> x3, local copies, waits for them, and re-layouts: 26.7 us -> 0.71 us  [the longest x1 0.67 us: per_device(): after = lax.ppermute(phase_label[:, :SIDE], 'gy', gy_down)]
    all_to_all x0 -> x1, blocking collectives: none -> 25.3 us  [per_device(): lax.all_to_all(turned.reshape(peers, tiles, in_rows, DEPTH), 'gy', split_...]
    add x11 -> x1, other arithmetic: 25 us -> 0.01 us  [per_device(): mine = local // TILE_COLS * band_cols + TILE_COLS * me + local % TILE_COLS]
    unnamed x419 -> x31, local copies, waits for them, and re-layouts: 30.9 us -> 7.03 us
    ppermute x22 -> x10, starting transfers between devices: 36.4 us -> 16.2 us  [the longest x1 3.82 us: per_device(): above = lax.ppermute(low, 'gx', gx_down)]
    unnamed x17 -> x0, other arithmetic: 19.6 us -> none
  transfers between devices with their start and end apart: 25 -> 13, of which waited for: 19 -> 5; matrix products, arithmetic and copies ran while one was open for 28% -> 3% of each run, Pallas kernels for 0% -> 20%
where the time goes in v1:
time: 153 us
  Pallas kernels  56.1 us (37%)
  waiting for transfers between devices  31.7 us (21%)
  starting transfers between devices  28.7 us (19%)
  blocking collectives  25.3 us (17%)
  local copies, waits for them, and re-layouts  7.84 us (5%)
  other arithmetic  2.16 us (1%)
    all_to_all x1, blocking collectives, per_device(): lax.all_to_all(turned.reshape(peers, tiles, in_rows, DEPTH), 'gy', split_...  25.3 us
    pallas_call x1, Pallas kernels, per_device(): pl.pallas_call(functools.partial(step_tile, peers), grid_spec=pltpu.Prefe...  22.9 us
    ppermute x1, waiting for transfers between devices, per_device(): before = lax.ppermute(right, 'gy', gy_up)  12.7 us
    pallas_call x1, Pallas kernels, per_device(): pl.pallas_call(solve, out_shape=[shape((rows, cols, DEPTH), f32), shape((...  10.1 us
    ppermute x1, waiting for transfers between devices, per_device(): before = lax.ppermute(phase_label[:, cols - SIDE:], 'gy', gy_up)  9.01 us
    unnamed x31, local copies, waits for them, and re-layouts  7.03 us
    pallas_call x1, Pallas kernels, per_device(): pl.pallas_call(face_weights, out_shape=[wide] * 4, in_specs=[SMEM, VMEM,...  6.93 us
    pallas_call x1, Pallas kernels, per_device(): pl.pallas_call(functools.partial(raw_faces, peers), grid=(tiles,), out_sh...  5.72 us
  transfers between devices with their start and end apart: 13, of which 5 were waited for; matrix products, arithmetic and copies ran while one was open for 3% of the time, Pallas kernels for 20%

profile of v1, /device:TPU:0, one launch (start us, length us, event | category | flops | bytes accessed | tf_op | source)
XLA Modules:
  0.0 152.5 jit_solution(6947643344993147168)
XLA Ops:
  0.6 2.1 %copy.14.mask = s32[4,18,18,128]{3,2,1,0:T(8,128)} copy(s32[4,18,18,128]{3,0,2,1:T(4,128)} %param.8) | data formatting | bytes 1327104 | tf_op args[2]
  2.7 2.4 %pack_source.1 = f32[8,264,128]{2,1,0:T(8,128)} custom-call(s32[4]{0:T(128)} %ids.3, f32[4,256,128]{2,1,0:T(8,128)} %bitcast.13, s32[4,18,18,128]{3,2,1,0:T(8,128)} %copy.14.mask), custom_call_target="tpu_custom_call" | custom-call | tf_op jit(solution)/shard_map/pack_source/pallas_call | solution.py:498
  5.1 0.0 copy-start.5
  5.1 5.3 %all-to-all-start = ((f32[8,264,128]{2,1,0:T(8,128)}), f32[8,264,128]{2,1,0:T(8,128)S(1)}, u32[]{:S(2)}, u32[]{:S(2)}) async-start(f32[8,264,128]{2,1,0:T(8,128)} %pack_source.1), calls=%async_computation | async-start | bytes 2162688 | tf_op jit(solution)/shard_map/all_to_all | solution.py:503
  10.4 0.0 copy-done.5
  10.5 0.7 fusion.6
  11.1 2.7 %collective-permute-start.5 = (s32[32,8,128]{2,1,0:T(8,128)}, s32[32,8,128]{2,1,0:T(8,128)S(1)}, u32[]{:S(2)}, u32[]{:S(2)}) collective-permute-start(s32[32,8,128]{2,1,0:T(8,128)} %get-tuple-element.33), channel_id=1, source_target_pairs={{1,0},{2,1},{3,2},{4,3},{5,4},{6,5},{7,6},{0,7},{9,8},{10,9},{11,1... | collective-permute-start | bytes 393224 | tf_op jit(solution)/shard_map/ppermute | solution.py:513
  13.8 0.0 collective-permute-start.4
  13.8 5.7 %raw_faces.1 = f32[8,4,88,128]{3,2,1,0:T(8,128)} custom-call(f32[19,4,256,128]{3,2,1,0:T(8,128)} %bitcast.8, f32[4,256,128]{2,1,0:T(8,128)} %bitcast.14), custom_call_target="tpu_custom_call" | custom-call | tf_op jit(solution)/shard_map/raw_faces/pallas_call | solution.py:524
  19.5 9.0 %collective-permute-done.4 = s32[32,8,128]{2,1,0:T(8,128)S(1)} collective-permute-done((s32[32,8,128]{2,1,0:T(8,128)S(1)}, s32[32,8,128]{2,1,0:T(8,128)S(1)}, u32[]{:S(2)}, u32[]{:S(2)}) %collective-permute-start.4) | collective-permute-done | bytes 131104 | tf_op jit(solution)/shard_map/ppermute | solution.py:512
  28.6 0.0 all-to-all-done.arrived
  28.6 0.0 copy-start.2
  28.6 3.6 %all-to-all-start.2 = ((f32[8,4,88,128]{3,2,1,0:T(8,128)}), f32[8,4,88,128]{3,2,1,0:T(8,128)S(1)}, u32[]{:S(2)}, u32[]{:S(2)}) async-start(f32[8,4,88,128]{3,2,1,0:T(8,128)} %raw_faces.1), calls=%async_computation.2 | async-start | bytes 2883584 | tf_op jit(solution)/shard_map/all_to_all | solution.py:535
  32.2 0.0 collective-permute-done.5
  32.2 0.0 copy-done.2
  32.3 0.0 copy-start.3
  32.3 0.1 convert_element_type.12.tile_at
  32.4 0.0 copy-start.12
  32.4 0.8 select_reduce_fusion.1.hold
  33.1 2.2 %assemble.1 = (f32[32,32,128]{2,1,0:T(8,128)}, f32[32,8,128]{2,1,0:T(8,128)}, f32[32,8,128]{2,1,0:T(8,128)}) custom-call(s32[4]{0:T(128)} %select_reduce_fusion.1.hold, f32[8,264,128]{2,1,0:T(8,128)} %copy-done.2), custom_call_target="tpu_custom_call" | custom-call | tf_op jit(solution)/shard_map/assemble/pallas_call | solution.py:553
  35.3 0.4 collective-permute-start
  35.7 3.7 %collective-permute-start.7 = (s32[6,48,128]{2,1,0:T(8,128)S(1)}, s32[6,48,128]{2,1,0:T(8,128)S(1)}, u32[]{:S(2)}, u32[]{:S(2)}) collective-permute-start(s32[6,48,128]{2,1,0:T(8,128)S(1)} %get-tuple-element.29), channel_id=1, source_target_pairs={{8,0},{16,8},{24,16},{0,24},{9,1},{17,9},{25,17},{1,25},{10,2},{18... | collective-permute-start | bytes 442376 | tf_op jit(solution)/shard_map/ppermute | solution.py:516
  39.4 0.0 collective-permute-start.6
  39.4 2.0 %collective-permute-start.1 = (f32[32,8,128]{2,1,0:T(8,128)}, f32[32,8,128]{2,1,0:T(8,128)S(1)}, u32[]{:S(2)}, u32[]{:S(2)}) collective-permute-start(f32[32,8,128]{2,1,0:T(8,128)} %get-tuple-element.18), channel_id=1, source_target_pairs={{1,0},{2,1},{3,2},{4,3},{5,4},{6,5},{7,6},{0,7},{9,8},{10,9},{11,1... | collective-permute-start | bytes 393224 | tf_op jit(solution)/shard_map/ppermute | solution.py:559
  41.4 12.7 %collective-permute-done = f32[32,8,128]{2,1,0:T(8,128)S(1)} collective-permute-done((f32[32,8,128]{2,1,0:T(8,128)}, f32[32,8,128]{2,1,0:T(8,128)S(1)}, u32[]{:S(2)}, u32[]{:S(2)}) %collective-permute-start) | collective-permute-done | bytes 131104 | tf_op jit(solution)/shard_map/ppermute | solution.py:558
  54.1 1.1 constant_dynamic-update-slice_fusion.1
  55.2 0.0 copy-done.3
  55.2 0.0 collective-permute-done.1
  55.2 0.0 copy-start.4
  55.3 3.7 %collective-permute-start.3 = (f32[5,48,128]{2,1,0:T(8,128)S(1)}, f32[5,48,128]{2,1,0:T(8,128)S(1)}, u32[]{:S(2)}, u32[]{:S(2)}) collective-permute-start(f32[5,48,128]{2,1,0:T(8,128)S(1)} %get-tuple-element.31), channel_id=1, source_target_pairs={{8,0},{16,8},{24,16},{0,24},{9,1},{17,9},{25,17},{1,25},{10,2},{18... | collective-permute-start | bytes 368648 | tf_op jit(solution)/shard_map/ppermute | solution.py:562
  58.9 0.0 collective-permute-start.2
  58.9 0.0 collective-permute-done.7.after
  58.9 0.0 copy-start.8
  58.9 0.0 collective-permute-done.6.before
  58.9 0.6 copy-done.8
  59.6 0.0 copy-start.9
  59.6 0.7 copy-done.9
  60.3 6.9 %face_weights.1 = (f32[44,48,128]{2,1,0:T(8,128)}, f32[44,48,128]{2,1,0:T(8,128)}, f32[44,48,128]{2,1,0:T(8,128)}, f32[44,48,128]{2,1,0:T(8,128)}) custom-call(f32[4]{0:T(128)} %table.1, s32[32,48,128]{2,1,0:T(8,128)} %copy-done.3, s32[6,48,128]{2,1,0:T(8,128)} %copy-done.9, s32[6,48,128]{2,1,0:T(8,128)} %copy-done.8), custom_call_target="tpu_custom_call" | custom-call | tf_op jit(solution)/shard_map/face_weights/pallas_call | solution.py:519
  67.2 0.0 collective-permute-done.3.after
  67.2 0.0 copy-start.10
  67.2 0.0 collective-permute-done.2.before
  67.2 0.0 copy-start.11
  67.2 0.0 copy-done.4
  67.2 0.6 copy-done.10
  67.8 0.0 copy-done.11
  67.9 10.1 %solve.1 = (f32[32,32,128]{2,1,0:T(8,128)}, f32[8,400,128]{2,1,0:T(8,128)}) custom-call(s32[4]{0:T(128)} %select_reduce_fusion.1.hold, f32[32,48,128]{2,1,0:T(8,128)} %copy-done.4, f32[5,48,128]{2,1,0:T(8,128)} %copy-done.11, f32[5,48,128]{2,1,0:T(8,128)} %copy-done.10, f32[44,48,128]{2,1,0:T(8,128)} %get-tuple-element.19.wx, ...), custom_call_target="tpu_custom_call" | custom-call | tf_op jit(solution)/shard_map/solve/pallas_call | solution.py:563
  78.0 0.0 all-to-all-done.2
  78.0 1.1 copy-done
  79.1 3.6 %all-to-all-start.1 = ((f32[8,400,128]{2,1,0:T(8,128)}), f32[8,400,128]{2,1,0:T(8,128)S(1)}, u32[]{:S(2)}, u32[]{:S(2)}) async-start(f32[8,400,128]{2,1,0:T(8,128)} %get-tuple-element.23), calls=%async_computation.1 | async-start | bytes 3276800 | tf_op jit(solution)/shard_map/all_to_all | solution.py:569
  82.7 0.0 copy-done.12
  82.7 0.7 select_reduce_fusion.slot_of
  83.4 2.1 %outer_rows.1 = (f32[16,24,128]{2,1,0:T(8,128)}, f32[16,24,128]{2,1,0:T(8,128)}) custom-call(s32[32]{0:T(128)} %select_reduce_fusion.slot_of, f32[32,88,128]{2,1,0:T(8,128)} %bitcast.10), custom_call_target="tpu_custom_call" | custom-call | tf_op jit(solution)/shard_map/outer_rows/pallas_call | solution.py:537
  85.6 0.0 collective-permute-start.8
  85.6 3.8 %collective-permute-start.9 = (f32[16,24,128]{2,1,0:T(8,128)}, f32[16,24,128]{2,1,0:T(8,128)S(1)}, u32[]{:S(2)}, u32[]{:S(2)}) collective-permute-start(f32[16,24,128]{2,1,0:T(8,128)} %get-tuple-element.25), channel_id=1, source_target_pairs={{8,0},{16,8},{24,16},{0,24},{9,1},{17,9},{25,17},{1,25},{10,2},{18... | collective-permute-start | bytes 589832 | tf_op jit(solution)/shard_map/ppermute | solution.py:543
  89.4 0.7 pad_add_fusion.odd
  90.1 5.3 %collective-permute-done.8.below = f32[16,24,128]{2,1,0:T(8,128)S(1)} collective-permute-done((f32[16,24,128]{2,1,0:T(8,128)}, f32[16,24,128]{2,1,0:T(8,128)S(1)}, u32[]{:S(2)}, u32[]{:S(2)}) %collective-permute-start.8) | collective-permute-done | bytes 196640 | tf_op jit(solution)/shard_map/ppermute | solution.py:542
  95.4 1.8 %collective-permute-done.9.above = f32[16,24,128]{2,1,0:T(8,128)S(1)} collective-permute-done((f32[16,24,128]{2,1,0:T(8,128)}, f32[16,24,128]{2,1,0:T(8,128)S(1)}, u32[]{:S(2)}, u32[]{:S(2)}) %collective-permute-start.9) | collective-permute-done | bytes 196640 | tf_op jit(solution)/shard_map/ppermute | solution.py:543
  97.2 0.0 copy-done.6
  97.2 0.7 copy-done.7
  97.9 3.7 %turn_faces.1 = f32[32,96,128]{2,1,0:T(8,128)} custom-call(s32[32]{0:T(128)} %select_reduce_fusion.slot_of, s32[32]{0:T(128)} %copy-done.12, s32[2]{0:T(128)} %pad_add_fusion.odd, f32[32,88,128]{2,1,0:T(8,128)} %bitcast.11, f32[16,24,128]{2,1,0:T(8,128)} %copy-done.6, f32[16,24,128]{2,1,0:T(8,128)} %copy-done.7), custom_call_target="tpu_custom_call" | custom-call | tf_op jit(solution)/shard_map/turn_faces/pallas_call | solution.py:545
  101.6 2.8 %all-to-all-done.1.frame = f32[8,400,128]{2,1,0:T(8,128)S(1)} async-done(((f32[8,400,128]{2,1,0:T(8,128)}), f32[8,400,128]{2,1,0:T(8,128)S(1)}, u32[]{:S(2)}, u32[]{:S(2)}) %all-to-all-start.1) | async-done | bytes 1638432 | tf_op jit(solution)/shard_map/all_to_all | solution.py:569
  104.4 25.3 %all_to_all.20.rims = f32[8,4,96,128]{3,2,1,0:T(8,128)} all-to-all(f32[8,4,96,128]{3,2,1,0:T(8,128)} %bitcast.12), channel_id=1, replica_groups=mesh['gx'=4,'gy'=8] {'gy'}, dimensions={0} | all-to-all | bytes 3145728 | tf_op jit(solution)/shard_map/all_to_all | solution.py:551
  129.6 0.0 copy-done.1
  129.6 22.9 %step_tile.1 = (f32[19,4,256,128]{3,2,1,0:T(8,128)}, f32[4,256,128]{2,1,0:T(8,128)}) custom-call(s32[4]{0:T(128)} %ids.3, f32[19,4,256,128]{3,2,1,0:T(8,128)} %bitcast.9, f32[4,256,128]{2,1,0:T(8,128)} %bitcast.15, s32[4,18,18,128]{3,2,1,0:T(8,128)} %copy.14.mask, f32[8,400,128]{2,1,0:T(8,128)} %copy-done.1, f32[8,4,96,128]{3,2,1,0:T(8,128)} %all_to_all.20.rims), custom_call_target="tpu_custom_call" | custom-call | tf_op jit(solution)/shard_map/step_tile/pallas_call | solution.py:573
  (14 shorter events, 0.2 us)
Async XLA Ops:
  5.1 5.3 %copy-start.5 = (s32[32,32,128]{2,1,0:T(8,128)S(1)}, s32[32,32,128]{2,1,0:T(8,128)}, u32[]{:S(2)}) copy-start(s32[32,32,128]{2,1,0:T(8,128)} %param.10) | copy-start | bytes 1572868
  5.1 23.5 %all-to-all-start = ((f32[8,264,128]{2,1,0:T(8,128)}), f32[8,264,128]{2,1,0:T(8,128)S(1)}, u32[]{:S(2)}, u32[]{:S(2)}) async-start(f32[8,264,128]{2,1,0:T(8,128)} %pack_source.1), calls=%async_computation | async-start | bytes 2162688 | tf_op jit(solution)/shard_map/all_to_all | solution.py:503
  11.1 21.1 %collective-permute-start.5 = (s32[32,8,128]{2,1,0:T(8,128)}, s32[32,8,128]{2,1,0:T(8,128)S(1)}, u32[]{:S(2)}, u32[]{:S(2)}) collective-permute-start(s32[32,8,128]{2,1,0:T(8,128)} %get-tuple-element.33), channel_id=1, source_target_pairs={{1,0},{2,1},{3,2},{4,3},{5,4},{6,5},{7,6},{0,7},{9,8},{10,9},{11,1... | collective-permute-start | bytes 393224 | tf_op jit(solution)/shard_map/ppermute | solution.py:513
  13.8 14.7 %collective-permute-start.4 = (s32[32,8,128]{2,1,0:T(8,128)S(1)}, s32[32,8,128]{2,1,0:T(8,128)S(1)}, u32[]{:S(2)}, u32[]{:S(2)}) collective-permute-start(s32[32,8,128]{2,1,0:T(8,128)S(1)} %get-tuple-element.34), channel_id=1, source_target_pairs={{0,1},{1,2},{2,3},{3,4},{4,5},{5,6},{6,7},{7,0},{8,9},{9,10},{10,1... | collective-permute-start | bytes 393224 | tf_op jit(solution)/shard_map/ppermute | solution.py:512
  28.6 3.6 %copy-start.2 = (f32[8,264,128]{2,1,0:T(8,128)}, f32[8,264,128]{2,1,0:T(8,128)S(1)}, u32[]{:S(2)}) copy-start(f32[8,264,128]{2,1,0:T(8,128)S(1)} %all-to-all-done.arrived) | copy-start | bytes 3244036
  28.6 49.3 %all-to-all-start.2 = ((f32[8,4,88,128]{3,2,1,0:T(8,128)}), f32[8,4,88,128]{3,2,1,0:T(8,128)S(1)}, u32[]{:S(2)}, u32[]{:S(2)}) async-start(f32[8,4,88,128]{3,2,1,0:T(8,128)} %raw_faces.1), calls=%async_computation.2 | async-start | bytes 2883584 | tf_op jit(solution)/shard_map/all_to_all | solution.py:535
  32.3 22.9 %copy-start.3 = (s32[32,48,128]{2,1,0:T(8,128)}, s32[32,48,128]{2,1,0:T(8,128)S(1)}, u32[]{:S(2)}) copy-start(s32[32,48,128]{2,1,0:T(8,128)S(1)} %constant_dynamic-update-slice_fusion.3.labels) | copy-start | bytes 2359300
  32.4 50.3 %copy-start.12 = (s32[32]{0:T(128)}, s32[32]{0:T(128)S(1)}, u32[]{:S(2)}) copy-start(s32[32]{0:T(128)S(1)} %convert_element_type.12.tile_at) | copy-start | bytes 388
  35.3 18.8 %collective-permute-start = (f32[32,8,128]{2,1,0:T(8,128)}, f32[32,8,128]{2,1,0:T(8,128)S(1)}, u32[]{:S(2)}, u32[]{:S(2)}) collective-permute-start(f32[32,8,128]{2,1,0:T(8,128)} %get-tuple-element.16), channel_id=1, source_target_pairs={{0,1},{1,2},{2,3},{3,4},{4,5},{5,6},{6,7},{7,0},{8,9},{9,10},{10,1... | collective-permute-start | bytes 393224 | tf_op jit(solution)/shard_map/ppermute | solution.py:558
  35.7 23.2 %collective-permute-start.7 = (s32[6,48,128]{2,1,0:T(8,128)S(1)}, s32[6,48,128]{2,1,0:T(8,128)S(1)}, u32[]{:S(2)}, u32[]{:S(2)}) collective-permute-start(s32[6,48,128]{2,1,0:T(8,128)S(1)} %get-tuple-element.29), channel_id=1, source_target_pairs={{8,0},{16,8},{24,16},{0,24},{9,1},{17,9},{25,17},{1,25},{10,2},{18... | collective-permute-start | bytes 442376 | tf_op jit(solution)/shard_map/ppermute | solution.py:516
  39.4 19.6 %collective-permute-start.6 = (s32[6,48,128]{2,1,0:T(8,128)S(1)}, s32[6,48,128]{2,1,0:T(8,128)S(1)}, u32[]{:S(2)}, u32[]{:S(2)}) collective-permute-start(s32[6,48,128]{2,1,0:T(8,128)S(1)} %get-tuple-element.30), channel_id=1, source_target_pairs={{0,8},{8,16},{16,24},{24,0},{1,9},{9,17},{17,25},{25,1},{2,10},{10... | collective-permute-start | bytes 442376 | tf_op jit(solution)/shard_map/ppermute | solution.py:515
  39.4 15.8 %collective-permute-start.1 = (f32[32,8,128]{2,1,0:T(8,128)}, f32[32,8,128]{2,1,0:T(8,128)S(1)}, u32[]{:S(2)}, u32[]{:S(2)}) collective-permute-start(f32[32,8,128]{2,1,0:T(8,128)} %get-tuple-element.18), channel_id=1, source_target_pairs={{1,0},{2,1},{3,2},{4,3},{5,4},{6,5},{7,6},{0,7},{9,8},{10,9},{11,1... | collective-permute-start | bytes 393224 | tf_op jit(solution)/shard_map/ppermute | solution.py:559
  55.2 12.0 %copy-start.4 = (f32[32,48,128]{2,1,0:T(8,128)}, f32[32,48,128]{2,1,0:T(8,128)S(1)}, u32[]{:S(2)}) copy-start(f32[32,48,128]{2,1,0:T(8,128)S(1)} %constant_dynamic-update-slice_fusion.middle) | copy-start | bytes 2359300
  55.3 11.9 %collective-permute-start.3 = (f32[5,48,128]{2,1,0:T(8,128)S(1)}, f32[5,48,128]{2,1,0:T(8,128)S(1)}, u32[]{:S(2)}, u32[]{:S(2)}) collective-permute-start(f32[5,48,128]{2,1,0:T(8,128)S(1)} %get-tuple-element.31), channel_id=1, source_target_pairs={{8,0},{16,8},{24,16},{0,24},{9,1},{17,9},{25,17},{1,25},{10,2},{18... | collective-permute-start | bytes 368648 | tf_op jit(solution)/shard_map/ppermute | solution.py:562
  58.9 8.3 %collective-permute-start.2 = (f32[5,48,128]{2,1,0:T(8,128)S(1)}, f32[5,48,128]{2,1,0:T(8,128)S(1)}, u32[]{:S(2)}, u32[]{:S(2)}) collective-permute-start(f32[5,48,128]{2,1,0:T(8,128)S(1)} %get-tuple-element.32), channel_id=1, source_target_pairs={{0,8},{8,16},{16,24},{24,0},{1,9},{9,17},{17,25},{25,1},{2,10},{10... | collective-permute-start | bytes 368648 | tf_op jit(solution)/shard_map/ppermute | solution.py:561
  58.9 0.7 copy-start.8
  59.6 0.7 copy-start.9
  67.2 0.6 copy-start.10
  67.2 0.7 copy-start.11
  78.0 1.1 copy-start
  79.1 25.3 %all-to-all-start.1 = ((f32[8,400,128]{2,1,0:T(8,128)}), f32[8,400,128]{2,1,0:T(8,128)S(1)}, u32[]{:S(2)}, u32[]{:S(2)}) async-start(f32[8,400,128]{2,1,0:T(8,128)} %get-tuple-element.23), calls=%async_computation.1 | async-start | bytes 3276800 | tf_op jit(solution)/shard_map/all_to_all | solution.py:569
  85.6 9.8 %collective-permute-start.8 = (f32[16,24,128]{2,1,0:T(8,128)}, f32[16,24,128]{2,1,0:T(8,128)S(1)}, u32[]{:S(2)}, u32[]{:S(2)}) collective-permute-start(f32[16,24,128]{2,1,0:T(8,128)} %get-tuple-element.24), channel_id=1, source_target_pairs={{0,8},{8,16},{16,24},{24,0},{1,9},{9,17},{17,25},{25,1},{2,10},{10... | collective-permute-start | bytes 589832 | tf_op jit(solution)/shard_map/ppermute | solution.py:542
  85.6 11.7 %collective-permute-start.9 = (f32[16,24,128]{2,1,0:T(8,128)}, f32[16,24,128]{2,1,0:T(8,128)S(1)}, u32[]{:S(2)}, u32[]{:S(2)}) collective-permute-start(f32[16,24,128]{2,1,0:T(8,128)} %get-tuple-element.25), channel_id=1, source_target_pairs={{8,0},{16,8},{24,16},{0,24},{9,1},{17,9},{25,17},{1,25},{10,2},{18... | collective-permute-start | bytes 589832 | tf_op jit(solution)/shard_map/ppermute | solution.py:543
  95.4 1.8 %copy-start.6 = (f32[16,24,128]{2,1,0:T(8,128)}, f32[16,24,128]{2,1,0:T(8,128)S(1)}, u32[]{:S(2)}) copy-start(f32[16,24,128]{2,1,0:T(8,128)S(1)} %collective-permute-done.8.below) | copy-start | bytes 589828
  97.2 0.7 copy-start.7
  104.4 25.3 %copy-start.1 = (f32[8,400,128]{2,1,0:T(8,128)}, f32[8,400,128]{2,1,0:T(8,128)S(1)}, u32[]{:S(2)}) copy-start(f32[8,400,128]{2,1,0:T(8,128)S(1)} %all-to-all-done.1.frame) | copy-start | bytes 4915204

commit v2 on v1

v2 whole, which is shorter than its diff:
```python
import functools

import jax
import jax.numpy as jnp
from jax import lax
from jax.experimental import pallas as pl
from jax.experimental.pallas import tpu as pltpu
from jax.sharding import PartitionSpec as P

EDGE = 16
DEPTH = 128
TILE_ROWS = 2
TILE_COLS = 2
PHASES = 4
SWEEPS = 4

LATTICE = (
    (0, 0, 0),
    (1, 0, 0),
    (-1, 0, 0),
    (0, 1, 0),
    (0, -1, 0),
    (0, 0, 1),
    (0, 0, -1),
    (1, 1, 0),
    (-1, -1, 0),
    (1, -1, 0),
    (-1, 1, 0),
    (1, 0, 1),
    (-1, 0, -1),
    (1, 0, -1),
    (-1, 0, 1),
    (0, 1, 1),
    (0, -1, -1),
    (0, 1, -1),
    (0, -1, 1),
)
relax_time = 0.8
screening = 0.001
spectrum_low = 0.1
spectrum_high = 2.0

AREA = EDGE * EDGE
SIDE = 8
RING = 2
WIDE = RING + SWEEPS - 1
WIDER = WIDE + 1
FRAME = EDGE + 2 * RING
PADDED = EDGE + 2 * SIDE
CHANNELS = 10
HALVES = 2 * CHANNELS
VMEM = pl.BlockSpec(memory_space=pltpu.VMEM)
SMEM = pl.BlockSpec(memory_space=pltpu.SMEM)


def room(mebibytes):
    return pltpu.CompilerParams(vmem_limit_bytes=mebibytes * 2**20)


def crossing(axis_index, face_sign):
    return [q for q in range(19) if LATTICE[q][axis_index] == face_sign]


def opposite(direction):
    return LATTICE.index(tuple(-entry for entry in LATTICE[direction]))


def lattice_weight(direction):
    return (1.0 / 3.0, 1.0 / 18.0, 1.0 / 36.0)[sum(abs(e) for e in LATTICE[direction])]


def along(direction, vector):
    total = None
    for entry, part in zip(LATTICE[direction], vector):
        if entry:
            term = part if entry > 0 else -part
            total = term if total is None else total + term
    return total


def moments(pops):
    density = pops[0]
    for q in range(1, 19):
        density = density + pops[q]
    momentum = []
    for axis in range(3):
        plus = sum_of([pops[q] for q in crossing(axis, 1)])
        minus = sum_of([pops[q] for q in crossing(axis, -1)])
        momentum.append(plus - minus)
    return density, momentum


def sum_of(values):
    total = values[0]
    for value in values[1:]:
        total = total + value
    return total


def collide(pops, density, momentum, force):
    source_scale = 1.0 - 0.5 / relax_time
    gain = 1.0 / relax_time
    inverse = 1.0 / density
    carried = [m + 0.5 * f for m, f in zip(momentum, force)]
    velocity = [c * inverse for c in carried]
    energy = sum_of([c * v for c, v in zip(carried, velocity)])
    power = sum_of([v * f for v, f in zip(velocity, force)])
    base = gain * density - (1.5 * gain) * energy - (3.0 * source_scale) * power
    relaxed = {}
    for q in pops:
        weight = lattice_weight(q)
        kept = (1.0 - gain) * pops[q]
        if q == 0:
            relaxed[q] = kept + weight * base
            continue
        if q in relaxed:
            continue
        p, g, rp = along(q, velocity), along(q, force), along(q, carried)
        even = weight * base + p * ((4.5 * gain * weight) * rp + (9.0 * source_scale * weight) * g)
        odd = (3.0 * gain * weight) * rp + (3.0 * source_scale * weight) * g
        relaxed[q] = kept + (even + odd)
        back = opposite(q)
        if back in pops:
            relaxed[back] = (1.0 - gain) * pops[back] + (even - odd)
    return relaxed, velocity


def ring_pairs(axis):
    size = lax.axis_size(axis)
    up = [(i, (i + 1) % size) for i in range(size)]
    return up, [(j, i) for i, j in up]


def pack_source(tiles, band_cols, ids, charge, mask, out):
    out[...] = jnp.zeros_like(out)
    lane = lax.broadcasted_iota(jnp.int32, (8, DEPTH), 1)
    header = jnp.zeros((8, DEPTH), jnp.int32)
    for t in range(tiles):
        owner = ids[t] % band_cols // TILE_COLS
        header = jnp.where(lane == t, ids[t], header)
        for i in range(EDGE):
            flags = mask[t, i + 1, 1 : EDGE + 1, :].astype(jnp.float32)
            out[owner, pl.ds(i * EDGE, EDGE), :] = charge[t, pl.ds(i * EDGE, EDGE), :] * flags
    for peer in range(out.shape[0]):
        out[peer, pl.ds(AREA, 8), :] = header.astype(jnp.float32)


def assemble(band, tiles, slot_of, arrived, block, left, right):
    for local in range(TILE_ROWS * TILE_COLS):
        r, c = local // TILE_COLS, local % TILE_COLS
        slot = slot_of[band + local] // tiles
        for i in range(EDGE):
            row = r * EDGE + i
            cells = arrived[slot, pl.ds(i * EDGE, EDGE), :]
            block[row, pl.ds(c * EDGE, EDGE), :] = cells
            if c == 0:
                left[row] = cells[:SIDE]
            if c == TILE_COLS - 1:
                right[row] = cells[EDGE - SIDE :]


def tick(_, out):
    out[...] = jnp.zeros_like(out)


def edge_rows(block, left, right, ups, downs):
    rows = block.shape[0]
    for row in range(WIDE):
        low = rows - WIDE + row
        ups[row] = jnp.concatenate([left[low], block[low], right[low]], axis=0)
        downs[row] = jnp.concatenate([left[row], block[row], right[row]], axis=0)


def harmonic(a, b):
    return 2.0 * a * b / (a + b)


def face_weights(table, labels, before, after, left, right, wx, wy, wz, inverse, permit):
    rows = labels.shape[0]
    total = rows + 2 * WIDER

    def look(label):
        value = jnp.full(label.shape, table[PHASES - 1], jnp.float32)
        for phase in range(PHASES - 1):
            value = jnp.where(label == phase, table[phase], value)
        return value

    for row in range(WIDER):
        low, high = row, WIDER + rows + row
        permit[low] = look(jnp.concatenate([left[low], before[row], right[low]], axis=0))
        permit[high] = look(jnp.concatenate([left[high], after[row], right[high]], axis=0))

    def fill(row, carry):
        row = WIDER + row
        permit[row] = look(jnp.concatenate([left[row], labels[row - WIDER], right[row]], axis=0))
        return carry

    lax.fori_loop(0, rows, fill, 0, unroll=2)
    width = permit.shape[1]
    wx[0] = harmonic(permit[0], permit[1])

    def weigh(row, carry):
        here = permit[row]
        x_plus = harmonic(here, permit[row + 1])
        y_plus = harmonic(here, pltpu.roll(here, width - 1, 0))
        z_plus = harmonic(here, pltpu.roll(here, DEPTH - 1, 1))
        wx[row] = x_plus
        wy[row] = y_plus
        wz[row] = z_plus
        diagonal = x_plus + wx[row - 1] + y_plus + pltpu.roll(y_plus, 1, 0)
        diagonal = diagonal + z_plus + pltpu.roll(z_plus, 1, 1) + screening
        inverse[row] = 1.0 / diagonal
        return carry

    lax.fori_loop(1, total - 1, weigh, 0, unroll=6)


def solve(band, tiles, slot_of, middle, left, right, before, after, wx, wy, wz, inverse, _, out, frames, u0, u1, residual, potential):
    rows, width = middle.shape[0], wx.shape[1]
    center_value = 0.5 * (spectrum_high + spectrum_low)
    half_width = 0.5 * (spectrum_high - spectrum_low)
    ratio = center_value / half_width

    def start(row, source):
        r = source * inverse[row]
        residual[row] = r
        u = r * (1.0 / center_value)
        u0[row] = u
        potential[row] = u

    for row in range(WIDE):
        start(1 + row, before[row])
        start(1 + WIDE + rows + row, after[row])

    def begin(row, carry):
        start(1 + WIDE + row, jnp.concatenate([left[row], middle[row], right[row]], axis=0))
        return carry

    lax.fori_loop(0, rows, begin, 0, unroll=2)
    old, new = u0, u1
    rho = 1.0 / ratio
    for sweep in range(1, SWEEPS):
        rho_new = 1.0 / (2.0 * ratio - rho)
        a, b = rho_new * rho, 2.0 * rho_new / half_width
        last = sweep == SWEEPS - 1

        def step(row, carry):
            u = old[row]
            y_weight, z_weight = wy[row], wz[row]
            spread = wx[row] * old[row + 1] + wx[row - 1] * old[row - 1]
            spread = spread + y_weight * pltpu.roll(u, width - 1, 0) + pltpu.roll(y_weight * u, 1, 0)
            spread = spread + z_weight * pltpu.roll(u, DEPTH - 1, 1) + pltpu.roll(z_weight * u, 1, 1)
            r = residual[row] - u + inverse[row] * spread
            u = a * u + b * r
            potential[row] = potential[row] + u
            if not last:
                residual[row] = r
                new[row] = u
            return carry

        lax.fori_loop(1 + sweep, rows + 2 * WIDER - 1 - sweep, step, 0, unroll=4)
        old, new = new, old
        rho = rho_new
    inner = width - 2 * SIDE

    def give(row, carry):
        out[row] = potential[WIDER + row, pl.ds(SIDE, inner), :]
        return carry

    lax.fori_loop(0, rows, give, 0, unroll=2)
    frames[...] = jnp.zeros_like(frames)
    for local in range(TILE_ROWS * TILE_COLS):
        r, c = local // TILE_COLS, local % TILE_COLS
        slot = slot_of[band + local] // tiles
        for a in range(FRAME):
            frames[slot, pl.ds(a * FRAME, FRAME), :] = potential[
                WIDER + r * EDGE - RING + a, pl.ds(SIDE + c * EDGE - RING, FRAME), :
            ]


def unit_counts(peers):
    per_x = -(-HALVES // peers)
    per_y = -(-2 * HALVES // peers)
    return per_x, per_y


def unit_places(peers):
    per_x, per_y = unit_counts(peers)
    places = {}
    for unit in range(HALVES):
        for face in range(2):
            places[face, unit // 2, unit % 2] = (unit % peers, (face * per_x + unit // peers) * 8)
    for unit in range(2 * HALVES):
        face, rest = 2 + unit // HALVES, unit % HALVES
        places[face, rest // 2, rest % 2] = (unit % peers, (2 * per_x + unit // peers) * 8)
    return places


FACES = ((0, -1), (0, 1), (1, -1), (1, 1))


def open_sides(mask, bits, flags):
    column = lax.broadcasted_iota(jnp.int32, (EDGE + 2, DEPTH), 0)
    inner = (column > 0) & (column < EDGE + 1)
    for i in range(EDGE + 2):
        row = jnp.where(inner, mask[0, i], 0) if 0 < i < EDGE + 1 else jnp.zeros((EDGE + 2, DEPTH), jnp.int32)
        flags[1, i, pl.ds(SIDE - 1, EDGE + 2), :] = row
        flags[2, i, pl.ds(SIDE - 1, EDGE + 2), :] = pltpu.roll(row, 1, 1)
        flags[0, i, pl.ds(SIDE - 1, EDGE + 2), :] = pltpu.roll(row, DEPTH - 1, 1)

    def gather(i, carry):
        total = jnp.zeros((EDGE, DEPTH), jnp.int32)
        for q in range(19):
            cx, cy, cz = LATTICE[q]
            total = total + flags[cz + 1, i + 1 - cx, pl.ds(SIDE - cy, EDGE), :] * (1 << q)
        own = flags[1, i + 1, pl.ds(SIDE, EDGE), :]
        bits[0, pl.ds(pl.multiple_of(i * EDGE, EDGE), EDGE), :] = jnp.where(own == 1, total, 0)
        return carry

    lax.fori_loop(0, EDGE, gather, 0, unroll=4)


def raw_faces(peers, pops, charge, mask, out, bits, flags):
    open_sides(mask, bits, flags)
    places = unit_places(peers)
    taken = set(places.values())
    for peer in range(peers):
        for row in range(0, out.shape[2], 8):
            if (peer, row) not in taken:
                out[peer, 0, pl.ds(row, 8), :] = jnp.zeros((8, DEPTH), jnp.float32)
    for face, (axis, sign) in enumerate(FACES):
        layer = 0 if sign < 0 else EDGE - 1
        for half in range(2):
            if axis == 0:
                where = pl.ds(layer * EDGE + 8 * half, 8)
            else:
                where = pl.ds(8 * half * EDGE + layer, 8, stride=EDGE)
            values = [pops[q, 0, where, :] for q in range(19)]
            density, momentum = moments(values)
            channels = [values[q] for q in crossing(axis, sign)]
            channels += [density] + momentum + [charge[0, where, :]]
            for channel, value in enumerate(channels):
                peer, row = places[face, channel, half]
                out[peer, 0, pl.ds(row, 8), :] = value


def outer_rows(band_cols, per_x, slot_of, arrived, low, high):
    size = per_x * 8
    for col in range(band_cols):
        low[col] = arrived[slot_of[col], pl.ds(0, size), :]
        high[col] = arrived[slot_of[(TILE_ROWS - 1) * band_cols + col], pl.ds(size, size), :]


def turn_faces(band_cols, per_x, slot_of, tile_at, odd, arrived, below, above, out, from_low, from_high):
    size = per_x * 8
    rest = arrived.shape[1] - 2 * size

    def lay(col, carry):
        from_low[col] = below[col]
        from_high[(TILE_ROWS - 1) * band_cols + col] = above[col]
        for row in range(1, TILE_ROWS):
            from_low[row * band_cols + col] = arrived[slot_of[(row - 1) * band_cols + col], pl.ds(size, size), :]
            from_high[(row - 1) * band_cols + col] = arrived[slot_of[row * band_cols + col], pl.ds(0, size), :]
        return carry

    lax.fori_loop(0, band_cols, lay, 0)
    half = odd[0]
    pick = 7 * half
    per_y = rest // 8
    me = odd[1]
    peers = out.shape[0] // (out.shape[0] // (band_cols // TILE_COLS))

    def send(d, carry):
        p = tile_at[d]
        row, col = p // band_cols, p % band_cols
        right, left = (col + 1) % band_cols, (col + band_cols - 1) % band_cols
        out[d, pl.ds(0, size), :] = from_high[p]
        out[d, pl.ds(size, size), :] = from_low[p]
        slot_right = slot_of[row * band_cols + right]
        slot_left = slot_of[row * band_cols + left]
        for q in range(per_y):
            is_low = q * peers + me < HALVES
            slot = jnp.where(is_low, slot_right, slot_left)
            out[d, pl.ds(2 * size + q * 8, 8), :] = arrived[slot, pl.ds(2 * size + q * 8, 8), :]
        beside = row * band_cols + jnp.where(half == 0, right, left)
        for q in range(per_x):
            out[d, pl.ds(2 * size + rest + q, 1), :] = from_high[beside, pl.ds(q * 8 + pick, 1), :]
            out[d, pl.ds(2 * size + rest + per_x + q, 1), :] = from_low[beside, pl.ds(q * 8 + pick, 1), :]
        return carry

    lax.fori_loop(0, out.shape[0], send, 0)


ACROSS_X = [q for q in range(19) if LATTICE[q][0]]
ACROSS_Y = [q for q in range(19) if LATTICE[q][1]]


def field_of(x_low, x_high, y_low, y_high, here):
    return [
        0.5 * (x_low - x_high),
        0.5 * (y_low - y_high),
        0.5 * (pltpu.roll(here, 1, 1) - pltpu.roll(here, DEPTH - 1, 1)),
    ]


def flux(speed_a, speed_b, a, b, flag_a, flag_b):
    face = 0.5 * (speed_a + speed_b)
    return jnp.where((flag_a == 1) & (flag_b == 1), face * jnp.where(face > 0, a, b), 0.0)


def step_inside(ids, pops, charge, bits, frame, out, charge_out, edges, bands, lines, near, relaxed, conc, vx, vy, vz):
    for a in range(FRAME):
        near[a, pl.ds(SIDE - RING, FRAME), :] = frame[0, pl.ds(a * FRAME, FRAME), :]

    def relax_row(i, carry):
        cells = pl.ds(pl.multiple_of(i * EDGE, EDGE), EDGE)
        field = field_of(
            near[i + RING - 1, pl.ds(SIDE, EDGE), :], near[i + RING + 1, pl.ds(SIDE, EDGE), :],
            near[i + RING, pl.ds(SIDE - 1, EDGE), :], near[i + RING, pl.ds(SIDE + 1, EDGE), :],
            near[i + RING, pl.ds(SIDE, EDGE), :],
        )
        values = [pops[q, 0, cells, :] for q in range(19)]
        held = charge[0, cells, :]
        force = [held * f for f in field]
        density, momentum = moments(values)
        done, velocity = collide(dict(enumerate(values)), density, momentum, force)
        for q in range(19):
            relaxed[q, i + 1, pl.ds(SIDE, EDGE), :] = done[q]
        conc[i + 1, pl.ds(SIDE, EDGE), :] = held
        vx[i + 1, pl.ds(SIDE, EDGE), :] = velocity[0]
        vy[i + 1, pl.ds(SIDE, EDGE), :] = velocity[1]
        vz[i + 1, pl.ds(SIDE, EDGE), :] = velocity[2]
        return carry

    lax.fori_loop(0, EDGE, relax_row, 0, unroll=4)
    flat_vy = vy.reshape((EDGE + 2) * PADDED, DEPTH)
    edges[0, 0] = vx[1, pl.ds(SIDE, EDGE), :]
    edges[0, 1] = vx[EDGE, pl.ds(SIDE, EDGE), :]
    edges[0, 2] = flat_vy[pl.ds(PADDED + SIDE, EDGE, stride=PADDED), :]
    edges[0, 3] = flat_vy[pl.ds(PADDED + SIDE + EDGE - 1, EDGE, stride=PADDED), :]

    def stream_row(i, carry):
        cells = pl.ds(pl.multiple_of(i * EDGE, EDGE), EDGE)
        here = i + 1
        mid = pl.ds(SIDE, EDGE)
        bit = bits[0, cells, :]
        is_open = [(bit & (1 << q)) != 0 for q in range(19)]
        for q in range(19):
            cx, cy, cz = LATTICE[q]
            pulled = relaxed[q, here - cx, pl.ds(SIDE - cy, EDGE), :]
            if cz:
                pulled = pltpu.roll(pulled, cz % DEPTH, 1)
            kept = pops[q, 0, cells, :]
            if q:
                kept = jnp.where(is_open[0], relaxed[opposite(q), here, mid, :], kept)
            out[q, 0, cells, :] = jnp.where(is_open[q], pulled, kept)
        held = conc[here, mid, :]

        def through(q, speed_a, speed_b, a, b):
            face = 0.5 * (speed_a + speed_b)
            return jnp.where(is_open[q], face * jnp.where(face > 0, a, b), 0.0)

        change = through(2, vx[here, mid, :], vx[here + 1, mid, :], held, conc[here + 1, mid, :])
        change = change - through(1, vx[here - 1, mid, :], vx[here, mid, :], conc[here - 1, mid, :], held)
        low, high = pl.ds(SIDE - 1, EDGE), pl.ds(SIDE + 1, EDGE)
        change = change + through(4, vy[here, mid, :], vy[here, high, :], held, conc[here, high, :])
        change = change - through(3, vy[here, low, :], vy[here, mid, :], conc[here, low, :], held)
        speed = vz[here, mid, :]
        z_flux = through(6, speed, pltpu.roll(speed, DEPTH - 1, 1), held, pltpu.roll(held, DEPTH - 1, 1))
        change = change + (z_flux - pltpu.roll(z_flux, 1, 1))
        charge_out[0, cells, :] = held - change
        return carry

    lax.fori_loop(0, EDGE, stream_row, 0, unroll=4)
    for n, q in enumerate(ACROSS_Y):
        first = 0 if LATTICE[q][1] > 0 else EDGE - 8
        for row in range(EDGE):
            bands[0, n, row] = out[q, 0, pl.ds(row * EDGE + first, 8), :]
    for n, q in enumerate(ACROSS_X):
        lines[0, n] = out[q, 0, pl.ds(0 if LATTICE[q][0] > 0 else AREA - EDGE, EDGE), :]


def step_faces(peers, tiles, band_cols, ids, charge, mask, frames, rims, edges, bands, lines, charge_in, _,
               charge_out, out, all_near, all_flags, all_rim, all_x, all_y, new_bands, new_lines, sems):
    per_x, per_y = unit_counts(peers)
    places = unit_places(peers)
    corner_row = (2 * per_x + per_y) * 8
    all_flat_near = all_near.reshape(tiles, FRAME * PADDED, DEPTH)
    all_flat_flags = all_flags.reshape(tiles, (EDGE + 2) * PADDED, DEPTH)
    flat_bands = new_bands.reshape(tiles, len(ACROSS_Y), EDGE * 8, DEPTH)

    def pieces(tile):
        made = []
        for n, q in enumerate(ACROSS_Y):
            first = 0 if LATTICE[q][1] > 0 else EDGE - 8
            made.append((new_bands.at[tile, n], out.at[q, tile, :, pl.ds(first, 8)]))
        for n, q in enumerate(ACROSS_X):
            layer = 0 if LATTICE[q][0] > 0 else EDGE - 1
            if LATTICE[q][1]:
                cells = pl.ds(8 if LATTICE[q][1] > 0 else 0, 8)
                made.append((new_lines.at[tile, n, cells], out.at[q, tile, layer, cells]))
            else:
                made.append((new_lines.at[tile, n], out.at[q, tile, layer]))
        return [pltpu.make_async_copy(a, b, sems.at[tile, n]) for n, (a, b) in enumerate(made)]

    def incoming(tile):
        return pltpu.make_async_copy(bands.at[tile], new_bands.at[tile], sems.at[tile, len(ACROSS_Y + ACROSS_X)])

    for tile in range(tiles):
        incoming(tile).start()

    def patch(t, carry):
        near, flags, rim, beside_x, beside_y = (x.at[t] for x in (all_near, all_flags, all_rim, all_x, all_y))
        flat_near, flat_flags = all_flat_near.at[t], all_flat_flags.at[t]
        owner = ids[t] % band_cols // TILE_COLS
        for a in range(FRAME):
            near[a, pl.ds(SIDE - RING, FRAME), :] = frames[owner, pl.ds(a * FRAME, FRAME), :]
        for i in range(EDGE + 2):
            flags[i, pl.ds(SIDE - 1, EDGE + 2), :] = mask[t, i]
        charge_out[t] = charge_in[t]
        incoming(t).wait()

        for side, face, layer in ((0, 1, 0), (1, 0, EDGE + 1)):
            for channel in range(CHANNELS):
                for half in range(2):
                    peer, row = places[face, channel, half]
                    rim[channel, pl.ds(SIDE + 8 * half, 8), :] = rims[peer, t, pl.ds(row, 8), :]
                    corner = corner_row + row // 8
                    column = SIDE + EDGE if half == 0 else SIDE - 1
                    rim[channel, pl.ds(column, 1), :] = rims[peer, t, pl.ds(corner, 1), :]
            here = near[layer + 1]
            field = field_of(
                near[layer], near[layer + 2], pltpu.roll(here, 1, 0), pltpu.roll(here, PADDED - 1, 0), here
            )
            density, momentum, held = rim[5], [rim[6], rim[7], rim[8]], rim[9]
            force = [held * f for f in field]
            dirs = crossing(*FACES[face])
            done, velocity = collide({q: rim[n] for n, q in enumerate(dirs)}, density, momentum, force)
            for n, q in enumerate(dirs):
                beside_x[side, n] = done[q]
            cells = pl.ds(0 if side == 0 else AREA - EDGE, EDGE)
            own_layer = 0 if side == 0 else EDGE - 1
            inner = slice(SIDE, SIDE + EDGE)
            speed, own_speed = velocity[0][inner], edges[t, side]
            amount, own_amount = held[inner], charge[t, cells, :]
            flag, own_flag = flags[layer, pl.ds(SIDE, EDGE), :], flags[own_layer + 1, pl.ds(SIDE, EDGE), :]
            if side == 0:
                charge_out[t, cells, :] += flux(speed, own_speed, amount, own_amount, flag, own_flag)
            else:
                charge_out[t, cells, :] -= flux(own_speed, speed, own_amount, amount, own_flag, flag)
            for n, q in enumerate(dirs):
                _, cy, cz = LATTICE[q]
                columns = pl.ds(SIDE - cy, EDGE)
                value, flag = beside_x[side, n, columns, :], flags[layer, columns, :]
                if cz:
                    value, flag = pltpu.roll(value, cz % DEPTH, 1), pltpu.roll(flag, cz % DEPTH, 1)
                line = ACROSS_X.index(q)
                taken = (flag == 1) & (own_flag == 1)
                merged = jnp.where(taken, value, lines[t, line])
                new_lines[t, line] = merged
                if cy:
                    new_bands[t, ACROSS_Y.index(q), own_layer] = merged[:8] if cy > 0 else merged[8:]

        for side, face, column in ((0, 3, SIDE - 1), (1, 2, SIDE + EDGE)):
            dirs = crossing(*FACES[face])
            x_dirs = [crossing(*FACES[1]), crossing(*FACES[0])]
            own_column = 0 if side == 0 else EDGE - 1
            for half in range(2):
                def at(row, col):
                    return flat_near[pl.ds((RING + 8 * half + row) * PADDED + col, 8, stride=PADDED), :]

                raw = [rims[places[face, c, half][0], t, pl.ds(places[face, c, half][1], 8), :]
                       for c in range(CHANNELS)]
                field = field_of(at(-1, column), at(1, column), at(0, column - 1), at(0, column + 1), at(0, column))
                force = [raw[9] * f for f in field]
                done, velocity = collide({q: raw[n] for n, q in enumerate(dirs)}, raw[5], raw[6:9], force)
                for n, q in enumerate(dirs):
                    beside_y[side, n, pl.ds(SIDE + 8 * half, 8), :] = done[q]
                cells = pl.ds(8 * half * EDGE + own_column, 8, stride=EDGE)
                own_flag = flat_flags[pl.ds((1 + 8 * half) * PADDED + SIDE + own_column, 8, stride=PADDED), :]
                flag = flat_flags[pl.ds((1 + 8 * half) * PADDED + column, 8, stride=PADDED), :]
                own_speed, own_amount = edges[t, 2 + side, pl.ds(8 * half, 8), :], charge[t, cells, :]
                if side == 0:
                    charge_out[t, cells, :] += flux(velocity[1], own_speed, raw[9], own_amount, flag, own_flag)
                else:
                    charge_out[t, cells, :] -= flux(own_speed, velocity[1], own_amount, raw[9], own_flag, flag)
            own_flag = flat_flags[pl.ds(PADDED + SIDE + own_column, EDGE, stride=PADDED), :]
            for n, q in enumerate(dirs):
                cx, _, cz = LATTICE[q]
                if cx:
                    end = 0 if cx > 0 else 1
                    row = SIDE - 1 if cx > 0 else SIDE + EDGE
                    beside_y[side, n, pl.ds(row, 1), :] = beside_x[end, x_dirs[end].index(q), pl.ds(column, 1), :]
                value = beside_y[side, n, pl.ds(SIDE - cx, EDGE), :]
                flag = flat_flags[pl.ds((1 - cx) * PADDED + column, EDGE, stride=PADDED), :]
                if cz:
                    value, flag = pltpu.roll(value, cz % DEPTH, 1), pltpu.roll(flag, cz % DEPTH, 1)
                band = ACROSS_Y.index(q)
                rows = pl.ds(own_column % 8, EDGE, stride=8)
                kept = flat_bands[t, band, rows, :]
                flat_bands[t, band, rows, :] = jnp.where((flag == 1) & (own_flag == 1), value, kept)
        for copy in pieces(t):
            copy.start()
        return carry

    lax.fori_loop(0, tiles, patch, 0, unroll=2)
    for tile in range(tiles):
        for copy in pieces(tile):
            copy.wait()


def per_device(populations, charge, fluid_mask, tile_ids, phase_label, permittivity):
    peers = lax.axis_size("gy")
    tiles = charge.shape[0]
    rows, cols = phase_label.shape[0], phase_label.shape[1]
    band_cols = TILE_COLS * peers
    band = peers * tiles
    per_x, per_y = unit_counts(peers)
    out_rows = (2 * per_x + per_y) * 8
    in_rows = out_rows + -(-2 * per_x // 8) * 8
    f32 = jnp.float32
    shape = jax.ShapeDtypeStruct
    gx_up, gx_down = ring_pairs("gx")
    gy_up, gy_down = ring_pairs("gy")
    me = lax.axis_index("gy").astype(jnp.int32)
    pops = pltpu.with_memory_space_constraint(populations.reshape(19, tiles, AREA, DEPTH), pltpu.HBM)
    held = charge.reshape(tiles, AREA, DEPTH)

    outgoing = pl.pallas_call(
        functools.partial(pack_source, tiles, band_cols),
        out_shape=pltpu.HBM((peers, AREA + 8, DEPTH), f32),
        in_specs=[SMEM, VMEM, VMEM], out_specs=VMEM, compiler_params=room(6), name="pack_source",
    )(tile_ids, held, fluid_mask)
    outgoing, phase_label = lax.optimization_barrier((outgoing, phase_label))
    arrived = lax.all_to_all(outgoing, "gy", split_axis=0, concat_axis=0, tiled=True)

    beside = [lax.ppermute(phase_label[rows - WIDER :], "gx", gx_up)]
    beside.append(lax.ppermute(phase_label[:WIDER], "gx", gx_down))
    beside = list(lax.optimization_barrier(tuple(beside)))
    tall = jnp.concatenate([beside[0][:, cols - SIDE :], phase_label[:, cols - SIDE :], beside[1][:, cols - SIDE :]])
    beside.append(lax.ppermute(tall, "gy", gy_up))
    tall = jnp.concatenate([beside[0][:, :SIDE], phase_label[:, :SIDE], beside[1][:, :SIDE]])
    beside.append(lax.ppermute(tall, "gy", gy_down))

    one_tile = pl.BlockSpec((1, AREA, DEPTH), lambda t: (t, 0, 0))
    raw, bits = pl.pallas_call(
        functools.partial(raw_faces, peers),
        grid=(tiles,),
        out_shape=[pltpu.HBM((peers, tiles, out_rows, DEPTH), f32), pltpu.HBM(held.shape, jnp.int32)],
        in_specs=[
            pl.BlockSpec((19, 1, AREA, DEPTH), lambda t: (0, t, 0, 0)),
            one_tile,
            pl.BlockSpec((1, EDGE + 2, EDGE + 2, DEPTH), lambda t: (t, 0, 0, 0)),
        ],
        out_specs=[pl.BlockSpec((peers, 1, out_rows, DEPTH), lambda t: (0, t, 0, 0)), one_tile],
        scratch_shapes=[pltpu.VMEM((3, EDGE + 2, PADDED, DEPTH), jnp.int32)],
        compiler_params=room(14), name="raw_faces",
    )(pops, held, fluid_mask)
    arrived, raw, beside = lax.optimization_barrier((arrived, raw, beside))
    beside = list(beside)

    tile_at = arrived[:, AREA, :tiles].astype(jnp.int32).reshape(band)
    slots = jnp.arange(band, dtype=jnp.int32)
    local = jnp.arange(tiles, dtype=jnp.int32)
    mine = local // TILE_COLS * band_cols + TILE_COLS * me + local % TILE_COLS
    wanted = jnp.concatenate([slots, mine])
    slot_of = jnp.sum(jnp.where(tile_at[None, :] == wanted[:, None], slots[None, :], 0), axis=1)

    block, left, right = pl.pallas_call(
        functools.partial(assemble, band, tiles),
        out_shape=[pltpu.VMEM((rows, cols, DEPTH), f32), shape((rows, SIDE, DEPTH), f32), shape((rows, SIDE, DEPTH), f32)],
        in_specs=[SMEM, VMEM], out_specs=[VMEM] * 3, compiler_params=room(5), name="assemble",
    )(slot_of, arrived)
    left, right = lax.ppermute(right, "gy", gy_up), lax.ppermute(left, "gy", gy_down)
    ends = shape((WIDE, cols + 2 * SIDE, DEPTH), f32)
    ups, downs = pl.pallas_call(
        edge_rows, out_shape=[ends, ends], in_specs=[VMEM] * 3, out_specs=[VMEM] * 2,
        compiler_params=room(3), name="edge_rows",
    )(block, left, right)
    ups, downs, beside[0] = lax.optimization_barrier((ups, downs, beside[0]))
    before, after = lax.ppermute(ups, "gx", gx_up), lax.ppermute(downs, "gx", gx_down)
    hbm = pl.BlockSpec(memory_space=pl.ANY)
    token = pl.pallas_call(
        tick, out_shape=shape((8, DEPTH), f32), in_specs=[hbm], out_specs=VMEM, compiler_params=room(1), name="tick"
    )(downs)
    raw, token = lax.optimization_barrier((raw, token))
    token, beside[0] = lax.optimization_barrier((token, beside[0]))
    wide = shape((rows + 2 * WIDER, cols + 2 * SIDE, DEPTH), f32)
    scratch = pltpu.VMEM(wide.shape, f32)
    weights = pl.pallas_call(
        face_weights, out_shape=[pltpu.VMEM(wide.shape, f32)] * 4, in_specs=[SMEM] + [VMEM] * 5, out_specs=[VMEM] * 4,
        scratch_shapes=[scratch], compiler_params=room(12), name="face_weights",
    )(permittivity, phase_label, *beside)

    faces = lax.all_to_all(raw, "gy", split_axis=0, concat_axis=0, tiled=True).reshape(band, out_rows, DEPTH)
    faces = pltpu.with_memory_space_constraint(faces, pltpu.HBM)
    potential, frames = pl.pallas_call(
        functools.partial(solve, band, tiles),
        out_shape=[shape((rows, cols, DEPTH), f32), pltpu.HBM((peers, FRAME * FRAME, DEPTH), f32)],
        in_specs=[SMEM] + [VMEM] * 9 + [hbm], out_specs=[VMEM, VMEM],
        scratch_shapes=[scratch] * 4, compiler_params=room(16), name="solve",
    )(slot_of, block, left, right, before, after, *weights, token)
    frames = lax.all_to_all(frames, "gy", split_axis=0, concat_axis=0, tiled=True)

    strip = shape((band_cols, per_x * 8, DEPTH), f32)
    low, high = pl.pallas_call(
        functools.partial(outer_rows, band_cols, per_x),
        out_shape=[strip, strip], in_specs=[SMEM, VMEM], out_specs=[VMEM] * 2,
        compiler_params=room(5), name="outer_rows",
    )(slot_of, faces)
    below = lax.ppermute(high, "gx", gx_up)
    above = lax.ppermute(low, "gx", gx_down)
    table = pltpu.VMEM((band, per_x * 8, DEPTH), f32)
    turned = pl.pallas_call(
        functools.partial(turn_faces, band_cols, per_x),
        out_shape=pltpu.HBM((band, in_rows, DEPTH), f32),
        in_specs=[SMEM, SMEM, SMEM, VMEM, VMEM, VMEM], out_specs=VMEM,
        scratch_shapes=[table, table], compiler_params=room(8), name="turn_faces",
    )(slot_of, tile_at, jnp.stack([me % 2, me]), faces, below, above)
    rims = lax.all_to_all(turned.reshape(peers, tiles, in_rows, DEPTH), "gy", split_axis=0, concat_axis=0, tiled=True)

    padded = pltpu.VMEM((EDGE + 2, PADDED, DEPTH), f32)
    near = pltpu.VMEM((FRAME, PADDED, DEPTH), f32)
    by_tile = pl.BlockSpec((1, AREA, DEPTH), lambda t, ids: (t, 0, 0))
    of_pops = pl.BlockSpec((19, 1, AREA, DEPTH), lambda t, ids: (0, t, 0, 0))
    of_frame = pl.BlockSpec((1, FRAME * FRAME, DEPTH), lambda t, ids: (ids[t] % band_cols // TILE_COLS, 0, 0))
    of_edges = pl.BlockSpec((1, 4, EDGE, DEPTH), lambda t, ids: (t, 0, 0, 0))
    bits = pltpu.with_memory_space_constraint(bits, pltpu.HBM)
    closed, closed_charge, edges, bands, lines = pl.pallas_call(
        step_inside,
        grid_spec=pltpu.PrefetchScalarGridSpec(
            num_scalar_prefetch=1,
            grid=(tiles,),
            in_specs=[of_pops, by_tile, by_tile, of_frame],
            out_specs=[
                of_pops, by_tile, of_edges,
                pl.BlockSpec((1, len(ACROSS_Y), EDGE, 8, DEPTH), lambda t, ids: (t, 0, 0, 0, 0)),
                pl.BlockSpec((1, len(ACROSS_X), EDGE, DEPTH), lambda t, ids: (t, 0, 0, 0)),
            ],
            scratch_shapes=[
                near,
                pltpu.VMEM((19, EDGE + 2, PADDED, DEPTH), f32),
                padded, padded, padded, padded,
            ],
        ),
        out_shape=[
            shape(pops.shape, f32), pltpu.HBM(held.shape, f32), shape((tiles, 4, EDGE, DEPTH), f32),
            pltpu.HBM((tiles, len(ACROSS_Y), EDGE, 8, DEPTH), f32),
            pltpu.HBM((tiles, len(ACROSS_X), EDGE, DEPTH), f32),
        ],
        compiler_params=room(24), name="step_inside",
    )(tile_ids, pops, held, bits, frames)
    bands, lines, closed_charge = (
        pltpu.with_memory_space_constraint(x, pltpu.HBM) for x in (bands, lines, closed_charge)
    )
    charge_next, populations_next = pl.pallas_call(
        functools.partial(step_faces, peers, tiles, band_cols),
        in_specs=[SMEM] + [VMEM] * 5 + [hbm, VMEM, VMEM, hbm],
        out_specs=[VMEM, hbm],
        scratch_shapes=[
            pltpu.VMEM((tiles, FRAME, PADDED, DEPTH), f32),
            pltpu.VMEM((tiles, EDGE + 2, PADDED, DEPTH), jnp.int32),
            pltpu.VMEM((tiles, CHANNELS, PADDED, DEPTH), f32),
            pltpu.VMEM((tiles, 2, 5, PADDED, DEPTH), f32),
            pltpu.VMEM((tiles, 2, 5, PADDED, DEPTH), f32),
            pltpu.VMEM((tiles, len(ACROSS_Y), EDGE, 8, DEPTH), f32),
            pltpu.VMEM((tiles, len(ACROSS_X), EDGE, DEPTH), f32),
            pltpu.SemaphoreType.DMA((tiles, 1 + len(ACROSS_Y + ACROSS_X))),
        ],
        out_shape=[shape(held.shape, f32), shape(populations.shape, f32)],
        input_output_aliases={9: 1},
        compiler_params=room(20), name="step_faces",
    )(tile_ids, held, fluid_mask, frames, rims, edges, bands, lines, closed_charge, closed.reshape(populations.shape))
    return (populations_next, charge_next.reshape(charge.shape), potential)


def solution(mesh):
    placed = (
        P(None, ("gx", "gy"), None, None, None),
        P(("gx", "gy"), None, None, None),
        P(("gx", "gy"), None, None, None),
        P(("gx", "gy")),
        P("gx", "gy", None),
        P(),
    )
    return jax.shard_map(
        per_device,
        mesh=mesh,
        in_specs=placed,
        out_specs=(
            P(None, ("gx", "gy"), None, None, None),
            P(("gx", "gy"), None, None, None),
            P("gx", "gy", None),
        ),
        check_vma=False,
    )
```

time: 153 us -> 117 us (0.76)
  blocking collectives: 25.3 us -> 0 us
  Pallas kernels: 56.1 us -> 43.5 us
  starting transfers between devices: 28.7 us -> 35 us
  local copies, waits for them, and re-layouts: 7.84 us -> 3.99 us
  other arithmetic: 2.16 us -> 0.29 us
    all_to_all x1 -> x0, blocking collectives: 25.3 us -> none  [per_device(): lax.all_to_all(turned.reshape(peers, tiles, in_rows, DEPTH), 'gy', split_...]
    pallas_call x4 -> x7, Pallas kernels: 42.1 us -> 29.5 us  [the longest x1 13.7 us: per_device(): pl.pallas_call(step_inside, grid_spec=pltpu.PrefetchScalarGridSpec(num_sc...]
    ppermute x8, waiting for transfers between devices: 21.8 us -> 11.1 us  [the longest x1 3.29 us: per_device(): beside.append(lax.ppermute(tall, 'gy', gy_up))]
    all_to_all x0 -> x1, waiting for transfers between devices: none -> 7.37 us  [per_device(): lax.all_to_all(turned.reshape(peers, tiles, in_rows, DEPTH), 'gy', split_...]
    unnamed x31 -> x23, local copies, waits for them, and re-layouts: 7.03 us -> 2.58 us
    all_to_all x0 -> x1, starting transfers between devices: none -> 4.29 us  [per_device(): lax.all_to_all(turned.reshape(peers, tiles, in_rows, DEPTH), 'gy', split_...]
    ppermute x1, starting transfers between devices: 0.01 us -> 2.95 us  [per_device(): below = lax.ppermute(high, 'gx', gx_up)]
    ppermute x1, starting transfers between devices: 3.82 us -> 0.92 us  [per_device(): above = lax.ppermute(low, 'gx', gx_down)]
  transfers between devices with their start and end apart: 13 -> 14, of which waited for: 5 -> 10; matrix products, arithmetic and copies ran while one was open for 3% -> 1% of each run, Pallas kernels for 20% -> 30%
where the time goes in v2:
time: 117 us; the launch traced here: 116 us
  Pallas kernels  43.5 us (37%)
  starting transfers between devices  35 us (30%)
  waiting for transfers between devices  33 us (28%)
  local copies, waits for them, and re-layouts  3.99 us (3%)
    pallas_call x1, Pallas kernels, per_device(): pl.pallas_call(step_inside, grid_spec=pltpu.PrefetchScalarGridSpec(num_sc...  13.7 us
    all_to_all x1, waiting for transfers between devices, per_device(): lax.all_to_all(turned.reshape(peers, tiles, in_rows, DEPTH), 'gy', split_...  7.37 us
    pallas_call x1, Pallas kernels, per_device(): pl.pallas_call(functools.partial(step_faces, peers, tiles, band_cols), in...  6.58 us
    pallas_call x1, Pallas kernels, per_device(): pl.pallas_call(functools.partial(raw_faces, peers), grid=(tiles,), out_sh...  6.56 us
    pallas_call x1, Pallas kernels, per_device(): pl.pallas_call(functools.partial(solve, band, tiles), out_shape=[shape((r...  6.39 us
    ppermute x1, waiting for transfers between devices, per_device(): below = lax.ppermute(high, 'gx', gx_up)  5.91 us
    all_to_all x1, starting transfers between devices, per_device(): lax.all_to_all(outgoing, 'gy', split_axis=0, concat_axis=0, tiled=True)  5.3 us
    all_to_all x1, starting transfers between devices, per_device(): lax.all_to_all(raw, 'gy', split_axis=0, concat_axis=0, tiled=True)  4.75 us
  transfers between devices with their start and end apart: 14, of which 10 were waited for; matrix products, arithmetic and copies ran while one was open for 1% of the time, Pallas kernels for 30%

profile of v2, /device:TPU:0, one launch (start us, length us, event | category | flops | bytes accessed | tf_op | source)
XLA Modules:
  0.0 116.4 jit_solution(17421654204364846000)
XLA Ops:
  0.6 0.0 copy-start.5
  0.6 0.0 copy-start
  0.7 1.2 %copy.18.mask = s32[4,18,18,128]{3,2,1,0:T(8,128)S(1)} copy(s32[4,18,18,128]{3,0,2,1:T(4,128)} %param.8) | data formatting | bytes 1327104 | tf_op args[2]
  1.9 0.0 copy-done.5
  1.9 0.0 copy-done
  1.9 1.6 %pack_source.1 = f32[8,264,128]{2,1,0:T(8,128)} custom-call(s32[4]{0:T(128)S(1)} %copy-done.5, f32[4,256,128]{2,1,0:T(8,128)S(1)} %bitcast.8, s32[4,18,18,128]{3,2,1,0:T(8,128)S(1)} %copy.18.mask), custom_call_target="tpu_custom_call" | custom-call | tf_op jit(solution)/shard_map/pack_source/pallas_call | solution.py:629
  3.5 0.0 copy-start.1
  3.5 5.3 %all-to-all-start = ((f32[8,264,128]{2,1,0:T(8,128)}), f32[8,264,128]{2,1,0:T(8,128)S(1)}, u32[]{:S(2)}, u32[]{:S(2)}) async-start(f32[8,264,128]{2,1,0:T(8,128)} %pack_source.1), calls=%async_computation | async-start | bytes 2162688 | tf_op jit(solution)/shard_map/all_to_all | solution.py:635
  8.8 0.0 copy-done.1
  8.8 0.7 fusion.4
  9.5 3.6 %collective-permute-start.1 = (s32[6,32,128]{2,1,0:T(8,128)}, s32[6,32,128]{2,1,0:T(8,128)S(1)}, u32[]{:S(2)}, u32[]{:S(2)}) collective-permute-start(s32[6,32,128]{2,1,0:T(8,128)} %get-tuple-element.83), channel_id=1, source_target_pairs={{8,0},{16,8},{24,16},{0,24},{9,1},{17,9},{25,17},{1,25},{10,2},{18... | collective-permute-start | bytes 294920 | tf_op jit(solution)/shard_map/ppermute | solution.py:638
  13.1 0.0 collective-permute-start
  13.1 0.7 fusion.3
  13.8 0.0 copy-start.10
  13.8 6.6 %raw_faces.1 = (f32[8,4,88,128]{3,2,1,0:T(8,128)}, s32[4,256,128]{2,1,0:T(8,128)}) custom-call(f32[19,4,256,128]{3,2,1,0:T(8,128)} %bitcast.12, f32[4,256,128]{2,1,0:T(8,128)S(1)} %bitcast.9, s32[4,18,18,128]{3,2,1,0:T(8,128)S(1)} %copy.18.mask), custom_call_target="tpu_custom_call" | custom-call | tf_op jit(solution)/shard_map/raw_faces/pallas_call | solution.py:646
  20.3 0.0 collective-permute-done.1.after
  20.3 0.0 collective-permute-done.before
  20.4 0.3 collective-permute-start.2
  20.7 0.0 copy-done.10
  20.7 2.5 %collective-permute-start.3 = (s32[44,8,128]{2,1,0:T(8,128)S(1)}, s32[44,8,128]{2,1,0:T(8,128)S(1)}, u32[]{:S(2)}, u32[]{:S(2)}) collective-permute-start(s32[44,8,128]{2,1,0:T(8,128)S(1)} %pad_add_fusion.1), channel_id=1, source_target_pairs={{1,0},{2,1},{3,2},{4,3},{5,4},{6,5},{7,6},{0,7},{9,8},{10,9},{11,1... | collective-permute-start | bytes 540680 | tf_op jit(solution)/shard_map/ppermute | solution.py:643
  23.2 0.1 pad_add_fusion.2
  23.2 3.3 %collective-permute-done.2.left = s32[44,8,128]{2,1,0:T(8,128)S(1)} collective-permute-done((s32[44,8,128]{2,1,0:T(8,128)S(1)}, s32[44,8,128]{2,1,0:T(8,128)S(1)}, u32[]{:S(2)}, u32[]{:S(2)}) %collective-permute-start.2) | collective-permute-done | bytes 180256 | tf_op jit(solution)/shard_map/ppermute | solution.py:641
  26.5 0.3 collective-permute-done.3.right
  26.8 0.0 copy-start.3
  26.8 0.7 copy-done.3
  27.5 0.0 all-to-all-done.arrived
  27.5 0.1 convert_element_type.12.tile_at
  27.6 0.0 copy-start.6
  27.6 0.1 select_reduce_fusion.slot_of
  27.7 0.6 assemble.1
  28.3 1.8 %collective-permute-start.4 = (f32[32,8,128]{2,1,0:T(8,128)S(1)}, f32[32,8,128]{2,1,0:T(8,128)S(1)}, u32[]{:S(2)}, u32[]{:S(2)}) collective-permute-start(f32[32,8,128]{2,1,0:T(8,128)S(1)} %get-tuple-element.49), channel_id=1, source_target_pairs={{0,1},{1,2},{2,3},{3,4},{4,5},{5,6},{6,7},{7,0},{8,9},{9,10},{10,1... | collective-permute-start | bytes 393224 | tf_op jit(solution)/shard_map/ppermute | solution.py:674
  30.1 1.1 collective-permute-start.5
  31.2 2.9 %collective-permute-done.4.left = f32[32,8,128]{2,1,0:T(8,128)S(1)} collective-permute-done((f32[32,8,128]{2,1,0:T(8,128)S(1)}, f32[32,8,128]{2,1,0:T(8,128)S(1)}, u32[]{:S(2)}, u32[]{:S(2)}) %collective-permute-start.4) | collective-permute-done | bytes 131104 | tf_op jit(solution)/shard_map/ppermute | solution.py:674
  34.1 0.0 collective-permute-done.5.right
  34.1 0.0 copy-done.6
  34.1 0.0 copy-start.9
  34.1 0.6 copy-done.9
  34.8 0.0 copy-start.2
  34.8 4.8 %all-to-all-start.2 = ((f32[8,4,88,128]{3,2,1,0:T(8,128)}), f32[8,4,88,128]{3,2,1,0:T(8,128)}, u32[]{:S(2)}, u32[]{:S(2)}) async-start(f32[8,4,88,128]{3,2,1,0:T(8,128)} %get-tuple-element.69), calls=%async_computation.2 | async-start | bytes 2883584 | tf_op jit(solution)/shard_map/all_to_all | solution.py:695
  39.5 3.1 %collective-permute-start.6 = (f32[5,48,128]{2,1,0:T(8,128)}, f32[5,48,128]{2,1,0:T(8,128)S(1)}, u32[]{:S(2)}, u32[]{:S(2)}) collective-permute-start(f32[5,48,128]{2,1,0:T(8,128)} %copy-done.9), channel_id=1, source_target_pairs={{0,8},{8,16},{16,24},{24,0},{1,9},{9,17},{17,25},{25,1},{2,10},{10... | collective-permute-start | bytes 368648 | tf_op jit(solution)/shard_map/ppermute | solution.py:681
  42.6 0.8 collective-permute-start.7
  43.4 0.0 copy-done.2
  43.4 0.0 copy-done.4
  43.4 0.0 copy-done.8
  43.4 2.3 %face_weights.1 = (f32[44,48,128]{2,1,0:T(8,128)S(1)}, f32[44,48,128]{2,1,0:T(8,128)S(1)}, f32[44,48,128]{2,1,0:T(8,128)S(1)}, f32[44,48,128]{2,1,0:T(8,128)S(1)}) custom-call(f32[4]{0:T(128)S(1)} %copy-done.8, s32[32,32,128]{2,1,0:T(8,128)S(1)} %copy-done.2, s32[6,32,128]{2,1,0:T(8,128)S(1)} %collective-permute-done.before, ...), custom_call_target="tpu_custom_call" | custom-call | tf_op jit(solution)/shard_map/face_weights/pallas_call | solution.py:690
  45.7 1.4 %collective-permute-done.6.before = f32[5,48,128]{2,1,0:T(8,128)S(1)} collective-permute-done((f32[5,48,128]{2,1,0:T(8,128)}, f32[5,48,128]{2,1,0:T(8,128)S(1)}, u32[]{:S(2)}, u32[]{:S(2)}) %collective-permute-start.6) | collective-permute-done | bytes 122912 | tf_op jit(solution)/shard_map/ppermute | solution.py:681
  47.1 3.2 %collective-permute-done.7.after = f32[5,48,128]{2,1,0:T(8,128)S(1)} collective-permute-done((f32[5,48,128]{2,1,0:T(8,128)S(1)}, f32[5,48,128]{2,1,0:T(8,128)S(1)}, u32[]{:S(2)}, u32[]{:S(2)}) %collective-permute-start.7) | collective-permute-done | bytes 122912 | tf_op jit(solution)/shard_map/ppermute | solution.py:681
  50.4 6.4 %solve.1 = (f32[32,32,128]{2,1,0:T(8,128)}, f32[8,400,128]{2,1,0:T(8,128)}) custom-call(s32[36]{0:T(128)S(1)} %select_reduce_fusion.slot_of, f32[32,32,128]{2,1,0:T(8,128)S(1)} %get-tuple-element.48.block.middle, f32[32,8,128]{2,1,0:T(8,128)S(1)} %collective-permute-done.4.left, f32[32,8,128]{2,1,0:T(8,128)S(1)} %collective-permute-done.5.right, ...), custom_call_target="tpu_custom_call" | custom-call | tf_op jit(solution)/shard_map/solve/pallas_call | solution.py:697
  56.8 2.5 %all-to-all-done.2 = f32[8,4,88,128]{3,2,1,0:T(8,128)} async-done(((f32[8,4,88,128]{3,2,1,0:T(8,128)}), f32[8,4,88,128]{3,2,1,0:T(8,128)}, u32[]{:S(2)}, u32[]{:S(2)}) %all-to-all-start.2) | async-done | bytes 1441824 | tf_op jit(solution)/shard_map/all_to_all | solution.py:695
  59.3 3.6 %all-to-all-start.1 = ((f32[8,400,128]{2,1,0:T(8,128)}), f32[8,400,128]{2,1,0:T(8,128)S(1)}, u32[]{:S(2)}, u32[]{:S(2)}) async-start(f32[8,400,128]{2,1,0:T(8,128)} %get-tuple-element.68), calls=%async_computation.1 | async-start | bytes 3276800 | tf_op jit(solution)/shard_map/all_to_all | solution.py:703
  62.9 0.0 copy-start.7
  62.9 2.2 %outer_rows.1 = (f32[16,24,128]{2,1,0:T(8,128)}, f32[16,24,128]{2,1,0:T(8,128)}) custom-call(s32[36]{0:T(128)S(1)} %select_reduce_fusion.slot_of, f32[32,88,128]{2,1,0:T(8,128)} %bitcast.4.arrived), custom_call_target="tpu_custom_call" | custom-call | tf_op jit(solution)/shard_map/outer_rows/pallas_call | solution.py:706
  65.1 2.9 %collective-permute-start.8 = (f32[16,24,128]{2,1,0:T(8,128)}, f32[16,24,128]{2,1,0:T(8,128)S(1)}, u32[]{:S(2)}, u32[]{:S(2)}) collective-permute-start(f32[16,24,128]{2,1,0:T(8,128)} %get-tuple-element.70), channel_id=1, source_target_pairs={{0,8},{8,16},{16,24},{24,0},{1,9},{9,17},{17,25},{25,1},{2,10},{10... | collective-permute-start | bytes 589832 | tf_op jit(solution)/shard_map/ppermute | solution.py:711
  68.0 0.9 collective-permute-start.9
  68.9 0.1 pad_add_fusion.3.odd
  69.0 5.9 %collective-permute-done.8.below = f32[16,24,128]{2,1,0:T(8,128)S(1)} collective-permute-done((f32[16,24,128]{2,1,0:T(8,128)}, f32[16,24,128]{2,1,0:T(8,128)S(1)}, u32[]{:S(2)}, u32[]{:S(2)}) %collective-permute-start.8) | collective-permute-done | bytes 196640 | tf_op jit(solution)/shard_map/ppermute | solution.py:711
  74.9 3.8 %collective-permute-done.9.above = f32[16,24,128]{2,1,0:T(8,128)S(1)} collective-permute-done((f32[16,24,128]{2,1,0:T(8,128)}, f32[16,24,128]{2,1,0:T(8,128)S(1)}, u32[]{:S(2)}, u32[]{:S(2)}) %collective-permute-start.9) | collective-permute-done | bytes 196640 | tf_op jit(solution)/shard_map/ppermute | solution.py:712
  78.8 0.0 copy-done.7
  78.8 3.6 %turn_faces.1 = f32[32,96,128]{2,1,0:T(8,128)} custom-call(s32[36]{0:T(128)S(1)} %select_reduce_fusion.slot_of, s32[32]{0:T(128)S(1)} %copy-done.7, s32[2]{0:T(128)S(1)} %pad_add_fusion.3.odd, f32[32,88,128]{2,1,0:T(8,128)} %bitcast.4.arrived, f32[16,24,128]{2,1,0:T(8,128)S(1)} %collective-permute-done.8.below, f32[16,24,128]{2,1,0:T(8,128)S(1)} %collective-permute-done.9.above), custom_call_target="tpu_custom_call" | custom-call | tf_op jit(solution)/shard_map/turn_faces/pallas_call | solution.py:714
  82.3 2.2 %all-to-all-done.1.frame.frames = f32[8,400,128]{2,1,0:T(8,128)S(1)} async-done(((f32[8,400,128]{2,1,0:T(8,128)}), f32[8,400,128]{2,1,0:T(8,128)S(1)}, u32[]{:S(2)}, u32[]{:S(2)}) %all-to-all-start.1) | async-done | bytes 1638432 | tf_op jit(solution)/shard_map/all_to_all | solution.py:703
  84.5 4.3 %all-to-all-start.3 = ((f32[8,4,96,128]{3,2,1,0:T(8,128)}), f32[8,4,96,128]{3,2,1,0:T(8,128)}, u32[]{:S(2)}, u32[]{:S(2)}) async-start(f32[8,4,96,128]{3,2,1,0:T(8,128)} %bitcast.15), calls=%async_computation.3 | async-start | bytes 3145728 | tf_op jit(solution)/shard_map/all_to_all | solution.py:720
  88.8 13.7 %step_inside.1 = (f32[19,4,256,128]{3,2,1,0:T(8,128)}, f32[4,256,128]{2,1,0:T(8,128)}, f32[4,4,16,128]{3,2,1,0:T(8,128)S(1)}, f32[4,10,16,8,128]{4,3,2,1,0:T(8,128)}, f32[4,10,16,128]{3,2,1,0:T(8,128)}) custom-call(s32[4]{0:T(128)S(1)} %copy-done.5, f32[19,4,256,128]{3,2,1,0:T(8,128)} %bitcast.13, f32[4,256,128]{2,1,0:T(8,128)S(1)} %bitcast.10, ...), custom_call_target="tpu_custom_call" | custom-call | tf_op jit(solution)/shard_map/step_inside/pallas_call | solution.py:729
  102.5 7.4 %all-to-all-done.3.rims = f32[8,4,96,128]{3,2,1,0:T(8,128)} async-done(((f32[8,4,96,128]{3,2,1,0:T(8,128)}), f32[8,4,96,128]{3,2,1,0:T(8,128)}, u32[]{:S(2)}, u32[]{:S(2)}) %all-to-all-start.3) | async-done | bytes 1572896 | tf_op jit(solution)/shard_map/all_to_all | solution.py:720
  109.9 6.6 %step_faces.1 = (f32[4,256,128]{2,1,0:T(8,128)}, f32[19,4,16,16,128]{4,3,2,1,0:T(8,128)}) custom-call(s32[4]{0:T(128)S(1)} %copy-done.5, f32[4,256,128]{2,1,0:T(8,128)S(1)} %bitcast.11, s32[4,18,18,128]{3,2,1,0:T(8,128)S(1)} %copy.18.mask, f32[8,400,128]{2,1,0:T(8,128)S(1)} %all-to-all-done.1.frame.frames, ...), custom_call_target="tpu_custom_call", output_to_operand_aliasing={{1}: (9, {})} | custom-call | tf_op jit(solution)/shard_map/step_faces/pallas_call | solution.py:756
  (10 shorter events, 0.1 us)
Async XLA Ops:
  0.6 1.3 %copy-start.5 = (s32[4]{0:T(128)S(1)}, s32[4]{0:T(128)}, u32[]{:S(2)}) copy-start(s32[4]{0:T(128)} %ids.5) | copy-start | bytes 52
  0.6 1.3 %copy-start = (f32[4,16,16,128]{3,2,1,0:T(8,128)S(1)}, f32[4,16,16,128]{3,2,1,0:T(8,128)}, u32[]{:S(2)}) copy-start(f32[4,16,16,128]{3,2,1,0:T(8,128)} %param.7) | copy-start | bytes 1572868
  3.5 5.3 %copy-start.1 = (s32[32,32,128]{2,1,0:T(8,128)S(1)}, s32[32,32,128]{2,1,0:T(8,128)}, u32[]{:S(2)}) copy-start(s32[32,32,128]{2,1,0:T(8,128)} %labels) | copy-start | bytes 1572868
  3.5 24.0 %all-to-all-start = ((f32[8,264,128]{2,1,0:T(8,128)}), f32[8,264,128]{2,1,0:T(8,128)S(1)}, u32[]{:S(2)}, u32[]{:S(2)}) async-start(f32[8,264,128]{2,1,0:T(8,128)} %pack_source.1), calls=%async_computation | async-start | bytes 2162688 | tf_op jit(solution)/shard_map/all_to_all | solution.py:635
  9.5 10.8 %collective-permute-start.1 = (s32[6,32,128]{2,1,0:T(8,128)}, s32[6,32,128]{2,1,0:T(8,128)S(1)}, u32[]{:S(2)}, u32[]{:S(2)}) collective-permute-start(s32[6,32,128]{2,1,0:T(8,128)} %get-tuple-element.83), channel_id=1, source_target_pairs={{8,0},{16,8},{24,16},{0,24},{9,1},{17,9},{25,17},{1,25},{10,2},{18... | collective-permute-start | bytes 294920 | tf_op jit(solution)/shard_map/ppermute | solution.py:638
  13.1 7.2 %collective-permute-start = (s32[6,32,128]{2,1,0:T(8,128)S(1)}, s32[6,32,128]{2,1,0:T(8,128)S(1)}, u32[]{:S(2)}, u32[]{:S(2)}) collective-permute-start(s32[6,32,128]{2,1,0:T(8,128)S(1)} %get-tuple-element.84), channel_id=1, source_target_pairs={{0,8},{8,16},{16,24},{24,0},{1,9},{9,17},{17,25},{25,1},{2,10},{10... | collective-permute-start | bytes 294920 | tf_op jit(solution)/shard_map/ppermute | solution.py:637
  13.8 6.9 %copy-start.10 = (s32[32,8,128]{2,1,0:T(8,128)S(1)}, s32[32,8,128]{2,1,0:T(8,128)}, u32[]{:S(2)}) copy-start(s32[32,8,128]{2,1,0:T(8,128)} %get-tuple-element.81) | copy-start | bytes 393220
  20.4 6.1 %collective-permute-start.2 = (s32[44,8,128]{2,1,0:T(8,128)S(1)}, s32[44,8,128]{2,1,0:T(8,128)S(1)}, u32[]{:S(2)}, u32[]{:S(2)}) collective-permute-start(s32[44,8,128]{2,1,0:T(8,128)S(1)} %pad_add_fusion), channel_id=1, source_target_pairs={{0,1},{1,2},{2,3},{3,4},{4,5},{5,6},{6,7},{7,0},{8,9},{9,10},{10,1... | collective-permute-start | bytes 540680 | tf_op jit(solution)/shard_map/ppermute | solution.py:641
  20.7 6.1 %collective-permute-start.3 = (s32[44,8,128]{2,1,0:T(8,128)S(1)}, s32[44,8,128]{2,1,0:T(8,128)S(1)}, u32[]{:S(2)}, u32[]{:S(2)}) collective-permute-start(s32[44,8,128]{2,1,0:T(8,128)S(1)} %pad_add_fusion.1), channel_id=1, source_target_pairs={{1,0},{2,1},{3,2},{4,3},{5,4},{6,5},{7,6},{0,7},{9,8},{10,9},{11,1... | collective-permute-start | bytes 540680 | tf_op jit(solution)/shard_map/ppermute | solution.py:643
  26.8 0.7 copy-start.3
  27.6 6.5 %copy-start.6 = (s32[32]{0:T(128)}, s32[32]{0:T(128)S(1)}, u32[]{:S(2)}) copy-start(s32[32]{0:T(128)S(1)} %convert_element_type.12.tile_at) | copy-start | bytes 388
  28.3 5.8 %collective-permute-start.4 = (f32[32,8,128]{2,1,0:T(8,128)S(1)}, f32[32,8,128]{2,1,0:T(8,128)S(1)}, u32[]{:S(2)}, u32[]{:S(2)}) collective-permute-start(f32[32,8,128]{2,1,0:T(8,128)S(1)} %get-tuple-element.49), channel_id=1, source_target_pairs={{0,1},{1,2},{2,3},{3,4},{4,5},{5,6},{6,7},{7,0},{8,9},{9,10},{10,1... | collective-permute-start | bytes 393224 | tf_op jit(solution)/shard_map/ppermute | solution.py:674
  30.1 4.0 %collective-permute-start.5 = (f32[32,8,128]{2,1,0:T(8,128)S(1)}, f32[32,8,128]{2,1,0:T(8,128)S(1)}, u32[]{:S(2)}, u32[]{:S(2)}) collective-permute-start(f32[32,8,128]{2,1,0:T(8,128)S(1)} %get-tuple-element.50), channel_id=1, source_target_pairs={{1,0},{2,1},{3,2},{4,3},{5,4},{6,5},{7,6},{0,7},{9,8},{10,9},{11,1... | collective-permute-start | bytes 393224 | tf_op jit(solution)/shard_map/ppermute | solution.py:674
  34.1 0.7 copy-start.9
  34.8 8.6 %copy-start.2 = (s32[32,32,128]{2,1,0:T(8,128)S(1)}, s32[32,32,128]{2,1,0:T(8,128)}, u32[]{:S(2)}) copy-start(s32[32,32,128]{2,1,0:T(8,128)} %labels) | copy-start | bytes 1572868
  34.8 8.6 %copy-start.4 = (s32[44,8,128]{2,1,0:T(8,128)S(1)}, s32[44,8,128]{2,1,0:T(8,128)}, u32[]{:S(2)}) copy-start(s32[44,8,128]{2,1,0:T(8,128)} %copy-done.3) | copy-start | bytes 540676
  34.8 8.6 %copy-start.8 = (f32[4]{0:T(128)S(1)}, f32[4]{0:T(128)}, u32[]{:S(2)}) copy-start(f32[4]{0:T(128)} %table.1) | copy-start | bytes 52
  34.8 24.5 %all-to-all-start.2 = ((f32[8,4,88,128]{3,2,1,0:T(8,128)}), f32[8,4,88,128]{3,2,1,0:T(8,128)}, u32[]{:S(2)}, u32[]{:S(2)}) async-start(f32[8,4,88,128]{3,2,1,0:T(8,128)} %get-tuple-element.69), calls=%async_computation.2 | async-start | bytes 2883584 | tf_op jit(solution)/shard_map/all_to_all | solution.py:695
  39.5 7.6 %collective-permute-start.6 = (f32[5,48,128]{2,1,0:T(8,128)}, f32[5,48,128]{2,1,0:T(8,128)S(1)}, u32[]{:S(2)}, u32[]{:S(2)}) collective-permute-start(f32[5,48,128]{2,1,0:T(8,128)} %copy-done.9), channel_id=1, source_target_pairs={{0,8},{8,16},{16,24},{24,0},{1,9},{9,17},{17,25},{25,1},{2,10},{10... | collective-permute-start | bytes 368648 | tf_op jit(solution)/shard_map/ppermute | solution.py:681
  42.6 7.8 %collective-permute-start.7 = (f32[5,48,128]{2,1,0:T(8,128)S(1)}, f32[5,48,128]{2,1,0:T(8,128)S(1)}, u32[]{:S(2)}, u32[]{:S(2)}) collective-permute-start(f32[5,48,128]{2,1,0:T(8,128)S(1)} %get-tuple-element.55._), channel_id=1, source_target_pairs={{8,0},{16,8},{24,16},{0,24},{9,1},{17,9},{25,17},{1,25},{10,2},{18... | collective-permute-start | bytes 368648 | tf_op jit(solution)/shard_map/ppermute | solution.py:681
  59.3 25.3 %all-to-all-start.1 = ((f32[8,400,128]{2,1,0:T(8,128)}), f32[8,400,128]{2,1,0:T(8,128)S(1)}, u32[]{:S(2)}, u32[]{:S(2)}) async-start(f32[8,400,128]{2,1,0:T(8,128)} %get-tuple-element.68), calls=%async_computation.1 | async-start | bytes 3276800 | tf_op jit(solution)/shard_map/all_to_all | solution.py:703
  62.9 15.9 %copy-start.7 = (s32[32]{0:T(128)S(1)}, s32[32]{0:T(128)}, u32[]{:S(2)}) copy-start(s32[32]{0:T(128)} %copy-done.6) | copy-start | bytes 388
  65.1 9.9 %collective-permute-start.8 = (f32[16,24,128]{2,1,0:T(8,128)}, f32[16,24,128]{2,1,0:T(8,128)S(1)}, u32[]{:S(2)}, u32[]{:S(2)}) collective-permute-start(f32[16,24,128]{2,1,0:T(8,128)} %get-tuple-element.70), channel_id=1, source_target_pairs={{0,8},{8,16},{16,24},{24,0},{1,9},{9,17},{17,25},{25,1},{2,10},{10... | collective-permute-start | bytes 589832 | tf_op jit(solution)/shard_map/ppermute | solution.py:711
  68.0 10.8 %collective-permute-start.9 = (f32[16,24,128]{2,1,0:T(8,128)}, f32[16,24,128]{2,1,0:T(8,128)S(1)}, u32[]{:S(2)}, u32[]{:S(2)}) collective-permute-start(f32[16,24,128]{2,1,0:T(8,128)} %get-tuple-element.71), channel_id=1, source_target_pairs={{8,0},{16,8},{24,16},{0,24},{9,1},{17,9},{25,17},{1,25},{10,2},{18... | collective-permute-start | bytes 589832 | tf_op jit(solution)/shard_map/ppermute | solution.py:712
  84.5 25.3 %all-to-all-start.3 = ((f32[8,4,96,128]{3,2,1,0:T(8,128)}), f32[8,4,96,128]{3,2,1,0:T(8,128)}, u32[]{:S(2)}, u32[]{:S(2)}) async-start(f32[8,4,96,128]{3,2,1,0:T(8,128)} %bitcast.15), calls=%async_computation.3 | async-start | bytes 3145728 | tf_op jit(solution)/shard_map/all_to_all | solution.py:720

commit v3 on v2

--- a/solution.py
+++ b/solution.py
@@ -278,22 +278,22 @@
             ]
 
 
-def unit_counts(peers):
-    per_x = -(-HALVES // peers)
-    per_y = -(-2 * HALVES // peers)
-    return per_x, per_y
+def unit_count(peers):
+    return -(-2 * HALVES // peers)
 
 
 def unit_places(peers):
-    per_x, per_y = unit_counts(peers)
     places = {}
-    for unit in range(HALVES):
-        for face in range(2):
-            places[face, unit // 2, unit % 2] = (unit % peers, (face * per_x + unit // peers) * 8)
-    for unit in range(2 * HALVES):
-        face, rest = 2 + unit // HALVES, unit % HALVES
-        places[face, rest // 2, rest % 2] = (unit % peers, (2 * per_x + unit // peers) * 8)
+    for face in range(4):
+        for rest in range(HALVES):
+            unit = face % 2 * HALVES + rest
+            row = (face // 2 * unit_count(peers) + unit // peers) * 8
+            places[face, rest // 2, rest % 2] = (unit % peers, row)
     return places
+
+
+def x_slots(peers):
+    return -(-HALVES // peers), HALVES // peers
 
 
 FACES = ((0, -1), (0, 1), (1, -1), (1, 1))
@@ -344,51 +344,56 @@
                 out[peer, 0, pl.ds(row, 8), :] = value
 
 
-def outer_rows(band_cols, per_x, slot_of, arrived, low, high):
-    size = per_x * 8
+def outer_rows(peers, band_cols, slot_of, arrived, low, high):
+    count = unit_count(peers)
+    low_count, first_high = x_slots(peers)
     for col in range(band_cols):
-        low[col] = arrived[slot_of[col], pl.ds(0, size), :]
-        high[col] = arrived[slot_of[(TILE_ROWS - 1) * band_cols + col], pl.ds(size, size), :]
-
-
-def turn_faces(band_cols, per_x, slot_of, tile_at, odd, arrived, below, above, out, from_low, from_high):
-    size = per_x * 8
-    rest = arrived.shape[1] - 2 * size
+        low[col] = arrived[slot_of[col], pl.ds(0, low_count * 8), :]
+        slot = slot_of[(TILE_ROWS - 1) * band_cols + col]
+        high[col] = arrived[slot, pl.ds(first_high * 8, (count - first_high) * 8), :]
+
+
+def turn_faces(peers, band_cols, slot_of, tile_at, me_ref, arrived, below, above, out, from_low, from_high):
+    count = unit_count(peers)
+    low_count, first_high = x_slots(peers)
+    lows, highs = pl.ds(0, low_count * 8), pl.ds(first_high * 8, (count - first_high) * 8)
 
     def lay(col, carry):
         from_low[col] = below[col]
         from_high[(TILE_ROWS - 1) * band_cols + col] = above[col]
         for row in range(1, TILE_ROWS):
-            from_low[row * band_cols + col] = arrived[slot_of[(row - 1) * band_cols + col], pl.ds(size, size), :]
-            from_high[(row - 1) * band_cols + col] = arrived[slot_of[row * band_cols + col], pl.ds(0, size), :]
-        return carry
-
-    lax.fori_loop(0, band_cols, lay, 0)
-    half = odd[0]
-    pick = 7 * half
-    per_y = rest // 8
-    me = odd[1]
-    peers = out.shape[0] // (out.shape[0] // (band_cols // TILE_COLS))
+            from_low[row * band_cols + col] = arrived[slot_of[(row - 1) * band_cols + col], highs, :]
+            from_high[(row - 1) * band_cols + col] = arrived[slot_of[row * band_cols + col], lows, :]
+        return carry
+
+    lax.fori_loop(0, band_cols, lay, 0, unroll=2)
+    me = me_ref[0]
+    half = me % 2
+    is_low = [n * peers + me < HALVES for n in range(count)]
+
+    def across_x(position, n, row, size):
+        if n < low_count:
+            value = from_high[position, pl.ds(n * 8 + row, size), :]
+        if n >= first_high:
+            other = from_low[position, pl.ds((n - first_high) * 8 + row, size), :]
+            value = jnp.where(is_low[n], value, other) if n < low_count else other
+        return value
 
     def send(d, carry):
         p = tile_at[d]
         row, col = p // band_cols, p % band_cols
         right, left = (col + 1) % band_cols, (col + band_cols - 1) % band_cols
-        out[d, pl.ds(0, size), :] = from_high[p]
-        out[d, pl.ds(size, size), :] = from_low[p]
         slot_right = slot_of[row * band_cols + right]
         slot_left = slot_of[row * band_cols + left]
-        for q in range(per_y):
-            is_low = q * peers + me < HALVES
-            slot = jnp.where(is_low, slot_right, slot_left)
-            out[d, pl.ds(2 * size + q * 8, 8), :] = arrived[slot, pl.ds(2 * size + q * 8, 8), :]
         beside = row * band_cols + jnp.where(half == 0, right, left)
-        for q in range(per_x):
-            out[d, pl.ds(2 * size + rest + q, 1), :] = from_high[beside, pl.ds(q * 8 + pick, 1), :]
-            out[d, pl.ds(2 * size + rest + per_x + q, 1), :] = from_low[beside, pl.ds(q * 8 + pick, 1), :]
-        return carry
-
-    lax.fori_loop(0, out.shape[0], send, 0)
+        for n in range(count):
+            out[d, pl.ds(n * 8, 8), :] = across_x(p, n, 0, 8)
+            cells = pl.ds((count + n) * 8, 8)
+            out[d, cells, :] = arrived[jnp.where(is_low[n], slot_right, slot_left), cells, :]
+            out[d, pl.ds(2 * count * 8 + n, 1), :] = across_x(beside, n, 7 * half, 1)
+        return carry
+
+    lax.fori_loop(0, out.shape[0], send, 0, unroll=2)
 
 
 ACROSS_X = [q for q in range(19) if LATTICE[q][0]]
@@ -473,52 +478,60 @@
 
     lax.fori_loop(0, EDGE, stream_row, 0, unroll=4)
     for n, q in enumerate(ACROSS_Y):
-        first = 0 if LATTICE[q][1] > 0 else EDGE - 8
-        for row in range(EDGE):
-            bands[0, n, row] = out[q, 0, pl.ds(row * EDGE + first, 8), :]
+        bands[0, n] = out[q, 0, pl.ds(0 if LATTICE[q][1] > 0 else EDGE - 1, EDGE, stride=EDGE), :]
     for n, q in enumerate(ACROSS_X):
         lines[0, n] = out[q, 0, pl.ds(0 if LATTICE[q][0] > 0 else AREA - EDGE, EDGE), :]
 
 
-def step_faces(peers, tiles, band_cols, ids, charge, mask, frames, rims, edges, bands, lines, charge_in, _,
-               charge_out, out, all_near, all_flags, all_rim, all_x, all_y, new_bands, new_lines, sems):
-    per_x, per_y = unit_counts(peers)
+def step_faces(peers, tiles, band_cols, ids, charge_at, mask_at, frames_at, rims_at, edges_at, bands_at, lines_at,
+               charge_in_at, _, charge_out_at, out, charge, mask, frames, rims, edges, new_bands, lines, charge_out,
+               all_near, all_flags, all_rim, all_x, all_y, new_lines, in_sems, out_sems):
     places = unit_places(peers)
-    corner_row = (2 * per_x + per_y) * 8
+    corner_row = 2 * unit_count(peers) * 8
     all_flat_near = all_near.reshape(tiles, FRAME * PADDED, DEPTH)
     all_flat_flags = all_flags.reshape(tiles, (EDGE + 2) * PADDED, DEPTH)
-    flat_bands = new_bands.reshape(tiles, len(ACROSS_Y), EDGE * 8, DEPTH)
 
     def pieces(tile):
         made = []
         for n, q in enumerate(ACROSS_Y):
-            first = 0 if LATTICE[q][1] > 0 else EDGE - 8
-            made.append((new_bands.at[tile, n], out.at[q, tile, :, pl.ds(first, 8)]))
+            made.append((new_bands.at[tile, n], out.at[q, tile, :, 0 if LATTICE[q][1] > 0 else EDGE - 1]))
         for n, q in enumerate(ACROSS_X):
             layer = 0 if LATTICE[q][0] > 0 else EDGE - 1
             if LATTICE[q][1]:
-                cells = pl.ds(8 if LATTICE[q][1] > 0 else 0, 8)
+                cells = pl.ds(1 if LATTICE[q][1] > 0 else 0, EDGE - 1)
                 made.append((new_lines.at[tile, n, cells], out.at[q, tile, layer, cells]))
             else:
                 made.append((new_lines.at[tile, n], out.at[q, tile, layer]))
-        return [pltpu.make_async_copy(a, b, sems.at[tile, n]) for n, (a, b) in enumerate(made)]
+        made.append((charge_out.at[tile], charge_out_at.at[tile]))
+        return [pltpu.make_async_copy(a, b, out_sems.at[tile, n]) for n, (a, b) in enumerate(made)]
 
     def incoming(tile):
-        return pltpu.make_async_copy(bands.at[tile], new_bands.at[tile], sems.at[tile, len(ACROSS_Y + ACROSS_X)])
+        owner = ids[tile] % band_cols // TILE_COLS
+        pairs = [
+            (mask_at.at[tile], mask.at[tile]),
+            (frames_at.at[owner], frames.at[tile]),
+            (rims_at.at[:, tile], rims.at[:, tile]),
+            (charge_at.at[tile], charge.at[tile]),
+            (charge_in_at.at[tile], charge_out.at[tile]),
+            (edges_at.at[tile], edges.at[tile]),
+            (lines_at.at[tile], lines.at[tile]),
+            (bands_at.at[tile], new_bands.at[tile]),
+        ]
+        return [pltpu.make_async_copy(a, b, in_sems.at[tile, n]) for n, (a, b) in enumerate(pairs)]
 
     for tile in range(tiles):
-        incoming(tile).start()
+        for copy in incoming(tile):
+            copy.start()
 
     def patch(t, carry):
         near, flags, rim, beside_x, beside_y = (x.at[t] for x in (all_near, all_flags, all_rim, all_x, all_y))
         flat_near, flat_flags = all_flat_near.at[t], all_flat_flags.at[t]
-        owner = ids[t] % band_cols // TILE_COLS
+        for copy in incoming(t):
+            copy.wait()
         for a in range(FRAME):
-            near[a, pl.ds(SIDE - RING, FRAME), :] = frames[owner, pl.ds(a * FRAME, FRAME), :]
+            near[a, pl.ds(SIDE - RING, FRAME), :] = frames[t, pl.ds(a * FRAME, FRAME), :]
         for i in range(EDGE + 2):
             flags[i, pl.ds(SIDE - 1, EDGE + 2), :] = mask[t, i]
-        charge_out[t] = charge_in[t]
-        incoming(t).wait()
 
         for side, face, layer in ((0, 1, 0), (1, 0, EDGE + 1)):
             for channel in range(CHANNELS):
@@ -558,8 +571,6 @@
                 taken = (flag == 1) & (own_flag == 1)
                 merged = jnp.where(taken, value, lines[t, line])
                 new_lines[t, line] = merged
-                if cy:
-                    new_bands[t, ACROSS_Y.index(q), own_layer] = merged[:8] if cy > 0 else merged[8:]
 
         for side, face, column in ((0, 3, SIDE - 1), (1, 2, SIDE + EDGE)):
             dirs = crossing(*FACES[face])
@@ -596,9 +607,7 @@
                 if cz:
                     value, flag = pltpu.roll(value, cz % DEPTH, 1), pltpu.roll(flag, cz % DEPTH, 1)
                 band = ACROSS_Y.index(q)
-                rows = pl.ds(own_column % 8, EDGE, stride=8)
-                kept = flat_bands[t, band, rows, :]
-                flat_bands[t, band, rows, :] = jnp.where((flag == 1) & (own_flag == 1), value, kept)
+                new_bands[t, band] = jnp.where((flag == 1) & (own_flag == 1), value, new_bands[t, band])
         for copy in pieces(t):
             copy.start()
         return carry
@@ -615,9 +624,10 @@
     rows, cols = phase_label.shape[0], phase_label.shape[1]
     band_cols = TILE_COLS * peers
     band = peers * tiles
-    per_x, per_y = unit_counts(peers)
-    out_rows = (2 * per_x + per_y) * 8
-    in_rows = out_rows + -(-2 * per_x // 8) * 8
+    count = unit_count(peers)
+    low_count, first_high = x_slots(peers)
+    out_rows = 2 * count * 8
+    in_rows = out_rows + -(-count // 8) * 8
     f32 = jnp.float32
     shape = jax.ShapeDtypeStruct
     gx_up, gx_down = ring_pairs("gx")
@@ -702,21 +712,21 @@
     )(slot_of, block, left, right, before, after, *weights, token)
     frames = lax.all_to_all(frames, "gy", split_axis=0, concat_axis=0, tiled=True)
 
-    strip = shape((band_cols, per_x * 8, DEPTH), f32)
+    lows = (band_cols, low_count * 8, DEPTH)
+    highs = (band_cols, (count - first_high) * 8, DEPTH)
     low, high = pl.pallas_call(
-        functools.partial(outer_rows, band_cols, per_x),
-        out_shape=[strip, strip], in_specs=[SMEM, VMEM], out_specs=[VMEM] * 2,
+        functools.partial(outer_rows, peers, band_cols),
+        out_shape=[shape(lows, f32), shape(highs, f32)], in_specs=[SMEM, VMEM], out_specs=[VMEM] * 2,
         compiler_params=room(5), name="outer_rows",
     )(slot_of, faces)
     below = lax.ppermute(high, "gx", gx_up)
     above = lax.ppermute(low, "gx", gx_down)
-    table = pltpu.VMEM((band, per_x * 8, DEPTH), f32)
     turned = pl.pallas_call(
-        functools.partial(turn_faces, band_cols, per_x),
+        functools.partial(turn_faces, peers, band_cols),
         out_shape=pltpu.HBM((band, in_rows, DEPTH), f32),
         in_specs=[SMEM, SMEM, SMEM, VMEM, VMEM, VMEM], out_specs=VMEM,
-        scratch_shapes=[table, table], compiler_params=room(8), name="turn_faces",
-    )(slot_of, tile_at, jnp.stack([me % 2, me]), faces, below, above)
+        scratch_shapes=[pltpu.VMEM((band,) + highs[1:], f32), pltpu.VMEM((band,) + lows[1:], f32)], compiler_params=room(8), name="turn_faces",
+    )(slot_of, tile_at, me[None], faces, below, above)
     rims = lax.all_to_all(turned.reshape(peers, tiles, in_rows, DEPTH), "gy", split_axis=0, concat_axis=0, tiled=True)
 
     padded = pltpu.VMEM((EDGE + 2, PADDED, DEPTH), f32)
@@ -734,7 +744,7 @@
             in_specs=[of_pops, by_tile, by_tile, of_frame],
             out_specs=[
                 of_pops, by_tile, of_edges,
-                pl.BlockSpec((1, len(ACROSS_Y), EDGE, 8, DEPTH), lambda t, ids: (t, 0, 0, 0, 0)),
+                pl.BlockSpec((1, len(ACROSS_Y), EDGE, DEPTH), lambda t, ids: (t, 0, 0, 0)),
                 pl.BlockSpec((1, len(ACROSS_X), EDGE, DEPTH), lambda t, ids: (t, 0, 0, 0)),
             ],
             scratch_shapes=[
@@ -745,7 +755,7 @@
         ),
         out_shape=[
             shape(pops.shape, f32), pltpu.HBM(held.shape, f32), shape((tiles, 4, EDGE, DEPTH), f32),
-            pltpu.HBM((tiles, len(ACROSS_Y), EDGE, 8, DEPTH), f32),
+            pltpu.HBM((tiles, len(ACROSS_Y), EDGE, DEPTH), f32),
             pltpu.HBM((tiles, len(ACROSS_X), EDGE, DEPTH), f32),
         ],
         compiler_params=room(24), name="step_inside",
@@ -755,16 +765,24 @@
     )
     charge_next, populations_next = pl.pallas_call(
         functools.partial(step_faces, peers, tiles, band_cols),
-        in_specs=[SMEM] + [VMEM] * 5 + [hbm, VMEM, VMEM, hbm],
-        out_specs=[VMEM, hbm],
+        in_specs=[SMEM] + [hbm] * 9,
+        out_specs=[hbm, hbm],
         scratch_shapes=[
+            pltpu.VMEM(held.shape, f32),
+            pltpu.VMEM(fluid_mask.shape, jnp.int32),
+            pltpu.VMEM((tiles, FRAME * FRAME, DEPTH), f32),
+            pltpu.VMEM(rims.shape, f32),
+            pltpu.VMEM(edges.shape, f32),
+            pltpu.VMEM(bands.shape, f32),
+            pltpu.VMEM(lines.shape, f32),
+            pltpu.VMEM(held.shape, f32),
             pltpu.VMEM((tiles, FRAME, PADDED, DEPTH), f32),
             pltpu.VMEM((tiles, EDGE + 2, PADDED, DEPTH), jnp.int32),
             pltpu.VMEM((tiles, CHANNELS, PADDED, DEPTH), f32),
             pltpu.VMEM((tiles, 2, 5, PADDED, DEPTH), f32),
             pltpu.VMEM((tiles, 2, 5, PADDED, DEPTH), f32),
-            pltpu.VMEM((tiles, len(ACROSS_Y), EDGE, 8, DEPTH), f32),
-            pltpu.VMEM((tiles, len(ACROSS_X), EDGE, DEPTH), f32),
+            pltpu.VMEM(lines.shape, f32),
+            pltpu.SemaphoreType.DMA((tiles, 8)),
             pltpu.SemaphoreType.DMA((tiles, 1 + len(ACROSS_Y + ACROSS_X))),
         ],
         out_shape=[shape(held.shape, f32), shape(populations.shape, f32)],

time: 117 us -> 113 us (0.966)
  Pallas kernels: 43.5 us -> 41.1 us
  waiting for transfers between devices: 33 us -> 31.7 us
    all_to_all x1, waiting for transfers between devices: 2.5 us -> 1.1 us  [per_device(): lax.all_to_all(raw, 'gy', split_axis=0, concat_axis=0, tiled=True)]
    all_to_all x1, waiting for transfers between devices: 2.19 us -> 3.45 us  [per_device(): lax.all_to_all(frames, 'gy', split_axis=0, concat_axis=0, tiled=True)]
  transfers between devices with their start and end apart: 14 -> 14, of which waited for: 10 -> 10; matrix products, arithmetic and copies ran while one was open for 1% -> 1% of each run, Pallas kernels for 30% -> 29%
where the time goes in v3:
time: 113 us
  Pallas kernels  41.1 us (36%)
  starting transfers between devices  35 us (31%)
  waiting for transfers between devices  31.7 us (28%)
  local copies, waits for them, and re-layouts  3.99 us (4%)
    pallas_call x1, Pallas kernels, per_device(): pl.pallas_call(step_inside, grid_spec=pltpu.PrefetchScalarGridSpec(num_sc...  13.2 us
    pallas_call x1, Pallas kernels, per_device(): pl.pallas_call(functools.partial(raw_faces, peers), grid=(tiles,), out_sh...  6.53 us
    all_to_all x1, waiting for transfers between devices, per_device(): lax.all_to_all(turned.reshape(peers, tiles, in_rows, DEPTH), 'gy', split_...  6.46 us
    pallas_call x1, Pallas kernels, per_device(): pl.pallas_call(functools.partial(solve, band, tiles), out_shape=[shape((r...  6.39 us
    pallas_call x1, Pallas kernels, per_device(): pl.pallas_call(functools.partial(step_faces, peers, tiles, band_cols), in...  5.87 us
    ppermute x1, waiting for transfers between devices, per_device(): below = lax.ppermute(high, 'gx', gx_up)  5.73 us
    all_to_all x1, starting transfers between devices, per_device(): lax.all_to_all(outgoing, 'gy', split_axis=0, concat_axis=0, tiled=True)  5.3 us
    all_to_all x1, starting transfers between devices, per_device(): lax.all_to_all(raw, 'gy', split_axis=0, concat_axis=0, tiled=True)  4.75 us
  transfers between devices with their start and end apart: 14, of which 10 were waited for; matrix products, arithmetic and copies ran while one was open for 1% of the time, Pallas kernels for 29%

profile of v3, /device:TPU:0, one launch (start us, length us, event | category | flops | bytes accessed | tf_op | source)
XLA Modules:
  0.0 112.9 jit_solution(9071838168424428130)
XLA Ops:
  0.6 0.0 copy-start.5
  0.6 0.0 copy-start
  0.7 1.2 %copy.18.mask.mask_at = s32[4,18,18,128]{3,2,1,0:T(8,128)S(1)} copy(s32[4,18,18,128]{3,0,2,1:T(4,128)} %param.8) | data formatting | bytes 1327104 | tf_op args[2]
  1.9 0.0 copy-done.5
  1.9 0.0 copy-done
  1.9 1.6 %pack_source.1 = f32[8,264,128]{2,1,0:T(8,128)} custom-call(s32[4]{0:T(128)S(1)} %copy-done.5, f32[4,256,128]{2,1,0:T(8,128)S(1)} %bitcast.7, s32[4,18,18,128]{3,2,1,0:T(8,128)S(1)} %copy.18.mask.mask_at), custom_call_target="tpu_custom_call" | custom-call | tf_op jit(solution)/shard_map/pack_source/pallas_call | solution.py:639
  3.5 0.0 copy-start.1
  3.5 5.3 %all-to-all-start = ((f32[8,264,128]{2,1,0:T(8,128)}), f32[8,264,128]{2,1,0:T(8,128)S(1)}, u32[]{:S(2)}, u32[]{:S(2)}) async-start(f32[8,264,128]{2,1,0:T(8,128)} %pack_source.1), calls=%async_computation | async-start | bytes 2162688 | tf_op jit(solution)/shard_map/all_to_all | solution.py:645
  8.8 0.0 copy-done.1
  8.8 0.7 fusion.4
  9.5 3.6 %collective-permute-start.1 = (s32[6,32,128]{2,1,0:T(8,128)}, s32[6,32,128]{2,1,0:T(8,128)S(1)}, u32[]{:S(2)}, u32[]{:S(2)}) collective-permute-start(s32[6,32,128]{2,1,0:T(8,128)} %get-tuple-element.83), channel_id=1, source_target_pairs={{8,0},{16,8},{24,16},{0,24},{9,1},{17,9},{25,17},{1,25},{10,2},{18... | collective-permute-start | bytes 294920 | tf_op jit(solution)/shard_map/ppermute | solution.py:648
  13.1 0.0 collective-permute-start
  13.1 0.7 fusion.3
  13.8 0.0 copy-start.10
  13.8 6.5 %raw_faces.1 = (f32[8,4,80,128]{3,2,1,0:T(8,128)}, s32[4,256,128]{2,1,0:T(8,128)}) custom-call(f32[19,4,256,128]{3,2,1,0:T(8,128)} %bitcast.11, f32[4,256,128]{2,1,0:T(8,128)S(1)} %bitcast.8, s32[4,18,18,128]{3,2,1,0:T(8,128)S(1)} %copy.18.mask.mask_at), custom_call_target="tpu_custom_call" | custom-call | tf_op jit(solution)/shard_map/raw_faces/pallas_call | solution.py:656
  20.3 0.0 collective-permute-done.1.after
  20.3 0.0 collective-permute-done.before
  20.4 0.3 collective-permute-start.2
  20.6 0.0 copy-done.10
  20.6 2.5 %collective-permute-start.3 = (s32[44,8,128]{2,1,0:T(8,128)S(1)}, s32[44,8,128]{2,1,0:T(8,128)S(1)}, u32[]{:S(2)}, u32[]{:S(2)}) collective-permute-start(s32[44,8,128]{2,1,0:T(8,128)S(1)} %pad_add_fusion.1), channel_id=1, source_target_pairs={{1,0},{2,1},{3,2},{4,3},{5,4},{6,5},{7,6},{0,7},{9,8},{10,9},{11,1... | collective-permute-start | bytes 540680 | tf_op jit(solution)/shard_map/ppermute | solution.py:653
  23.1 0.1 pad_add_fusion.2
  23.2 3.3 %collective-permute-done.2.left = s32[44,8,128]{2,1,0:T(8,128)S(1)} collective-permute-done((s32[44,8,128]{2,1,0:T(8,128)S(1)}, s32[44,8,128]{2,1,0:T(8,128)S(1)}, u32[]{:S(2)}, u32[]{:S(2)}) %collective-permute-start.2) | collective-permute-done | bytes 180256 | tf_op jit(solution)/shard_map/ppermute | solution.py:651
  26.5 0.3 collective-permute-done.3.right
  26.8 0.0 copy-start.3
  26.8 0.7 copy-done.3
  27.5 0.0 all-to-all-done.arrived
  27.5 0.1 convert_element_type.12.tile_at
  27.6 0.0 copy-start.6
  27.6 0.1 select_reduce_fusion.slot_of
  27.7 0.6 assemble.1
  28.3 1.8 %collective-permute-start.4 = (f32[32,8,128]{2,1,0:T(8,128)S(1)}, f32[32,8,128]{2,1,0:T(8,128)S(1)}, u32[]{:S(2)}, u32[]{:S(2)}) collective-permute-start(f32[32,8,128]{2,1,0:T(8,128)S(1)} %get-tuple-element.49), channel_id=1, source_target_pairs={{0,1},{1,2},{2,3},{3,4},{4,5},{5,6},{6,7},{7,0},{8,9},{9,10},{10,1... | collective-permute-start | bytes 393224 | tf_op jit(solution)/shard_map/ppermute | solution.py:684
  30.1 1.1 %collective-permute-start.5 = (f32[32,8,128]{2,1,0:T(8,128)S(1)}, f32[32,8,128]{2,1,0:T(8,128)S(1)}, u32[]{:S(2)}, u32[]{:S(2)}) collective-permute-start(f32[32,8,128]{2,1,0:T(8,128)S(1)} %get-tuple-element.50), channel_id=1, source_target_pairs={{1,0},{2,1},{3,2},{4,3},{5,4},{6,5},{7,6},{0,7},{9,8},{10,9},{11,1... | collective-permute-start | bytes 393224 | tf_op jit(solution)/shard_map/ppermute | solution.py:684
  31.2 2.9 %collective-permute-done.4.left = f32[32,8,128]{2,1,0:T(8,128)S(1)} collective-permute-done((f32[32,8,128]{2,1,0:T(8,128)S(1)}, f32[32,8,128]{2,1,0:T(8,128)S(1)}, u32[]{:S(2)}, u32[]{:S(2)}) %collective-permute-start.4) | collective-permute-done | bytes 131104 | tf_op jit(solution)/shard_map/ppermute | solution.py:684
  34.1 0.0 collective-permute-done.5.right
  34.1 0.0 copy-done.6
  34.1 0.0 copy-start.9
  34.1 0.6 copy-done.9
  34.8 0.0 copy-start.2
  34.8 0.0 copy-start.4
  34.8 4.8 %all-to-all-start.2 = ((f32[8,4,80,128]{3,2,1,0:T(8,128)}), f32[8,4,80,128]{3,2,1,0:T(8,128)}, u32[]{:S(2)}, u32[]{:S(2)}) async-start(f32[8,4,80,128]{3,2,1,0:T(8,128)} %get-tuple-element.69), calls=%async_computation.2 | async-start | bytes 2621440 | tf_op jit(solution)/shard_map/all_to_all | solution.py:705
  39.5 3.1 %collective-permute-start.6 = (f32[5,48,128]{2,1,0:T(8,128)}, f32[5,48,128]{2,1,0:T(8,128)S(1)}, u32[]{:S(2)}, u32[]{:S(2)}) collective-permute-start(f32[5,48,128]{2,1,0:T(8,128)} %copy-done.9), channel_id=1, source_target_pairs={{0,8},{8,16},{16,24},{24,0},{1,9},{9,17},{17,25},{25,1},{2,10},{10... | collective-permute-start | bytes 368648 | tf_op jit(solution)/shard_map/ppermute | solution.py:691
  42.6 0.8 collective-permute-start.7
  43.4 0.0 copy-done.2
  43.4 0.0 copy-done.4
  43.4 0.0 copy-done.8
  43.4 2.3 %face_weights.1 = (f32[44,48,128]{2,1,0:T(8,128)S(1)}, f32[44,48,128]{2,1,0:T(8,128)S(1)}, f32[44,48,128]{2,1,0:T(8,128)S(1)}, f32[44,48,128]{2,1,0:T(8,128)S(1)}) custom-call(f32[4]{0:T(128)S(1)} %copy-done.8, s32[32,32,128]{2,1,0:T(8,128)S(1)} %copy-done.2, s32[6,32,128]{2,1,0:T(8,128)S(1)} %collective-permute-done.before, ...), custom_call_target="tpu_custom_call" | custom-call | tf_op jit(solution)/shard_map/face_weights/pallas_call | solution.py:700
  45.7 1.5 %collective-permute-done.6.before = f32[5,48,128]{2,1,0:T(8,128)S(1)} collective-permute-done((f32[5,48,128]{2,1,0:T(8,128)}, f32[5,48,128]{2,1,0:T(8,128)S(1)}, u32[]{:S(2)}, u32[]{:S(2)}) %collective-permute-start.6) | collective-permute-done | bytes 122912 | tf_op jit(solution)/shard_map/ppermute | solution.py:691
  47.1 3.2 %collective-permute-done.7.after = f32[5,48,128]{2,1,0:T(8,128)S(1)} collective-permute-done((f32[5,48,128]{2,1,0:T(8,128)S(1)}, f32[5,48,128]{2,1,0:T(8,128)S(1)}, u32[]{:S(2)}, u32[]{:S(2)}) %collective-permute-start.7) | collective-permute-done | bytes 122912 | tf_op jit(solution)/shard_map/ppermute | solution.py:691
  50.4 6.4 %solve.1 = (f32[32,32,128]{2,1,0:T(8,128)}, f32[8,400,128]{2,1,0:T(8,128)}) custom-call(s32[36]{0:T(128)S(1)} %select_reduce_fusion.slot_of, f32[32,32,128]{2,1,0:T(8,128)S(1)} %get-tuple-element.48.block.middle, f32[32,8,128]{2,1,0:T(8,128)S(1)} %collective-permute-done.4.left, f32[32,8,128]{2,1,0:T(8,128)S(1)} %collective-permute-done.5.right, ...), custom_call_target="tpu_custom_call" | custom-call | tf_op jit(solution)/shard_map/solve/pallas_call | solution.py:707
  56.7 1.1 all-to-all-done.2
  57.8 3.6 %all-to-all-start.1 = ((f32[8,400,128]{2,1,0:T(8,128)}), f32[8,400,128]{2,1,0:T(8,128)S(1)}, u32[]{:S(2)}, u32[]{:S(2)}) async-start(f32[8,400,128]{2,1,0:T(8,128)} %get-tuple-element.68), calls=%async_computation.1 | async-start | bytes 3276800 | tf_op jit(solution)/shard_map/all_to_all | solution.py:713
  61.4 0.0 copy-start.7
  61.4 1.4 %outer_rows.1 = (f32[16,24,128]{2,1,0:T(8,128)S(1)}, f32[16,24,128]{2,1,0:T(8,128)S(1)}) custom-call(s32[36]{0:T(128)S(1)} %select_reduce_fusion.slot_of, f32[32,80,128]{2,1,0:T(8,128)} %bitcast.3.arrived), custom_call_target="tpu_custom_call" | custom-call | tf_op jit(solution)/shard_map/outer_rows/pallas_call | solution.py:717
  62.8 3.0 %collective-permute-start.8 = (f32[16,24,128]{2,1,0:T(8,128)S(1)}, f32[16,24,128]{2,1,0:T(8,128)S(1)}, u32[]{:S(2)}, u32[]{:S(2)}) collective-permute-start(f32[16,24,128]{2,1,0:T(8,128)S(1)} %get-tuple-element.70), channel_id=1, source_target_pairs={{0,8},{8,16},{16,24},{24,0},{1,9},{9,17},{17,25},{25,1},{2,10},{10... | collective-permute-start | bytes 589832 | tf_op jit(solution)/shard_map/ppermute | solution.py:722
  65.8 0.9 collective-permute-start.9
  66.8 5.7 %collective-permute-done.8.below = f32[16,24,128]{2,1,0:T(8,128)S(1)} collective-permute-done((f32[16,24,128]{2,1,0:T(8,128)S(1)}, f32[16,24,128]{2,1,0:T(8,128)S(1)}, u32[]{:S(2)}, u32[]{:S(2)}) %collective-permute-start.8) | collective-permute-done | bytes 196640 | tf_op jit(solution)/shard_map/ppermute | solution.py:722
  72.5 3.8 %collective-permute-done.9.above = f32[16,24,128]{2,1,0:T(8,128)S(1)} collective-permute-done((f32[16,24,128]{2,1,0:T(8,128)S(1)}, f32[16,24,128]{2,1,0:T(8,128)S(1)}, u32[]{:S(2)}, u32[]{:S(2)}) %collective-permute-start.9) | collective-permute-done | bytes 196640 | tf_op jit(solution)/shard_map/ppermute | solution.py:723
  76.4 0.0 copy-done.7
  76.4 3.3 %turn_faces.1 = f32[32,88,128]{2,1,0:T(8,128)} custom-call(s32[36]{0:T(128)S(1)} %select_reduce_fusion.slot_of, s32[32]{0:T(128)S(1)} %copy-done.7, s32[1]{0:T(128)} %bitcast.2.me_ref, f32[32,80,128]{2,1,0:T(8,128)} %bitcast.3.arrived, f32[16,24,128]{2,1,0:T(8,128)S(1)} %collective-permute-done.8.below, f32[16,24,128]{2,1,0:T(8,128)S(1)} %collective-permute-done.9.above), custom_call_target="tpu_custom_call" | custom-call | tf_op jit(solution)/shard_map/turn_faces/pallas_call | solution.py:724
  79.6 3.5 %all-to-all-done.1.frame.frames_at = f32[8,400,128]{2,1,0:T(8,128)S(1)} async-done(((f32[8,400,128]{2,1,0:T(8,128)}), f32[8,400,128]{2,1,0:T(8,128)S(1)}, u32[]{:S(2)}, u32[]{:S(2)}) %all-to-all-start.1) | async-done | bytes 1638432 | tf_op jit(solution)/shard_map/all_to_all | solution.py:713
  83.1 4.3 %all-to-all-start.3 = ((f32[8,4,88,128]{3,2,1,0:T(8,128)}), f32[8,4,88,128]{3,2,1,0:T(8,128)}, u32[]{:S(2)}, u32[]{:S(2)}) async-start(f32[8,4,88,128]{3,2,1,0:T(8,128)} %bitcast.14), calls=%async_computation.3 | async-start | bytes 2883584 | tf_op jit(solution)/shard_map/all_to_all | solution.py:730
  87.4 13.2 %step_inside.1 = (f32[19,4,256,128]{3,2,1,0:T(8,128)}, f32[4,256,128]{2,1,0:T(8,128)}, f32[4,4,16,128]{3,2,1,0:T(8,128)S(1)}, f32[4,10,16,128]{3,2,1,0:T(8,128)}, f32[4,10,16,128]{3,2,1,0:T(8,128)}) custom-call(s32[4]{0:T(128)S(1)} %copy-done.5, f32[19,4,256,128]{3,2,1,0:T(8,128)} %bitcast.12, f32[4,256,128]{2,1,0:T(8,128)S(1)} %bitcast.9, ...), custom_call_target="tpu_custom_call" | custom-call | tf_op jit(solution)/shard_map/step_inside/pallas_call | solution.py:739
  100.6 6.5 %all-to-all-done.3.rims_at = f32[8,4,88,128]{3,2,1,0:T(8,128)} async-done(((f32[8,4,88,128]{3,2,1,0:T(8,128)}), f32[8,4,88,128]{3,2,1,0:T(8,128)}, u32[]{:S(2)}, u32[]{:S(2)}) %all-to-all-start.3) | async-done | bytes 1441824 | tf_op jit(solution)/shard_map/all_to_all | solution.py:730
  107.0 5.9 %step_faces.1 = (f32[4,256,128]{2,1,0:T(8,128)}, f32[19,4,16,16,128]{4,3,2,1,0:T(8,128)}) custom-call(s32[4]{0:T(128)S(1)} %copy-done.5, f32[4,256,128]{2,1,0:T(8,128)S(1)} %bitcast.10, s32[4,18,18,128]{3,2,1,0:T(8,128)S(1)} %copy.18.mask.mask_at, f32[8,400,128]{2,1,0:T(8,128)S(1)} %all-to-all-done.1.frame.frames_at, ...), custom_call_target="tpu_custom_call", output_to_operand_aliasing={{1}: (9, {})} | custom-call | tf_op jit(solution)/shard_map/step_faces/pallas_call | solution.py:766
  (9 shorter events, 0.1 us)
Async XLA Ops:
  0.6 1.3 %copy-start.5 = (s32[4]{0:T(128)S(1)}, s32[4]{0:T(128)}, u32[]{:S(2)}) copy-start(s32[4]{0:T(128)} %ids.5) | copy-start | bytes 52
  0.6 1.3 %copy-start = (f32[4,16,16,128]{3,2,1,0:T(8,128)S(1)}, f32[4,16,16,128]{3,2,1,0:T(8,128)}, u32[]{:S(2)}) copy-start(f32[4,16,16,128]{3,2,1,0:T(8,128)} %param.7) | copy-start | bytes 1572868
  3.5 5.3 %copy-start.1 = (s32[32,32,128]{2,1,0:T(8,128)S(1)}, s32[32,32,128]{2,1,0:T(8,128)}, u32[]{:S(2)}) copy-start(s32[32,32,128]{2,1,0:T(8,128)} %labels) | copy-start | bytes 1572868
  3.5 23.9 %all-to-all-start = ((f32[8,264,128]{2,1,0:T(8,128)}), f32[8,264,128]{2,1,0:T(8,128)S(1)}, u32[]{:S(2)}, u32[]{:S(2)}) async-start(f32[8,264,128]{2,1,0:T(8,128)} %pack_source.1), calls=%async_computation | async-start | bytes 2162688 | tf_op jit(solution)/shard_map/all_to_all | solution.py:645
  9.5 10.8 %collective-permute-start.1 = (s32[6,32,128]{2,1,0:T(8,128)}, s32[6,32,128]{2,1,0:T(8,128)S(1)}, u32[]{:S(2)}, u32[]{:S(2)}) collective-permute-start(s32[6,32,128]{2,1,0:T(8,128)} %get-tuple-element.83), channel_id=1, source_target_pairs={{8,0},{16,8},{24,16},{0,24},{9,1},{17,9},{25,17},{1,25},{10,2},{18... | collective-permute-start | bytes 294920 | tf_op jit(solution)/shard_map/ppermute | solution.py:648
  13.1 7.2 %collective-permute-start = (s32[6,32,128]{2,1,0:T(8,128)S(1)}, s32[6,32,128]{2,1,0:T(8,128)S(1)}, u32[]{:S(2)}, u32[]{:S(2)}) collective-permute-start(s32[6,32,128]{2,1,0:T(8,128)S(1)} %get-tuple-element.84), channel_id=1, source_target_pairs={{0,8},{8,16},{16,24},{24,0},{1,9},{9,17},{17,25},{25,1},{2,10},{10... | collective-permute-start | bytes 294920 | tf_op jit(solution)/shard_map/ppermute | solution.py:647
  13.8 6.9 %copy-start.10 = (s32[32,8,128]{2,1,0:T(8,128)S(1)}, s32[32,8,128]{2,1,0:T(8,128)}, u32[]{:S(2)}) copy-start(s32[32,8,128]{2,1,0:T(8,128)} %get-tuple-element.81) | copy-start | bytes 393220
  20.4 6.2 %collective-permute-start.2 = (s32[44,8,128]{2,1,0:T(8,128)S(1)}, s32[44,8,128]{2,1,0:T(8,128)S(1)}, u32[]{:S(2)}, u32[]{:S(2)}) collective-permute-start(s32[44,8,128]{2,1,0:T(8,128)S(1)} %pad_add_fusion), channel_id=1, source_target_pairs={{0,1},{1,2},{2,3},{3,4},{4,5},{5,6},{6,7},{7,0},{8,9},{9,10},{10,1... | collective-permute-start | bytes 540680 | tf_op jit(solution)/shard_map/ppermute | solution.py:651
  20.6 6.1 %collective-permute-start.3 = (s32[44,8,128]{2,1,0:T(8,128)S(1)}, s32[44,8,128]{2,1,0:T(8,128)S(1)}, u32[]{:S(2)}, u32[]{:S(2)}) collective-permute-start(s32[44,8,128]{2,1,0:T(8,128)S(1)} %pad_add_fusion.1), channel_id=1, source_target_pairs={{1,0},{2,1},{3,2},{4,3},{5,4},{6,5},{7,6},{0,7},{9,8},{10,9},{11,1... | collective-permute-start | bytes 540680 | tf_op jit(solution)/shard_map/ppermute | solution.py:653
  26.8 0.7 copy-start.3
  27.6 6.5 %copy-start.6 = (s32[32]{0:T(128)}, s32[32]{0:T(128)S(1)}, u32[]{:S(2)}) copy-start(s32[32]{0:T(128)S(1)} %convert_element_type.12.tile_at) | copy-start | bytes 388
  28.3 5.8 %collective-permute-start.4 = (f32[32,8,128]{2,1,0:T(8,128)S(1)}, f32[32,8,128]{2,1,0:T(8,128)S(1)}, u32[]{:S(2)}, u32[]{:S(2)}) collective-permute-start(f32[32,8,128]{2,1,0:T(8,128)S(1)} %get-tuple-element.49), channel_id=1, source_target_pairs={{0,1},{1,2},{2,3},{3,4},{4,5},{5,6},{6,7},{7,0},{8,9},{9,10},{10,1... | collective-permute-start | bytes 393224 | tf_op jit(solution)/shard_map/ppermute | solution.py:684
  30.1 4.0 %collective-permute-start.5 = (f32[32,8,128]{2,1,0:T(8,128)S(1)}, f32[32,8,128]{2,1,0:T(8,128)S(1)}, u32[]{:S(2)}, u32[]{:S(2)}) collective-permute-start(f32[32,8,128]{2,1,0:T(8,128)S(1)} %get-tuple-element.50), channel_id=1, source_target_pairs={{1,0},{2,1},{3,2},{4,3},{5,4},{6,5},{7,6},{0,7},{9,8},{10,9},{11,1... | collective-permute-start | bytes 393224 | tf_op jit(solution)/shard_map/ppermute | solution.py:684
  34.1 0.7 copy-start.9
  34.8 8.6 %copy-start.2 = (s32[32,32,128]{2,1,0:T(8,128)S(1)}, s32[32,32,128]{2,1,0:T(8,128)}, u32[]{:S(2)}) copy-start(s32[32,32,128]{2,1,0:T(8,128)} %labels) | copy-start | bytes 1572868
  34.8 8.6 %copy-start.4 = (s32[44,8,128]{2,1,0:T(8,128)S(1)}, s32[44,8,128]{2,1,0:T(8,128)}, u32[]{:S(2)}) copy-start(s32[44,8,128]{2,1,0:T(8,128)} %copy-done.3) | copy-start | bytes 540676
  34.8 8.6 %copy-start.8 = (f32[4]{0:T(128)S(1)}, f32[4]{0:T(128)}, u32[]{:S(2)}) copy-start(f32[4]{0:T(128)} %table.1) | copy-start | bytes 52
  34.8 23.1 %all-to-all-start.2 = ((f32[8,4,80,128]{3,2,1,0:T(8,128)}), f32[8,4,80,128]{3,2,1,0:T(8,128)}, u32[]{:S(2)}, u32[]{:S(2)}) async-start(f32[8,4,80,128]{3,2,1,0:T(8,128)} %get-tuple-element.69), calls=%async_computation.2 | async-start | bytes 2621440 | tf_op jit(solution)/shard_map/all_to_all | solution.py:705
  39.5 7.6 %collective-permute-start.6 = (f32[5,48,128]{2,1,0:T(8,128)}, f32[5,48,128]{2,1,0:T(8,128)S(1)}, u32[]{:S(2)}, u32[]{:S(2)}) collective-permute-start(f32[5,48,128]{2,1,0:T(8,128)} %copy-done.9), channel_id=1, source_target_pairs={{0,8},{8,16},{16,24},{24,0},{1,9},{9,17},{17,25},{25,1},{2,10},{10... | collective-permute-start | bytes 368648 | tf_op jit(solution)/shard_map/ppermute | solution.py:691
  42.6 7.7 %collective-permute-start.7 = (f32[5,48,128]{2,1,0:T(8,128)S(1)}, f32[5,48,128]{2,1,0:T(8,128)S(1)}, u32[]{:S(2)}, u32[]{:S(2)}) collective-permute-start(f32[5,48,128]{2,1,0:T(8,128)S(1)} %get-tuple-element.55._), channel_id=1, source_target_pairs={{8,0},{16,8},{24,16},{0,24},{9,1},{17,9},{25,17},{1,25},{10,2},{18... | collective-permute-start | bytes 368648 | tf_op jit(solution)/shard_map/ppermute | solution.py:691
  57.8 25.3 %all-to-all-start.1 = ((f32[8,400,128]{2,1,0:T(8,128)}), f32[8,400,128]{2,1,0:T(8,128)S(1)}, u32[]{:S(2)}, u32[]{:S(2)}) async-start(f32[8,400,128]{2,1,0:T(8,128)} %get-tuple-element.68), calls=%async_computation.1 | async-start | bytes 3276800 | tf_op jit(solution)/shard_map/all_to_all | solution.py:713
  61.4 14.9 %copy-start.7 = (s32[32]{0:T(128)S(1)}, s32[32]{0:T(128)}, u32[]{:S(2)}) copy-start(s32[32]{0:T(128)} %copy-done.6) | copy-start | bytes 388
  62.8 9.7 %collective-permute-start.8 = (f32[16,24,128]{2,1,0:T(8,128)S(1)}, f32[16,24,128]{2,1,0:T(8,128)S(1)}, u32[]{:S(2)}, u32[]{:S(2)}) collective-permute-start(f32[16,24,128]{2,1,0:T(8,128)S(1)} %get-tuple-element.70), channel_id=1, source_target_pairs={{0,8},{8,16},{16,24},{24,0},{1,9},{9,17},{17,25},{25,1},{2,10},{10... | collective-permute-start | bytes 589832 | tf_op jit(solution)/shard_map/ppermute | solution.py:722
  65.8 10.5 %collective-permute-start.9 = (f32[16,24,128]{2,1,0:T(8,128)S(1)}, f32[16,24,128]{2,1,0:T(8,128)S(1)}, u32[]{:S(2)}, u32[]{:S(2)}) collective-permute-start(f32[16,24,128]{2,1,0:T(8,128)S(1)} %get-tuple-element.71), channel_id=1, source_target_pairs={{8,0},{16,8},{24,16},{0,24},{9,1},{17,9},{25,17},{1,25},{10,2},{18... | collective-permute-start | bytes 589832 | tf_op jit(solution)/shard_map/ppermute | solution.py:723
  83.1 23.9 %all-to-all-start.3 = ((f32[8,4,88,128]{3,2,1,0:T(8,128)}), f32[8,4,88,128]{3,2,1,0:T(8,128)}, u32[]{:S(2)}, u32[]{:S(2)}) async-start(f32[8,4,88,128]{3,2,1,0:T(8,128)} %bitcast.14), calls=%async_computation.3 | async-start | bytes 2883584 | tf_op jit(solution)/shard_map/all_to_all | solution.py:730

commit v4 on v3

--- a/solution.py
+++ b/solution.py
@@ -154,21 +154,33 @@
             cells = arrived[slot, pl.ds(i * EDGE, EDGE), :]
             block[row, pl.ds(c * EDGE, EDGE), :] = cells
             if c == 0:
-                left[row] = cells[:SIDE]
+                left[pl.ds(row * WIDE, WIDE), :] = cells[:WIDE]
             if c == TILE_COLS - 1:
-                right[row] = cells[EDGE - SIDE :]
-
-
-def tick(_, out):
-    out[...] = jnp.zeros_like(out)
+                right[pl.ds(row * WIDE, WIDE), :] = cells[EDGE - WIDE :]
+
+
+def edge_columns(before, labels, after, lows, highs):
+    rows, cols = labels.shape[0], labels.shape[1]
+    for row in range(rows + 2 * WIDER):
+        if row < WIDER:
+            line = before.at[row]
+        elif row < WIDER + rows:
+            line = labels.at[row - WIDER]
+        else:
+            line = after.at[row - WIDER - rows]
+        lows[pl.ds(row * WIDER, WIDER), :] = line[pl.ds(0, WIDER), :]
+        highs[pl.ds(row * WIDER, WIDER), :] = line[pl.ds(cols - WIDER, WIDER), :]
 
 
 def edge_rows(block, left, right, ups, downs):
-    rows = block.shape[0]
+    rows, cols = block.shape[0], block.shape[1]
     for row in range(WIDE):
-        low = rows - WIDE + row
-        ups[row] = jnp.concatenate([left[low], block[low], right[low]], axis=0)
-        downs[row] = jnp.concatenate([left[row], block[row], right[row]], axis=0)
+        for out, source in ((ups, rows - WIDE + row), (downs, row)):
+            out[row, pl.ds(0, SIDE), :] = jnp.zeros((SIDE, DEPTH), jnp.float32)
+            out[row, pl.ds(SIDE + cols, SIDE), :] = jnp.zeros((SIDE, DEPTH), jnp.float32)
+            out[row, pl.ds(SIDE - WIDE, WIDE), :] = left[pl.ds(source * WIDE, WIDE), :]
+            out[row, pl.ds(SIDE, cols), :] = block[source]
+            out[row, pl.ds(SIDE + cols, WIDE), :] = right[pl.ds(source * WIDE, WIDE), :]
 
 
 def harmonic(a, b):
@@ -176,7 +188,7 @@
 
 
 def face_weights(table, labels, before, after, left, right, wx, wy, wz, inverse, permit):
-    rows = labels.shape[0]
+    rows, cols = labels.shape[0], labels.shape[1]
     total = rows + 2 * WIDER
 
     def look(label):
@@ -186,13 +198,17 @@
         return value
 
     for row in range(WIDER):
-        low, high = row, WIDER + rows + row
-        permit[low] = look(jnp.concatenate([left[low], before[row], right[low]], axis=0))
-        permit[high] = look(jnp.concatenate([left[high], after[row], right[high]], axis=0))
+        permit[row, pl.ds(SIDE, cols), :] = look(before[row])
+        permit[WIDER + rows + row, pl.ds(SIDE, cols), :] = look(after[row])
+
+    for row in range(total):
+        permit[row, pl.ds(0, SIDE), :] = jnp.ones((SIDE, DEPTH), jnp.float32)
+        permit[row, pl.ds(SIDE + cols, SIDE), :] = jnp.ones((SIDE, DEPTH), jnp.float32)
+        permit[row, pl.ds(SIDE - WIDER, WIDER), :] = look(left[pl.ds(row * WIDER, WIDER), :])
+        permit[row, pl.ds(SIDE + cols, WIDER), :] = look(right[pl.ds(row * WIDER, WIDER), :])
 
     def fill(row, carry):
-        row = WIDER + row
-        permit[row] = look(jnp.concatenate([left[row], labels[row - WIDER], right[row]], axis=0))
+        permit[WIDER + row, pl.ds(SIDE, cols), :] = look(labels[row])
         return carry
 
     lax.fori_loop(0, rows, fill, 0, unroll=2)
@@ -215,7 +231,7 @@
     lax.fori_loop(1, total - 1, weigh, 0, unroll=6)
 
 
-def solve(band, tiles, slot_of, middle, left, right, before, after, wx, wy, wz, inverse, _, out, frames, u0, u1, residual, potential):
+def solve(band, tiles, slot_of, middle, left, right, before, after, wx, wy, wz, inverse, out, frames, u0, u1, residual, potential):
     rows, width = middle.shape[0], wx.shape[1]
     center_value = 0.5 * (spectrum_high + spectrum_low)
     half_width = 0.5 * (spectrum_high - spectrum_low)
@@ -232,8 +248,16 @@
         start(1 + row, before[row])
         start(1 + WIDE + rows + row, after[row])
 
+    nothing = jnp.zeros((SIDE, DEPTH), jnp.float32)
+    for row in range(rows):
+        u1[row, pl.ds(0, SIDE), :] = nothing
+        u1[row, pl.ds(width - SIDE, SIDE), :] = nothing
+        u1[row, pl.ds(SIDE - WIDE, WIDE), :] = left[pl.ds(row * WIDE, WIDE), :]
+        u1[row, pl.ds(width - SIDE, WIDE), :] = right[pl.ds(row * WIDE, WIDE), :]
+
     def begin(row, carry):
-        start(1 + WIDE + row, jnp.concatenate([left[row], middle[row], right[row]], axis=0))
+        lows, highs = u1[row, pl.ds(0, SIDE), :], u1[row, pl.ds(width - SIDE, SIDE), :]
+        start(1 + WIDE + row, jnp.concatenate([lows, middle[row], highs], axis=0))
         return carry
 
     lax.fori_loop(0, rows, begin, 0, unroll=2)
@@ -646,11 +670,6 @@
 
     beside = [lax.ppermute(phase_label[rows - WIDER :], "gx", gx_up)]
     beside.append(lax.ppermute(phase_label[:WIDER], "gx", gx_down))
-    beside = list(lax.optimization_barrier(tuple(beside)))
-    tall = jnp.concatenate([beside[0][:, cols - SIDE :], phase_label[:, cols - SIDE :], beside[1][:, cols - SIDE :]])
-    beside.append(lax.ppermute(tall, "gy", gy_up))
-    tall = jnp.concatenate([beside[0][:, :SIDE], phase_label[:, :SIDE], beside[1][:, :SIDE]])
-    beside.append(lax.ppermute(tall, "gy", gy_down))
 
     one_tile = pl.BlockSpec((1, AREA, DEPTH), lambda t: (t, 0, 0))
     raw, bits = pl.pallas_call(
@@ -666,6 +685,13 @@
         scratch_shapes=[pltpu.VMEM((3, EDGE + 2, PADDED, DEPTH), jnp.int32)],
         compiler_params=room(14), name="raw_faces",
     )(pops, held, fluid_mask)
+    beside[0], beside[1], raw = lax.optimization_barrier((beside[0], beside[1], raw))
+    columns = (rows + 2 * WIDER) * WIDER
+    lows, highs = pl.pallas_call(
+        edge_columns, out_shape=[shape((columns, DEPTH), jnp.int32)] * 2, in_specs=[VMEM] * 3, out_specs=[VMEM] * 2,
+        compiler_params=room(4), name="edge_columns",
+    )(beside[0], phase_label, beside[1])
+    beside += [lax.ppermute(highs, "gy", gy_up), lax.ppermute(lows, "gy", gy_down)]
     arrived, raw, beside = lax.optimization_barrier((arrived, raw, beside))
     beside = list(beside)
 
@@ -678,10 +704,11 @@
 
     block, left, right = pl.pallas_call(
         functools.partial(assemble, band, tiles),
-        out_shape=[pltpu.VMEM((rows, cols, DEPTH), f32), shape((rows, SIDE, DEPTH), f32), shape((rows, SIDE, DEPTH), f32)],
+        out_shape=[pltpu.VMEM((rows, cols, DEPTH), f32), shape((rows * WIDE, DEPTH), f32), shape((rows * WIDE, DEPTH), f32)],
         in_specs=[SMEM, VMEM], out_specs=[VMEM] * 3, compiler_params=room(5), name="assemble",
     )(slot_of, arrived)
     left, right = lax.ppermute(right, "gy", gy_up), lax.ppermute(left, "gy", gy_down)
+    left, right, raw = lax.optimization_barrier((left, right, raw))
     ends = shape((WIDE, cols + 2 * SIDE, DEPTH), f32)
     ups, downs = pl.pallas_call(
         edge_rows, out_shape=[ends, ends], in_specs=[VMEM] * 3, out_specs=[VMEM] * 2,
@@ -690,11 +717,6 @@
     ups, downs, beside[0] = lax.optimization_barrier((ups, downs, beside[0]))
     before, after = lax.ppermute(ups, "gx", gx_up), lax.ppermute(downs, "gx", gx_down)
     hbm = pl.BlockSpec(memory_space=pl.ANY)
-    token = pl.pallas_call(
-        tick, out_shape=shape((8, DEPTH), f32), in_specs=[hbm], out_specs=VMEM, compiler_params=room(1), name="tick"
-    )(downs)
-    raw, token = lax.optimization_barrier((raw, token))
-    token, beside[0] = lax.optimization_barrier((token, beside[0]))
     wide = shape((rows + 2 * WIDER, cols + 2 * SIDE, DEPTH), f32)
     scratch = pltpu.VMEM(wide.shape, f32)
     weights = pl.pallas_call(
@@ -707,9 +729,9 @@
     potential, frames = pl.pallas_call(
         functools.partial(solve, band, tiles),
         out_shape=[shape((rows, cols, DEPTH), f32), pltpu.HBM((peers, FRAME * FRAME, DEPTH), f32)],
-        in_specs=[SMEM] + [VMEM] * 9 + [hbm], out_specs=[VMEM, VMEM],
+        in_specs=[SMEM] + [VMEM] * 9, out_specs=[VMEM, VMEM],
         scratch_shapes=[scratch] * 4, compiler_params=room(16), name="solve",
-    )(slot_of, block, left, right, before, after, *weights, token)
+    )(slot_of, block, left, right, before, after, *weights)
     frames = lax.all_to_all(frames, "gy", split_axis=0, concat_axis=0, tiled=True)
 
     lows = (band_cols, low_count * 8, DEPTH)

time: 113 us -> 112 us (level)
  local copies, waits for them, and re-layouts: 3.99 us -> 2.13 us
  waiting for transfers between devices: 31.7 us -> 33 us
    ppermute x1, starting transfers between devices: 1.79 us -> 0.02 us  [per_device(): lax.ppermute(right, 'gy', gy_up)]
    ppermute x1, starting transfers between devices: 1.13 us -> 2.63 us  [per_device(): lax.ppermute(left, 'gy', gy_down)]
    ppermute x1, waiting for transfers between devices: 3.23 us -> 1.9 us  [per_device(): lax.ppermute(downs, 'gx', gx_down)]
    unnamed x23 -> x13, local copies, waits for them, and re-layouts: 2.58 us -> 2.04 us
  transfers between devices with their start and end apart: 14 -> 14, of which waited for: 10 -> 10; matrix products, arithmetic and copies ran while one was open for 1% -> 0% of each run, Pallas kernels for 29% -> 30%
where the time goes in v4:
time: 112 us; the launch traced here: 111 us
  Pallas kernels  41.1 us (37%)
  starting transfers between devices  34.2 us (31%)
  waiting for transfers between devices  33 us (29%)
  local copies, waits for them, and re-layouts  2.13 us (2%)
    pallas_call x1, Pallas kernels, per_device(): pl.pallas_call(step_inside, grid_spec=pltpu.PrefetchScalarGridSpec(num_sc...  13.2 us
    pallas_call x1, Pallas kernels, per_device(): pl.pallas_call(functools.partial(raw_faces, peers), grid=(tiles,), out_sh...  6.52 us
    all_to_all x1, waiting for transfers between devices, per_device(): lax.all_to_all(turned.reshape(peers, tiles, in_rows, DEPTH), 'gy', split_...  6.46 us
    pallas_call x1, Pallas kernels, per_device(): pl.pallas_call(functools.partial(solve, band, tiles), out_shape=[shape((r...  6.33 us
    pallas_call x1, Pallas kernels, per_device(): pl.pallas_call(functools.partial(step_faces, peers, tiles, band_cols), in...  5.87 us
    ppermute x1, waiting for transfers between devices, per_device(): below = lax.ppermute(high, 'gx', gx_up)  5.73 us
    all_to_all x1, starting transfers between devices, per_device(): lax.all_to_all(outgoing, 'gy', split_axis=0, concat_axis=0, tiled=True)  5.3 us
    ppermute x1, waiting for transfers between devices, per_device(): lax.ppermute(highs, 'gy', gy_up)  4.63 us
  transfers between devices with their start and end apart: 14, of which 10 were waited for; matrix products, arithmetic and copies ran while one was open for 0% of the time, Pallas kernels for 30%

profile of v4, /device:TPU:0, one launch (start us, length us, event | category | flops | bytes accessed | tf_op | source)
XLA Modules:
  0.0 111.4 jit_solution(2240191689960152174)
XLA Ops:
  0.6 0.0 copy-start.4
  0.6 0.0 copy-start
  0.7 1.2 %copy.18.mask.mask_at = s32[4,18,18,128]{3,2,1,0:T(8,128)S(1)} copy(s32[4,18,18,128]{3,0,2,1:T(4,128)} %param.8) | data formatting | bytes 1327104 | tf_op args[2]
  1.9 0.0 copy-done.4
  1.9 0.0 copy-done
  1.9 1.6 %pack_source.1 = f32[8,264,128]{2,1,0:T(8,128)} custom-call(s32[4]{0:T(128)S(1)} %copy-done.4, f32[4,256,128]{2,1,0:T(8,128)S(1)} %bitcast.7, s32[4,18,18,128]{3,2,1,0:T(8,128)S(1)} %copy.18.mask.mask_at), custom_call_target="tpu_custom_call" | custom-call | tf_op jit(solution)/shard_map/pack_source/pallas_call | solution.py:663
  3.5 0.0 copy-start.1
  3.5 5.3 %all-to-all-start = ((f32[8,264,128]{2,1,0:T(8,128)}), f32[8,264,128]{2,1,0:T(8,128)S(1)}, u32[]{:S(2)}, u32[]{:S(2)}) async-start(f32[8,264,128]{2,1,0:T(8,128)} %pack_source.1), calls=%async_computation | async-start | bytes 2162688 | tf_op jit(solution)/shard_map/all_to_all | solution.py:669
  8.8 0.0 copy-done.1
  8.9 3.7 %collective-permute-start.1 = (s32[6,32,128]{2,1,0:T(8,128)S(1)}, s32[6,32,128]{2,1,0:T(8,128)S(1)}, u32[]{:S(2)}, u32[]{:S(2)}) collective-permute-start(s32[6,32,128]{2,1,0:T(8,128)S(1)} %get-tuple-element.85), channel_id=1, source_target_pairs={{8,0},{16,8},{24,16},{0,24},{9,1},{17,9},{25,17},{1,25},{10,2},{18... | collective-permute-start | bytes 294920 | tf_op jit(solution)/shard_map/ppermute | solution.py:672
  12.5 0.0 collective-permute-start
  12.5 6.5 %raw_faces.1 = (f32[8,4,80,128]{3,2,1,0:T(8,128)}, s32[4,256,128]{2,1,0:T(8,128)}) custom-call(f32[19,4,256,128]{3,2,1,0:T(8,128)} %bitcast.11, f32[4,256,128]{2,1,0:T(8,128)S(1)} %bitcast.8, s32[4,18,18,128]{3,2,1,0:T(8,128)S(1)} %copy.18.mask.mask_at), custom_call_target="tpu_custom_call" | custom-call | tf_op jit(solution)/shard_map/raw_faces/pallas_call | solution.py:675
  19.0 0.0 collective-permute-done.1.after
  19.0 0.2 collective-permute-done.before
  19.3 0.1 collective-permute-start.2
  19.4 2.6 %collective-permute-start.3 = (s32[264,128]{1,0:T(8,128)S(1)}, s32[264,128]{1,0:T(8,128)S(1)}, u32[]{:S(2)}, u32[]{:S(2)}) collective-permute-start(s32[264,128]{1,0:T(8,128)S(1)} %get-tuple-element.51), channel_id=1, source_target_pairs={{1,0},{2,1},{3,2},{4,3},{5,4},{6,5},{7,6},{0,7},{9,8},{10,9},{11,1... | collective-permute-start | bytes 405512 | tf_op jit(solution)/shard_map/ppermute | solution.py:694
  22.0 0.1 pad_add_fusion
  22.1 4.6 %collective-permute-done.2.left = s32[264,128]{1,0:T(8,128)S(1)} collective-permute-done((s32[264,128]{1,0:T(8,128)S(1)}, s32[264,128]{1,0:T(8,128)S(1)}, u32[]{:S(2)}, u32[]{:S(2)}) %collective-permute-start.2) | collective-permute-done | bytes 135200 | tf_op jit(solution)/shard_map/ppermute | solution.py:694
  26.7 0.0 collective-permute-done.3.right
  26.7 0.0 all-to-all-done.arrived
  26.7 0.1 convert_element_type.12.tile_at
  26.8 0.1 select_reduce_fusion.slot_of
  26.9 0.6 assemble.1
  27.5 0.0 copy-start.2
  27.5 0.8 copy-done.2
  28.3 0.0 collective-permute-start.4
  28.3 0.0 copy-start.3
  28.3 0.0 copy-start.5
  28.3 2.6 %collective-permute-start.5 = (f32[160,128]{1,0:T(8,128)S(1)}, f32[160,128]{1,0:T(8,128)S(1)}, u32[]{:S(2)}, u32[]{:S(2)}) collective-permute-start(f32[160,128]{1,0:T(8,128)S(1)} %get-tuple-element.55), channel_id=1, source_target_pairs={{1,0},{2,1},{3,2},{4,3},{5,4},{6,5},{7,6},{0,7},{9,8},{10,9},{11,1... | collective-permute-start | bytes 245768 | tf_op jit(solution)/shard_map/ppermute | solution.py:710
  30.9 2.9 %collective-permute-done.4.left = f32[160,128]{1,0:T(8,128)S(1)} collective-permute-done((f32[160,128]{1,0:T(8,128)S(1)}, f32[160,128]{1,0:T(8,128)S(1)}, u32[]{:S(2)}, u32[]{:S(2)}) %collective-permute-start.4) | collective-permute-done | bytes 81952 | tf_op jit(solution)/shard_map/ppermute | solution.py:710
  33.9 0.0 collective-permute-done.5.right
  33.9 4.3 %all-to-all-start.2 = ((f32[8,4,80,128]{3,2,1,0:T(8,128)}), f32[8,4,80,128]{3,2,1,0:T(8,128)}, u32[]{:S(2)}, u32[]{:S(2)}) async-start(f32[8,4,80,128]{3,2,1,0:T(8,128)} %get-tuple-element.73), calls=%async_computation.2 | async-start | bytes 2621440 | tf_op jit(solution)/shard_map/all_to_all | solution.py:727
  38.2 0.0 copy-done.3
  38.2 2.0 %collective-permute-start.6 = (f32[5,48,128]{2,1,0:T(8,128)S(1)}, f32[5,48,128]{2,1,0:T(8,128)S(1)}, u32[]{:S(2)}, u32[]{:S(2)}) collective-permute-start(f32[5,48,128]{2,1,0:T(8,128)S(1)} %get-tuple-element.62), channel_id=1, source_target_pairs={{0,8},{8,16},{16,24},{24,0},{1,9},{9,17},{17,25},{25,1},{2,10},{10... | collective-permute-start | bytes 368648 | tf_op jit(solution)/shard_map/ppermute | solution.py:718
  40.2 1.9 %collective-permute-start.7 = (f32[5,48,128]{2,1,0:T(8,128)S(1)}, f32[5,48,128]{2,1,0:T(8,128)S(1)}, u32[]{:S(2)}, u32[]{:S(2)}) collective-permute-start(f32[5,48,128]{2,1,0:T(8,128)S(1)} %get-tuple-element.63), channel_id=1, source_target_pairs={{8,0},{16,8},{24,16},{0,24},{9,1},{17,9},{25,17},{1,25},{10,2},{18... | collective-permute-start | bytes 368648 | tf_op jit(solution)/shard_map/ppermute | solution.py:718
  42.1 0.0 copy-done.5
  42.1 2.3 %face_weights.1 = (f32[44,48,128]{2,1,0:T(8,128)S(1)}, f32[44,48,128]{2,1,0:T(8,128)S(1)}, f32[44,48,128]{2,1,0:T(8,128)S(1)}, f32[44,48,128]{2,1,0:T(8,128)S(1)}) custom-call(f32[4]{0:T(128)S(1)} %copy-done.5, s32[32,32,128]{2,1,0:T(8,128)S(1)} %copy-done.1, s32[6,32,128]{2,1,0:T(8,128)S(1)} %collective-permute-done.before, ...), custom_call_target="tpu_custom_call" | custom-call | tf_op jit(solution)/shard_map/face_weights/pallas_call | solution.py:722
  44.4 1.8 %collective-permute-done.6.before = f32[5,48,128]{2,1,0:T(8,128)S(1)} collective-permute-done((f32[5,48,128]{2,1,0:T(8,128)S(1)}, f32[5,48,128]{2,1,0:T(8,128)S(1)}, u32[]{:S(2)}, u32[]{:S(2)}) %collective-permute-start.6) | collective-permute-done | bytes 122912 | tf_op jit(solution)/shard_map/ppermute | solution.py:718
  46.2 1.9 %collective-permute-done.7.after = f32[5,48,128]{2,1,0:T(8,128)S(1)} collective-permute-done((f32[5,48,128]{2,1,0:T(8,128)S(1)}, f32[5,48,128]{2,1,0:T(8,128)S(1)}, u32[]{:S(2)}, u32[]{:S(2)}) %collective-permute-start.7) | collective-permute-done | bytes 122912 | tf_op jit(solution)/shard_map/ppermute | solution.py:718
  48.1 6.3 %solve.1 = (f32[32,32,128]{2,1,0:T(8,128)}, f32[8,400,128]{2,1,0:T(8,128)}) custom-call(s32[36]{0:T(128)S(1)} %select_reduce_fusion.slot_of, f32[32,32,128]{2,1,0:T(8,128)S(1)} %copy-done.3, f32[160,128]{1,0:T(8,128)S(1)} %collective-permute-done.4.left, f32[160,128]{1,0:T(8,128)S(1)} %collective-permute-done.5.right, ...), custom_call_target="tpu_custom_call" | custom-call | tf_op jit(solution)/shard_map/solve/pallas_call | solution.py:729
  54.4 1.9 %all-to-all-done.2 = f32[8,4,80,128]{3,2,1,0:T(8,128)} async-done(((f32[8,4,80,128]{3,2,1,0:T(8,128)}), f32[8,4,80,128]{3,2,1,0:T(8,128)}, u32[]{:S(2)}, u32[]{:S(2)}) %all-to-all-start.2) | async-done | bytes 1310752 | tf_op jit(solution)/shard_map/all_to_all | solution.py:727
  56.4 3.6 %all-to-all-start.1 = ((f32[8,400,128]{2,1,0:T(8,128)}), f32[8,400,128]{2,1,0:T(8,128)S(1)}, u32[]{:S(2)}, u32[]{:S(2)}) async-start(f32[8,400,128]{2,1,0:T(8,128)} %get-tuple-element.72), calls=%async_computation.1 | async-start | bytes 3276800 | tf_op jit(solution)/shard_map/all_to_all | solution.py:735
  60.0 1.4 %outer_rows.1 = (f32[16,24,128]{2,1,0:T(8,128)S(1)}, f32[16,24,128]{2,1,0:T(8,128)S(1)}) custom-call(s32[36]{0:T(128)S(1)} %select_reduce_fusion.slot_of, f32[32,80,128]{2,1,0:T(8,128)} %bitcast.3.arrived), custom_call_target="tpu_custom_call" | custom-call | tf_op jit(solution)/shard_map/outer_rows/pallas_call | solution.py:739
  61.3 2.0 %collective-permute-start.8 = (f32[16,24,128]{2,1,0:T(8,128)S(1)}, f32[16,24,128]{2,1,0:T(8,128)S(1)}, u32[]{:S(2)}, u32[]{:S(2)}) collective-permute-start(f32[16,24,128]{2,1,0:T(8,128)S(1)} %get-tuple-element.74), channel_id=1, source_target_pairs={{0,8},{8,16},{16,24},{24,0},{1,9},{9,17},{17,25},{25,1},{2,10},{10... | collective-permute-start | bytes 589832 | tf_op jit(solution)/shard_map/ppermute | solution.py:744
  63.3 1.9 %collective-permute-start.9 = (f32[16,24,128]{2,1,0:T(8,128)S(1)}, f32[16,24,128]{2,1,0:T(8,128)S(1)}, u32[]{:S(2)}, u32[]{:S(2)}) collective-permute-start(f32[16,24,128]{2,1,0:T(8,128)S(1)} %get-tuple-element.75), channel_id=1, source_target_pairs={{8,0},{16,8},{24,16},{0,24},{9,1},{17,9},{25,17},{1,25},{10,2},{18... | collective-permute-start | bytes 589832 | tf_op jit(solution)/shard_map/ppermute | solution.py:745
  65.2 5.7 %collective-permute-done.8.below = f32[16,24,128]{2,1,0:T(8,128)S(1)} collective-permute-done((f32[16,24,128]{2,1,0:T(8,128)S(1)}, f32[16,24,128]{2,1,0:T(8,128)S(1)}, u32[]{:S(2)}, u32[]{:S(2)}) %collective-permute-start.8) | collective-permute-done | bytes 196640 | tf_op jit(solution)/shard_map/ppermute | solution.py:744
  70.9 3.5 %collective-permute-done.9.above = f32[16,24,128]{2,1,0:T(8,128)S(1)} collective-permute-done((f32[16,24,128]{2,1,0:T(8,128)S(1)}, f32[16,24,128]{2,1,0:T(8,128)S(1)}, u32[]{:S(2)}, u32[]{:S(2)}) %collective-permute-start.9) | collective-permute-done | bytes 196640 | tf_op jit(solution)/shard_map/ppermute | solution.py:745
  74.5 3.3 %turn_faces.1 = f32[32,88,128]{2,1,0:T(8,128)} custom-call(s32[36]{0:T(128)S(1)} %select_reduce_fusion.slot_of, s32[32]{0:T(128)S(1)} %convert_element_type.12.tile_at, s32[1]{0:T(128)} %bitcast.2.me_ref, f32[32,80,128]{2,1,0:T(8,128)} %bitcast.3.arrived, f32[16,24,128]{2,1,0:T(8,128)S(1)} %collective-permute-done.8.below, ...), custom_call_target="tpu_custom_call" | custom-call | tf_op jit(solution)/shard_map/turn_faces/pallas_call | solution.py:746
  77.7 3.9 %all-to-all-done.1.frame.frames_at = f32[8,400,128]{2,1,0:T(8,128)S(1)} async-done(((f32[8,400,128]{2,1,0:T(8,128)}), f32[8,400,128]{2,1,0:T(8,128)S(1)}, u32[]{:S(2)}, u32[]{:S(2)}) %all-to-all-start.1) | async-done | bytes 1638432 | tf_op jit(solution)/shard_map/all_to_all | solution.py:735
  81.6 4.3 %all-to-all-start.3 = ((f32[8,4,88,128]{3,2,1,0:T(8,128)}), f32[8,4,88,128]{3,2,1,0:T(8,128)}, u32[]{:S(2)}, u32[]{:S(2)}) async-start(f32[8,4,88,128]{3,2,1,0:T(8,128)} %bitcast.14), calls=%async_computation.3 | async-start | bytes 2883584 | tf_op jit(solution)/shard_map/all_to_all | solution.py:752
  85.9 13.2 %step_inside.1 = (f32[19,4,256,128]{3,2,1,0:T(8,128)}, f32[4,256,128]{2,1,0:T(8,128)}, f32[4,4,16,128]{3,2,1,0:T(8,128)S(1)}, f32[4,10,16,128]{3,2,1,0:T(8,128)}, f32[4,10,16,128]{3,2,1,0:T(8,128)}) custom-call(s32[4]{0:T(128)S(1)} %copy-done.4, f32[19,4,256,128]{3,2,1,0:T(8,128)} %bitcast.12, f32[4,256,128]{2,1,0:T(8,128)S(1)} %bitcast.9, ...), custom_call_target="tpu_custom_call" | custom-call | tf_op jit(solution)/shard_map/step_inside/pallas_call | solution.py:761
  99.1 6.5 %all-to-all-done.3.rims_at = f32[8,4,88,128]{3,2,1,0:T(8,128)} async-done(((f32[8,4,88,128]{3,2,1,0:T(8,128)}), f32[8,4,88,128]{3,2,1,0:T(8,128)}, u32[]{:S(2)}, u32[]{:S(2)}) %all-to-all-start.3) | async-done | bytes 1441824 | tf_op jit(solution)/shard_map/all_to_all | solution.py:752
  105.6 5.9 %step_faces.1 = (f32[4,256,128]{2,1,0:T(8,128)}, f32[19,4,16,16,128]{4,3,2,1,0:T(8,128)}) custom-call(s32[4]{0:T(128)S(1)} %copy-done.4, f32[4,256,128]{2,1,0:T(8,128)S(1)} %bitcast.10, s32[4,18,18,128]{3,2,1,0:T(8,128)S(1)} %copy.18.mask.mask_at, f32[8,400,128]{2,1,0:T(8,128)S(1)} %all-to-all-done.1.frame.frames_at, ...), custom_call_target="tpu_custom_call", output_to_operand_aliasing={{1}: (9, {})} | custom-call | tf_op jit(solution)/shard_map/step_faces/pallas_call | solution.py:788
  (6 shorter events, 0.1 us)
Async XLA Ops:
  0.6 1.3 %copy-start.4 = (s32[4]{0:T(128)S(1)}, s32[4]{0:T(128)}, u32[]{:S(2)}) copy-start(s32[4]{0:T(128)} %ids.5) | copy-start | bytes 52
  0.6 1.3 %copy-start = (f32[4,16,16,128]{3,2,1,0:T(8,128)S(1)}, f32[4,16,16,128]{3,2,1,0:T(8,128)}, u32[]{:S(2)}) copy-start(f32[4,16,16,128]{3,2,1,0:T(8,128)} %param.7) | copy-start | bytes 1572868
  3.5 5.3 %copy-start.1 = (s32[32,32,128]{2,1,0:T(8,128)S(1)}, s32[32,32,128]{2,1,0:T(8,128)}, u32[]{:S(2)}) copy-start(s32[32,32,128]{2,1,0:T(8,128)} %labels.1) | copy-start | bytes 1572868
  3.5 23.2 %all-to-all-start = ((f32[8,264,128]{2,1,0:T(8,128)}), f32[8,264,128]{2,1,0:T(8,128)S(1)}, u32[]{:S(2)}, u32[]{:S(2)}) async-start(f32[8,264,128]{2,1,0:T(8,128)} %pack_source.1), calls=%async_computation | async-start | bytes 2162688 | tf_op jit(solution)/shard_map/all_to_all | solution.py:669
  8.9 10.2 %collective-permute-start.1 = (s32[6,32,128]{2,1,0:T(8,128)S(1)}, s32[6,32,128]{2,1,0:T(8,128)S(1)}, u32[]{:S(2)}, u32[]{:S(2)}) collective-permute-start(s32[6,32,128]{2,1,0:T(8,128)S(1)} %get-tuple-element.85), channel_id=1, source_target_pairs={{8,0},{16,8},{24,16},{0,24},{9,1},{17,9},{25,17},{1,25},{10,2},{18... | collective-permute-start | bytes 294920 | tf_op jit(solution)/shard_map/ppermute | solution.py:672
  12.5 6.7 %collective-permute-start = (s32[6,32,128]{2,1,0:T(8,128)S(1)}, s32[6,32,128]{2,1,0:T(8,128)S(1)}, u32[]{:S(2)}, u32[]{:S(2)}) collective-permute-start(s32[6,32,128]{2,1,0:T(8,128)S(1)} %get-tuple-element.86), channel_id=1, source_target_pairs={{0,8},{8,16},{16,24},{24,0},{1,9},{9,17},{17,25},{25,1},{2,10},{10... | collective-permute-start | bytes 294920 | tf_op jit(solution)/shard_map/ppermute | solution.py:671
  19.3 7.4 %collective-permute-start.2 = (s32[264,128]{1,0:T(8,128)S(1)}, s32[264,128]{1,0:T(8,128)S(1)}, u32[]{:S(2)}, u32[]{:S(2)}) collective-permute-start(s32[264,128]{1,0:T(8,128)S(1)} %get-tuple-element.50), channel_id=1, source_target_pairs={{0,1},{1,2},{2,3},{3,4},{4,5},{5,6},{6,7},{7,0},{8,9},{9,10},{10,1... | collective-permute-start | bytes 405512 | tf_op jit(solution)/shard_map/ppermute | solution.py:694
  19.4 7.3 %collective-permute-start.3 = (s32[264,128]{1,0:T(8,128)S(1)}, s32[264,128]{1,0:T(8,128)S(1)}, u32[]{:S(2)}, u32[]{:S(2)}) collective-permute-start(s32[264,128]{1,0:T(8,128)S(1)} %get-tuple-element.51), channel_id=1, source_target_pairs={{1,0},{2,1},{3,2},{4,3},{5,4},{6,5},{7,6},{0,7},{9,8},{10,9},{11,1... | collective-permute-start | bytes 405512 | tf_op jit(solution)/shard_map/ppermute | solution.py:694
  27.5 0.8 copy-start.2
  28.3 5.6 %collective-permute-start.4 = (f32[160,128]{1,0:T(8,128)S(1)}, f32[160,128]{1,0:T(8,128)S(1)}, u32[]{:S(2)}, u32[]{:S(2)}) collective-permute-start(f32[160,128]{1,0:T(8,128)S(1)} %get-tuple-element.54), channel_id=1, source_target_pairs={{0,1},{1,2},{2,3},{3,4},{4,5},{5,6},{6,7},{7,0},{8,9},{9,10},{10,1... | collective-permute-start | bytes 245768 | tf_op jit(solution)/shard_map/ppermute | solution.py:710
  28.3 9.8 %copy-start.3 = (f32[32,32,128]{2,1,0:T(8,128)S(1)}, f32[32,32,128]{2,1,0:T(8,128)}, u32[]{:S(2)}) copy-start(f32[32,32,128]{2,1,0:T(8,128)} %copy-done.2) | copy-start | bytes 1572868
  28.3 13.8 %copy-start.5 = (f32[4]{0:T(128)S(1)}, f32[4]{0:T(128)}, u32[]{:S(2)}) copy-start(f32[4]{0:T(128)} %table.1) | copy-start | bytes 52
  28.3 5.5 %collective-permute-start.5 = (f32[160,128]{1,0:T(8,128)S(1)}, f32[160,128]{1,0:T(8,128)S(1)}, u32[]{:S(2)}, u32[]{:S(2)}) collective-permute-start(f32[160,128]{1,0:T(8,128)S(1)} %get-tuple-element.55), channel_id=1, source_target_pairs={{1,0},{2,1},{3,2},{4,3},{5,4},{6,5},{7,6},{0,7},{9,8},{10,9},{11,1... | collective-permute-start | bytes 245768 | tf_op jit(solution)/shard_map/ppermute | solution.py:710
  33.9 22.5 %all-to-all-start.2 = ((f32[8,4,80,128]{3,2,1,0:T(8,128)}), f32[8,4,80,128]{3,2,1,0:T(8,128)}, u32[]{:S(2)}, u32[]{:S(2)}) async-start(f32[8,4,80,128]{3,2,1,0:T(8,128)} %get-tuple-element.73), calls=%async_computation.2 | async-start | bytes 2621440 | tf_op jit(solution)/shard_map/all_to_all | solution.py:727
  38.2 8.0 %collective-permute-start.6 = (f32[5,48,128]{2,1,0:T(8,128)S(1)}, f32[5,48,128]{2,1,0:T(8,128)S(1)}, u32[]{:S(2)}, u32[]{:S(2)}) collective-permute-start(f32[5,48,128]{2,1,0:T(8,128)S(1)} %get-tuple-element.62), channel_id=1, source_target_pairs={{0,8},{8,16},{16,24},{24,0},{1,9},{9,17},{17,25},{25,1},{2,10},{10... | collective-permute-start | bytes 368648 | tf_op jit(solution)/shard_map/ppermute | solution.py:718
  40.2 7.9 %collective-permute-start.7 = (f32[5,48,128]{2,1,0:T(8,128)S(1)}, f32[5,48,128]{2,1,0:T(8,128)S(1)}, u32[]{:S(2)}, u32[]{:S(2)}) collective-permute-start(f32[5,48,128]{2,1,0:T(8,128)S(1)} %get-tuple-element.63), channel_id=1, source_target_pairs={{8,0},{16,8},{24,16},{0,24},{9,1},{17,9},{25,17},{1,25},{10,2},{18... | collective-permute-start | bytes 368648 | tf_op jit(solution)/shard_map/ppermute | solution.py:718
  56.4 25.3 %all-to-all-start.1 = ((f32[8,400,128]{2,1,0:T(8,128)}), f32[8,400,128]{2,1,0:T(8,128)S(1)}, u32[]{:S(2)}, u32[]{:S(2)}) async-start(f32[8,400,128]{2,1,0:T(8,128)} %get-tuple-element.72), calls=%async_computation.1 | async-start | bytes 3276800 | tf_op jit(solution)/shard_map/all_to_all | solution.py:735
  61.3 9.6 %collective-permute-start.8 = (f32[16,24,128]{2,1,0:T(8,128)S(1)}, f32[16,24,128]{2,1,0:T(8,128)S(1)}, u32[]{:S(2)}, u32[]{:S(2)}) collective-permute-start(f32[16,24,128]{2,1,0:T(8,128)S(1)} %get-tuple-element.74), channel_id=1, source_target_pairs={{0,8},{8,16},{16,24},{24,0},{1,9},{9,17},{17,25},{25,1},{2,10},{10... | collective-permute-start | bytes 589832 | tf_op jit(solution)/shard_map/ppermute | solution.py:744
  63.3 11.2 %collective-permute-start.9 = (f32[16,24,128]{2,1,0:T(8,128)S(1)}, f32[16,24,128]{2,1,0:T(8,128)S(1)}, u32[]{:S(2)}, u32[]{:S(2)}) collective-permute-start(f32[16,24,128]{2,1,0:T(8,128)S(1)} %get-tuple-element.75), channel_id=1, source_target_pairs={{8,0},{16,8},{24,16},{0,24},{9,1},{17,9},{25,17},{1,25},{10,2},{18... | collective-permute-start | bytes 589832 | tf_op jit(solution)/shard_map/ppermute | solution.py:745
  81.6 23.9 %all-to-all-start.3 = ((f32[8,4,88,128]{3,2,1,0:T(8,128)}), f32[8,4,88,128]{3,2,1,0:T(8,128)}, u32[]{:S(2)}, u32[]{:S(2)}) async-start(f32[8,4,88,128]{3,2,1,0:T(8,128)} %bitcast.14), calls=%async_computation.3 | async-start | bytes 2883584 | tf_op jit(solution)/shard_map/all_to_all | solution.py:752

commit v5 on v4

--- a/solution.py
+++ b/solution.py
@@ -515,19 +515,22 @@
     all_flat_near = all_near.reshape(tiles, FRAME * PADDED, DEPTH)
     all_flat_flags = all_flags.reshape(tiles, (EDGE + 2) * PADDED, DEPTH)
 
-    def pieces(tile):
+    group = tiles // 2 if tiles % 2 == 0 else tiles
+
+    def pieces(part):
+        some = pl.ds(part * group, group)
         made = []
         for n, q in enumerate(ACROSS_Y):
-            made.append((new_bands.at[tile, n], out.at[q, tile, :, 0 if LATTICE[q][1] > 0 else EDGE - 1]))
+            made.append((new_bands.at[some, n], out.at[q, some, :, 0 if LATTICE[q][1] > 0 else EDGE - 1]))
         for n, q in enumerate(ACROSS_X):
             layer = 0 if LATTICE[q][0] > 0 else EDGE - 1
             if LATTICE[q][1]:
                 cells = pl.ds(1 if LATTICE[q][1] > 0 else 0, EDGE - 1)
-                made.append((new_lines.at[tile, n, cells], out.at[q, tile, layer, cells]))
+                made.append((new_lines.at[some, n, cells], out.at[q, some, layer, cells]))
             else:
-                made.append((new_lines.at[tile, n], out.at[q, tile, layer]))
-        made.append((charge_out.at[tile], charge_out_at.at[tile]))
-        return [pltpu.make_async_copy(a, b, out_sems.at[tile, n]) for n, (a, b) in enumerate(made)]
+                made.append((new_lines.at[some, n], out.at[q, some, layer]))
+        made.append((charge_out.at[some], charge_out_at.at[some]))
+        return [pltpu.make_async_copy(a, b, out_sems.at[part, n]) for n, (a, b) in enumerate(made)]
 
     def incoming(tile):
         owner = ids[tile] % band_cols // TILE_COLS
@@ -632,13 +635,14 @@
                     value, flag = pltpu.roll(value, cz % DEPTH, 1), pltpu.roll(flag, cz % DEPTH, 1)
                 band = ACROSS_Y.index(q)
                 new_bands[t, band] = jnp.where((flag == 1) & (own_flag == 1), value, new_bands[t, band])
-        for copy in pieces(t):
+        return carry
+
+    for part in range(tiles // group):
+        lax.fori_loop(part * group, (part + 1) * group, patch, 0, unroll=2)
+        for copy in pieces(part):
             copy.start()
-        return carry
-
-    lax.fori_loop(0, tiles, patch, 0, unroll=2)
-    for tile in range(tiles):
-        for copy in pieces(tile):
+    for part in range(tiles // group):
+        for copy in pieces(part):
             copy.wait()
 
 
@@ -805,7 +809,7 @@
             pltpu.VMEM((tiles, 2, 5, PADDED, DEPTH), f32),
             pltpu.VMEM(lines.shape, f32),
             pltpu.SemaphoreType.DMA((tiles, 8)),
-            pltpu.SemaphoreType.DMA((tiles, 1 + len(ACROSS_Y + ACROSS_X))),
+            pltpu.SemaphoreType.DMA((2, 1 + len(ACROSS_Y + ACROSS_X))),
         ],
         out_shape=[shape(held.shape, f32), shape(populations.shape, f32)],
         input_output_aliases={9: 1},

time: 112 us -> 112 us (level)
  no operation moved by 1% of the time
where the time goes in v5:
time: 112 us; the launch traced here: 111 us
  Pallas kernels  40.7 us (36%)
  starting transfers between devices  34.2 us (31%)
  waiting for transfers between devices  33 us (29%)
  local copies, waits for them, and re-layouts  2.13 us (2%)
    pallas_call x1, Pallas kernels, per_device(): pl.pallas_call(step_inside, grid_spec=pltpu.PrefetchScalarGridSpec(num_sc...  13.2 us
    pallas_call x1, Pallas kernels, per_device(): pl.pallas_call(functools.partial(raw_faces, peers), grid=(tiles,), out_sh...  6.52 us
    all_to_all x1, waiting for transfers between devices, per_device(): lax.all_to_all(turned.reshape(peers, tiles, in_rows, DEPTH), 'gy', split_...  6.46 us
    pallas_call x1, Pallas kernels, per_device(): pl.pallas_call(functools.partial(solve, band, tiles), out_shape=[shape((r...  6.33 us
    ppermute x1, waiting for transfers between devices, per_device(): below = lax.ppermute(high, 'gx', gx_up)  5.73 us
    pallas_call x1, Pallas kernels, per_device(): pl.pallas_call(functools.partial(step_faces, peers, tiles, band_cols), in...  5.47 us
    all_to_all x1, starting transfers between devices, per_device(): lax.all_to_all(outgoing, 'gy', split_axis=0, concat_axis=0, tiled=True)  5.3 us
    ppermute x1, waiting for transfers between devices, per_device(): lax.ppermute(highs, 'gy', gy_up)  4.63 us
  transfers between devices with their start and end apart: 14, of which 10 were waited for; matrix products, arithmetic and copies ran while one was open for 0% of the time, Pallas kernels for 30%

profile of v5, /device:TPU:0, one launch (start us, length us, event | category | flops | bytes accessed | tf_op | source)
XLA Modules:
  0.0 111.0 jit_solution(6146867539008453844)
XLA Ops:
  0.6 0.0 copy-start.4
  0.6 0.0 copy-start
  0.7 1.2 %copy.18.mask.mask_at = s32[4,18,18,128]{3,2,1,0:T(8,128)S(1)} copy(s32[4,18,18,128]{3,0,2,1:T(4,128)} %param.8) | data formatting | bytes 1327104 | tf_op args[2]
  1.9 0.0 copy-done.4
  1.9 0.0 copy-done
  1.9 1.6 %pack_source.1 = f32[8,264,128]{2,1,0:T(8,128)} custom-call(s32[4]{0:T(128)S(1)} %copy-done.4, f32[4,256,128]{2,1,0:T(8,128)S(1)} %bitcast.7, s32[4,18,18,128]{3,2,1,0:T(8,128)S(1)} %copy.18.mask.mask_at), custom_call_target="tpu_custom_call" | custom-call | tf_op jit(solution)/shard_map/pack_source/pallas_call | solution.py:667
  3.5 0.0 copy-start.1
  3.5 5.3 %all-to-all-start = ((f32[8,264,128]{2,1,0:T(8,128)}), f32[8,264,128]{2,1,0:T(8,128)S(1)}, u32[]{:S(2)}, u32[]{:S(2)}) async-start(f32[8,264,128]{2,1,0:T(8,128)} %pack_source.1), calls=%async_computation | async-start | bytes 2162688 | tf_op jit(solution)/shard_map/all_to_all | solution.py:673
  8.8 0.0 copy-done.1
  8.9 3.7 %collective-permute-start.1 = (s32[6,32,128]{2,1,0:T(8,128)S(1)}, s32[6,32,128]{2,1,0:T(8,128)S(1)}, u32[]{:S(2)}, u32[]{:S(2)}) collective-permute-start(s32[6,32,128]{2,1,0:T(8,128)S(1)} %get-tuple-element.85), channel_id=1, source_target_pairs={{8,0},{16,8},{24,16},{0,24},{9,1},{17,9},{25,17},{1,25},{10,2},{18... | collective-permute-start | bytes 294920 | tf_op jit(solution)/shard_map/ppermute | solution.py:676
  12.5 0.0 collective-permute-start
  12.5 6.5 %raw_faces.1 = (f32[8,4,80,128]{3,2,1,0:T(8,128)}, s32[4,256,128]{2,1,0:T(8,128)}) custom-call(f32[19,4,256,128]{3,2,1,0:T(8,128)} %bitcast.11, f32[4,256,128]{2,1,0:T(8,128)S(1)} %bitcast.8, s32[4,18,18,128]{3,2,1,0:T(8,128)S(1)} %copy.18.mask.mask_at), custom_call_target="tpu_custom_call" | custom-call | tf_op jit(solution)/shard_map/raw_faces/pallas_call | solution.py:679
  19.0 0.0 collective-permute-done.1.after
  19.0 0.2 collective-permute-done.before
  19.3 0.1 collective-permute-start.2
  19.4 2.6 %collective-permute-start.3 = (s32[264,128]{1,0:T(8,128)S(1)}, s32[264,128]{1,0:T(8,128)S(1)}, u32[]{:S(2)}, u32[]{:S(2)}) collective-permute-start(s32[264,128]{1,0:T(8,128)S(1)} %get-tuple-element.51), channel_id=1, source_target_pairs={{1,0},{2,1},{3,2},{4,3},{5,4},{6,5},{7,6},{0,7},{9,8},{10,9},{11,1... | collective-permute-start | bytes 405512 | tf_op jit(solution)/shard_map/ppermute | solution.py:698
  22.0 0.1 pad_add_fusion
  22.1 4.6 %collective-permute-done.2.left = s32[264,128]{1,0:T(8,128)S(1)} collective-permute-done((s32[264,128]{1,0:T(8,128)S(1)}, s32[264,128]{1,0:T(8,128)S(1)}, u32[]{:S(2)}, u32[]{:S(2)}) %collective-permute-start.2) | collective-permute-done | bytes 135200 | tf_op jit(solution)/shard_map/ppermute | solution.py:698
  26.7 0.0 collective-permute-done.3.right
  26.7 0.0 all-to-all-done.arrived
  26.7 0.1 convert_element_type.12.tile_at
  26.8 0.1 select_reduce_fusion.slot_of
  26.9 0.6 assemble.1
  27.5 0.0 copy-start.2
  27.5 0.8 copy-done.2
  28.3 0.0 collective-permute-start.4
  28.3 0.0 copy-start.3
  28.3 0.0 copy-start.5
  28.3 2.6 %collective-permute-start.5 = (f32[160,128]{1,0:T(8,128)S(1)}, f32[160,128]{1,0:T(8,128)S(1)}, u32[]{:S(2)}, u32[]{:S(2)}) collective-permute-start(f32[160,128]{1,0:T(8,128)S(1)} %get-tuple-element.55), channel_id=1, source_target_pairs={{1,0},{2,1},{3,2},{4,3},{5,4},{6,5},{7,6},{0,7},{9,8},{10,9},{11,1... | collective-permute-start | bytes 245768 | tf_op jit(solution)/shard_map/ppermute | solution.py:714
  30.9 2.9 %collective-permute-done.4.left = f32[160,128]{1,0:T(8,128)S(1)} collective-permute-done((f32[160,128]{1,0:T(8,128)S(1)}, f32[160,128]{1,0:T(8,128)S(1)}, u32[]{:S(2)}, u32[]{:S(2)}) %collective-permute-start.4) | collective-permute-done | bytes 81952 | tf_op jit(solution)/shard_map/ppermute | solution.py:714
  33.9 0.0 collective-permute-done.5.right
  33.9 4.3 %all-to-all-start.2 = ((f32[8,4,80,128]{3,2,1,0:T(8,128)}), f32[8,4,80,128]{3,2,1,0:T(8,128)}, u32[]{:S(2)}, u32[]{:S(2)}) async-start(f32[8,4,80,128]{3,2,1,0:T(8,128)} %get-tuple-element.73), calls=%async_computation.2 | async-start | bytes 2621440 | tf_op jit(solution)/shard_map/all_to_all | solution.py:731
  38.2 0.0 copy-done.3
  38.2 2.0 %collective-permute-start.6 = (f32[5,48,128]{2,1,0:T(8,128)S(1)}, f32[5,48,128]{2,1,0:T(8,128)S(1)}, u32[]{:S(2)}, u32[]{:S(2)}) collective-permute-start(f32[5,48,128]{2,1,0:T(8,128)S(1)} %get-tuple-element.62), channel_id=1, source_target_pairs={{0,8},{8,16},{16,24},{24,0},{1,9},{9,17},{17,25},{25,1},{2,10},{10... | collective-permute-start | bytes 368648 | tf_op jit(solution)/shard_map/ppermute | solution.py:722
  40.2 1.9 %collective-permute-start.7 = (f32[5,48,128]{2,1,0:T(8,128)S(1)}, f32[5,48,128]{2,1,0:T(8,128)S(1)}, u32[]{:S(2)}, u32[]{:S(2)}) collective-permute-start(f32[5,48,128]{2,1,0:T(8,128)S(1)} %get-tuple-element.63), channel_id=1, source_target_pairs={{8,0},{16,8},{24,16},{0,24},{9,1},{17,9},{25,17},{1,25},{10,2},{18... | collective-permute-start | bytes 368648 | tf_op jit(solution)/shard_map/ppermute | solution.py:722
  42.1 0.0 copy-done.5
  42.1 2.3 %face_weights.1 = (f32[44,48,128]{2,1,0:T(8,128)S(1)}, f32[44,48,128]{2,1,0:T(8,128)S(1)}, f32[44,48,128]{2,1,0:T(8,128)S(1)}, f32[44,48,128]{2,1,0:T(8,128)S(1)}) custom-call(f32[4]{0:T(128)S(1)} %copy-done.5, s32[32,32,128]{2,1,0:T(8,128)S(1)} %copy-done.1, s32[6,32,128]{2,1,0:T(8,128)S(1)} %collective-permute-done.before, ...), custom_call_target="tpu_custom_call" | custom-call | tf_op jit(solution)/shard_map/face_weights/pallas_call | solution.py:726
  44.4 1.8 %collective-permute-done.6.before = f32[5,48,128]{2,1,0:T(8,128)S(1)} collective-permute-done((f32[5,48,128]{2,1,0:T(8,128)S(1)}, f32[5,48,128]{2,1,0:T(8,128)S(1)}, u32[]{:S(2)}, u32[]{:S(2)}) %collective-permute-start.6) | collective-permute-done | bytes 122912 | tf_op jit(solution)/shard_map/ppermute | solution.py:722
  46.2 1.9 %collective-permute-done.7.after = f32[5,48,128]{2,1,0:T(8,128)S(1)} collective-permute-done((f32[5,48,128]{2,1,0:T(8,128)S(1)}, f32[5,48,128]{2,1,0:T(8,128)S(1)}, u32[]{:S(2)}, u32[]{:S(2)}) %collective-permute-start.7) | collective-permute-done | bytes 122912 | tf_op jit(solution)/shard_map/ppermute | solution.py:722
  48.1 6.3 %solve.1 = (f32[32,32,128]{2,1,0:T(8,128)}, f32[8,400,128]{2,1,0:T(8,128)}) custom-call(s32[36]{0:T(128)S(1)} %select_reduce_fusion.slot_of, f32[32,32,128]{2,1,0:T(8,128)S(1)} %copy-done.3, f32[160,128]{1,0:T(8,128)S(1)} %collective-permute-done.4.left, f32[160,128]{1,0:T(8,128)S(1)} %collective-permute-done.5.right, ...), custom_call_target="tpu_custom_call" | custom-call | tf_op jit(solution)/shard_map/solve/pallas_call | solution.py:733
  54.4 1.9 %all-to-all-done.2 = f32[8,4,80,128]{3,2,1,0:T(8,128)} async-done(((f32[8,4,80,128]{3,2,1,0:T(8,128)}), f32[8,4,80,128]{3,2,1,0:T(8,128)}, u32[]{:S(2)}, u32[]{:S(2)}) %all-to-all-start.2) | async-done | bytes 1310752 | tf_op jit(solution)/shard_map/all_to_all | solution.py:731
  56.4 3.6 %all-to-all-start.1 = ((f32[8,400,128]{2,1,0:T(8,128)}), f32[8,400,128]{2,1,0:T(8,128)S(1)}, u32[]{:S(2)}, u32[]{:S(2)}) async-start(f32[8,400,128]{2,1,0:T(8,128)} %get-tuple-element.72), calls=%async_computation.1 | async-start | bytes 3276800 | tf_op jit(solution)/shard_map/all_to_all | solution.py:739
  60.0 1.4 %outer_rows.1 = (f32[16,24,128]{2,1,0:T(8,128)S(1)}, f32[16,24,128]{2,1,0:T(8,128)S(1)}) custom-call(s32[36]{0:T(128)S(1)} %select_reduce_fusion.slot_of, f32[32,80,128]{2,1,0:T(8,128)} %bitcast.3.arrived), custom_call_target="tpu_custom_call" | custom-call | tf_op jit(solution)/shard_map/outer_rows/pallas_call | solution.py:743
  61.3 2.0 %collective-permute-start.8 = (f32[16,24,128]{2,1,0:T(8,128)S(1)}, f32[16,24,128]{2,1,0:T(8,128)S(1)}, u32[]{:S(2)}, u32[]{:S(2)}) collective-permute-start(f32[16,24,128]{2,1,0:T(8,128)S(1)} %get-tuple-element.74), channel_id=1, source_target_pairs={{0,8},{8,16},{16,24},{24,0},{1,9},{9,17},{17,25},{25,1},{2,10},{10... | collective-permute-start | bytes 589832 | tf_op jit(solution)/shard_map/ppermute | solution.py:748
  63.3 1.9 %collective-permute-start.9 = (f32[16,24,128]{2,1,0:T(8,128)S(1)}, f32[16,24,128]{2,1,0:T(8,128)S(1)}, u32[]{:S(2)}, u32[]{:S(2)}) collective-permute-start(f32[16,24,128]{2,1,0:T(8,128)S(1)} %get-tuple-element.75), channel_id=1, source_target_pairs={{8,0},{16,8},{24,16},{0,24},{9,1},{17,9},{25,17},{1,25},{10,2},{18... | collective-permute-start | bytes 589832 | tf_op jit(solution)/shard_map/ppermute | solution.py:749
  65.2 5.7 %collective-permute-done.8.below = f32[16,24,128]{2,1,0:T(8,128)S(1)} collective-permute-done((f32[16,24,128]{2,1,0:T(8,128)S(1)}, f32[16,24,128]{2,1,0:T(8,128)S(1)}, u32[]{:S(2)}, u32[]{:S(2)}) %collective-permute-start.8) | collective-permute-done | bytes 196640 | tf_op jit(solution)/shard_map/ppermute | solution.py:748
  70.9 3.5 %collective-permute-done.9.above = f32[16,24,128]{2,1,0:T(8,128)S(1)} collective-permute-done((f32[16,24,128]{2,1,0:T(8,128)S(1)}, f32[16,24,128]{2,1,0:T(8,128)S(1)}, u32[]{:S(2)}, u32[]{:S(2)}) %collective-permute-start.9) | collective-permute-done | bytes 196640 | tf_op jit(solution)/shard_map/ppermute | solution.py:749
  74.5 3.3 %turn_faces.1 = f32[32,88,128]{2,1,0:T(8,128)} custom-call(s32[36]{0:T(128)S(1)} %select_reduce_fusion.slot_of, s32[32]{0:T(128)S(1)} %convert_element_type.12.tile_at, s32[1]{0:T(128)} %bitcast.2.me_ref, f32[32,80,128]{2,1,0:T(8,128)} %bitcast.3.arrived, f32[16,24,128]{2,1,0:T(8,128)S(1)} %collective-permute-done.8.below, ...), custom_call_target="tpu_custom_call" | custom-call | tf_op jit(solution)/shard_map/turn_faces/pallas_call | solution.py:750
  77.7 3.9 %all-to-all-done.1.frame.frames_at = f32[8,400,128]{2,1,0:T(8,128)S(1)} async-done(((f32[8,400,128]{2,1,0:T(8,128)}), f32[8,400,128]{2,1,0:T(8,128)S(1)}, u32[]{:S(2)}, u32[]{:S(2)}) %all-to-all-start.1) | async-done | bytes 1638432 | tf_op jit(solution)/shard_map/all_to_all | solution.py:739
  81.6 4.3 %all-to-all-start.3 = ((f32[8,4,88,128]{3,2,1,0:T(8,128)}), f32[8,4,88,128]{3,2,1,0:T(8,128)}, u32[]{:S(2)}, u32[]{:S(2)}) async-start(f32[8,4,88,128]{3,2,1,0:T(8,128)} %bitcast.14), calls=%async_computation.3 | async-start | bytes 2883584 | tf_op jit(solution)/shard_map/all_to_all | solution.py:756
  85.9 13.2 %step_inside.1 = (f32[19,4,256,128]{3,2,1,0:T(8,128)}, f32[4,256,128]{2,1,0:T(8,128)}, f32[4,4,16,128]{3,2,1,0:T(8,128)S(1)}, f32[4,10,16,128]{3,2,1,0:T(8,128)}, f32[4,10,16,128]{3,2,1,0:T(8,128)}) custom-call(s32[4]{0:T(128)S(1)} %copy-done.4, f32[19,4,256,128]{3,2,1,0:T(8,128)} %bitcast.12, f32[4,256,128]{2,1,0:T(8,128)S(1)} %bitcast.9, ...), custom_call_target="tpu_custom_call" | custom-call | tf_op jit(solution)/shard_map/step_inside/pallas_call | solution.py:765
  99.1 6.5 %all-to-all-done.3.rims_at = f32[8,4,88,128]{3,2,1,0:T(8,128)} async-done(((f32[8,4,88,128]{3,2,1,0:T(8,128)}), f32[8,4,88,128]{3,2,1,0:T(8,128)}, u32[]{:S(2)}, u32[]{:S(2)}) %all-to-all-start.3) | async-done | bytes 1441824 | tf_op jit(solution)/shard_map/all_to_all | solution.py:756
  105.6 5.5 %step_faces.1 = (f32[4,256,128]{2,1,0:T(8,128)}, f32[19,4,16,16,128]{4,3,2,1,0:T(8,128)}) custom-call(s32[4]{0:T(128)S(1)} %copy-done.4, f32[4,256,128]{2,1,0:T(8,128)S(1)} %bitcast.10, s32[4,18,18,128]{3,2,1,0:T(8,128)S(1)} %copy.18.mask.mask_at, f32[8,400,128]{2,1,0:T(8,128)S(1)} %all-to-all-done.1.frame.frames_at, ...), custom_call_target="tpu_custom_call", output_to_operand_aliasing={{1}: (9, {})} | custom-call | tf_op jit(solution)/shard_map/step_faces/pallas_call | solution.py:792
  (6 shorter events, 0.1 us)
Async XLA Ops:
  0.6 1.3 %copy-start.4 = (s32[4]{0:T(128)S(1)}, s32[4]{0:T(128)}, u32[]{:S(2)}) copy-start(s32[4]{0:T(128)} %ids.5) | copy-start | bytes 52
  0.6 1.3 %copy-start = (f32[4,16,16,128]{3,2,1,0:T(8,128)S(1)}, f32[4,16,16,128]{3,2,1,0:T(8,128)}, u32[]{:S(2)}) copy-start(f32[4,16,16,128]{3,2,1,0:T(8,128)} %param.7) | copy-start | bytes 1572868
  3.5 5.3 %copy-start.1 = (s32[32,32,128]{2,1,0:T(8,128)S(1)}, s32[32,32,128]{2,1,0:T(8,128)}, u32[]{:S(2)}) copy-start(s32[32,32,128]{2,1,0:T(8,128)} %labels.1) | copy-start | bytes 1572868
  3.5 23.2 %all-to-all-start = ((f32[8,264,128]{2,1,0:T(8,128)}), f32[8,264,128]{2,1,0:T(8,128)S(1)}, u32[]{:S(2)}, u32[]{:S(2)}) async-start(f32[8,264,128]{2,1,0:T(8,128)} %pack_source.1), calls=%async_computation | async-start | bytes 2162688 | tf_op jit(solution)/shard_map/all_to_all | solution.py:673
  8.9 10.2 %collective-permute-start.1 = (s32[6,32,128]{2,1,0:T(8,128)S(1)}, s32[6,32,128]{2,1,0:T(8,128)S(1)}, u32[]{:S(2)}, u32[]{:S(2)}) collective-permute-start(s32[6,32,128]{2,1,0:T(8,128)S(1)} %get-tuple-element.85), channel_id=1, source_target_pairs={{8,0},{16,8},{24,16},{0,24},{9,1},{17,9},{25,17},{1,25},{10,2},{18... | collective-permute-start | bytes 294920 | tf_op jit(solution)/shard_map/ppermute | solution.py:676
  12.5 6.7 %collective-permute-start = (s32[6,32,128]{2,1,0:T(8,128)S(1)}, s32[6,32,128]{2,1,0:T(8,128)S(1)}, u32[]{:S(2)}, u32[]{:S(2)}) collective-permute-start(s32[6,32,128]{2,1,0:T(8,128)S(1)} %get-tuple-element.86), channel_id=1, source_target_pairs={{0,8},{8,16},{16,24},{24,0},{1,9},{9,17},{17,25},{25,1},{2,10},{10... | collective-permute-start | bytes 294920 | tf_op jit(solution)/shard_map/ppermute | solution.py:675
  19.3 7.4 %collective-permute-start.2 = (s32[264,128]{1,0:T(8,128)S(1)}, s32[264,128]{1,0:T(8,128)S(1)}, u32[]{:S(2)}, u32[]{:S(2)}) collective-permute-start(s32[264,128]{1,0:T(8,128)S(1)} %get-tuple-element.50), channel_id=1, source_target_pairs={{0,1},{1,2},{2,3},{3,4},{4,5},{5,6},{6,7},{7,0},{8,9},{9,10},{10,1... | collective-permute-start | bytes 405512 | tf_op jit(solution)/shard_map/ppermute | solution.py:698
  19.4 7.3 %collective-permute-start.3 = (s32[264,128]{1,0:T(8,128)S(1)}, s32[264,128]{1,0:T(8,128)S(1)}, u32[]{:S(2)}, u32[]{:S(2)}) collective-permute-start(s32[264,128]{1,0:T(8,128)S(1)} %get-tuple-element.51), channel_id=1, source_target_pairs={{1,0},{2,1},{3,2},{4,3},{5,4},{6,5},{7,6},{0,7},{9,8},{10,9},{11,1... | collective-permute-start | bytes 405512 | tf_op jit(solution)/shard_map/ppermute | solution.py:698
  27.5 0.8 copy-start.2
  28.3 5.6 %collective-permute-start.4 = (f32[160,128]{1,0:T(8,128)S(1)}, f32[160,128]{1,0:T(8,128)S(1)}, u32[]{:S(2)}, u32[]{:S(2)}) collective-permute-start(f32[160,128]{1,0:T(8,128)S(1)} %get-tuple-element.54), channel_id=1, source_target_pairs={{0,1},{1,2},{2,3},{3,4},{4,5},{5,6},{6,7},{7,0},{8,9},{9,10},{10,1... | collective-permute-start | bytes 245768 | tf_op jit(solution)/shard_map/ppermute | solution.py:714
  28.3 9.8 %copy-start.3 = (f32[32,32,128]{2,1,0:T(8,128)S(1)}, f32[32,32,128]{2,1,0:T(8,128)}, u32[]{:S(2)}) copy-start(f32[32,32,128]{2,1,0:T(8,128)} %copy-done.2) | copy-start | bytes 1572868
  28.3 13.8 %copy-start.5 = (f32[4]{0:T(128)S(1)}, f32[4]{0:T(128)}, u32[]{:S(2)}) copy-start(f32[4]{0:T(128)} %table.1) | copy-start | bytes 52
  28.3 5.5 %collective-permute-start.5 = (f32[160,128]{1,0:T(8,128)S(1)}, f32[160,128]{1,0:T(8,128)S(1)}, u32[]{:S(2)}, u32[]{:S(2)}) collective-permute-start(f32[160,128]{1,0:T(8,128)S(1)} %get-tuple-element.55), channel_id=1, source_target_pairs={{1,0},{2,1},{3,2},{4,3},{5,4},{6,5},{7,6},{0,7},{9,8},{10,9},{11,1... | collective-permute-start | bytes 245768 | tf_op jit(solution)/shard_map/ppermute | solution.py:714
  33.9 22.5 %all-to-all-start.2 = ((f32[8,4,80,128]{3,2,1,0:T(8,128)}), f32[8,4,80,128]{3,2,1,0:T(8,128)}, u32[]{:S(2)}, u32[]{:S(2)}) async-start(f32[8,4,80,128]{3,2,1,0:T(8,128)} %get-tuple-element.73), calls=%async_computation.2 | async-start | bytes 2621440 | tf_op jit(solution)/shard_map/all_to_all | solution.py:731
  38.2 8.0 %collective-permute-start.6 = (f32[5,48,128]{2,1,0:T(8,128)S(1)}, f32[5,48,128]{2,1,0:T(8,128)S(1)}, u32[]{:S(2)}, u32[]{:S(2)}) collective-permute-start(f32[5,48,128]{2,1,0:T(8,128)S(1)} %get-tuple-element.62), channel_id=1, source_target_pairs={{0,8},{8,16},{16,24},{24,0},{1,9},{9,17},{17,25},{25,1},{2,10},{10... | collective-permute-start | bytes 368648 | tf_op jit(solution)/shard_map/ppermute | solution.py:722
  40.2 7.9 %collective-permute-start.7 = (f32[5,48,128]{2,1,0:T(8,128)S(1)}, f32[5,48,128]{2,1,0:T(8,128)S(1)}, u32[]{:S(2)}, u32[]{:S(2)}) collective-permute-start(f32[5,48,128]{2,1,0:T(8,128)S(1)} %get-tuple-element.63), channel_id=1, source_target_pairs={{8,0},{16,8},{24,16},{0,24},{9,1},{17,9},{25,17},{1,25},{10,2},{18... | collective-permute-start | bytes 368648 | tf_op jit(solution)/shard_map/ppermute | solution.py:722
  56.4 25.3 %all-to-all-start.1 = ((f32[8,400,128]{2,1,0:T(8,128)}), f32[8,400,128]{2,1,0:T(8,128)S(1)}, u32[]{:S(2)}, u32[]{:S(2)}) async-start(f32[8,400,128]{2,1,0:T(8,128)} %get-tuple-element.72), calls=%async_computation.1 | async-start | bytes 3276800 | tf_op jit(solution)/shard_map/all_to_all | solution.py:739
  61.3 9.6 %collective-permute-start.8 = (f32[16,24,128]{2,1,0:T(8,128)S(1)}, f32[16,24,128]{2,1,0:T(8,128)S(1)}, u32[]{:S(2)}, u32[]{:S(2)}) collective-permute-start(f32[16,24,128]{2,1,0:T(8,128)S(1)} %get-tuple-element.74), channel_id=1, source_target_pairs={{0,8},{8,16},{16,24},{24,0},{1,9},{9,17},{17,25},{25,1},{2,10},{10... | collective-permute-start | bytes 589832 | tf_op jit(solution)/shard_map/ppermute | solution.py:748
  63.3 11.2 %collective-permute-start.9 = (f32[16,24,128]{2,1,0:T(8,128)S(1)}, f32[16,24,128]{2,1,0:T(8,128)S(1)}, u32[]{:S(2)}, u32[]{:S(2)}) collective-permute-start(f32[16,24,128]{2,1,0:T(8,128)S(1)} %get-tuple-element.75), channel_id=1, source_target_pairs={{8,0},{16,8},{24,16},{0,24},{9,1},{17,9},{25,17},{1,25},{10,2},{18... | collective-permute-start | bytes 589832 | tf_op jit(solution)/shard_map/ppermute | solution.py:749
  81.6 23.9 %all-to-all-start.3 = ((f32[8,4,88,128]{3,2,1,0:T(8,128)}), f32[8,4,88,128]{3,2,1,0:T(8,128)}, u32[]{:S(2)}, u32[]{:S(2)}) async-start(f32[8,4,88,128]{3,2,1,0:T(8,128)} %bitcast.14), calls=%async_computation.3 | async-start | bytes 2883584 | tf_op jit(solution)/shard_map/all_to_all | solution.py:756
